TPU v7x, 32 devices: a whole 2x2x4 slice. The times are simulated.
32 devices in a mesh: rep: 4 (over x, core), shard: 8 (over z, y).
Axes of the slice: x: 2, y: 2, z: 4, core: 2. Of those that a mesh axis runs over, the one named last changes fastest.
Arguments:
- token_ids: int32 [2, 8, 512], P(None, 'shard', 'rep'), may hold values from 0 to 50303
- pic_start: int32 [2, 8], P(None, 'shard'), may hold values from 0 to 256
- comp_pos: int32 [2, 8, 128], P(None, 'shard', 'rep'), may hold values from 0 to 128, as said below
- comp_tgt: int32 [2, 8, 128], P(None, 'shard', 'rep'), may hold values from 0 to 50303
- proj_in: float32 [1024, 7168], P('shard'), may hold values from -0.1875 to 0.1875
- proj_back: float32 [5120, 1024], P('shard')
- small_params: float32 [14336], P('shard')
- head_table: float32 [1024, 50304], P(None, 'shard')
- embed_table: float32 [1024, 50304], P('shard'), may hold values from -6 to 6
- first_in: float32 [1024, 7168], P('shard'), may hold values from -0.00015258789 to 0.00015258789
- second_in: float32 [1024, 7168], P('shard'), may hold values from 5.1894206e-10 to 1.729807e-09
- first_back: float32 [5120, 1024], P('shard'), may hold values from -0.00015258789 to 0.00015258789
- second_back: float32 [5120, 1024], P('shard'), may hold values from 5.1894206e-10 to 1.729807e-09
- first_small: float32 [14336], P('shard'), may hold values from -0.0007324219 to 0.0007324219
- second_small: float32 [14336], P('shard'), may hold values from 1.2973552e-08 to 4.3245173e-08
- first_head: float32 [1024, 50304], P(None, 'shard'), may hold values from -0.00015258789 to 0.00015258789
- second_head: float32 [1024, 50304], P(None, 'shard'), may hold values from 5.1894206e-10 to 1.729807e-09
- first_embed: float32 [1024, 50304], P('shard'), may hold values from -0.00015258789 to 0.00015258789
- second_embed: float32 [1024, 50304], P('shard'), may hold values from 5.1894206e-10 to 1.729807e-09
Outputs:
- loss_parts: float32 [2], replicated
- grad_norm: float32 [1], replicated
- next_in: float32 [1024, 7168], P('shard')
- moment_in: float32 [1024, 7168], P('shard')
- square_in: float32 [1024, 7168], P('shard')
- next_back: float32 [5120, 1024], P('shard')
- moment_back: float32 [5120, 1024], P('shard')
- square_back: float32 [5120, 1024], P('shard')
- next_small: float32 [14336], P('shard')
- moment_small: float32 [14336], P('shard')
- square_small: float32 [14336], P('shard')
- next_head: float32 [1024, 50304], P(None, 'shard')
- moment_head: float32 [1024, 50304], P(None, 'shard')
- square_head: float32 [1024, 50304], P(None, 'shard')
- next_embed: float32 [1024, 50304], P('shard')
- moment_embed: float32 [1024, 50304], P('shard')
- square_embed: float32 [1024, 50304], P('shard')
Inputs may be any that keep to these rules, and one draw needn't show every extreme that they name: `comp_pos`: in each block of 32 slots the used slots come first and name distinct positions below 128; the other slots hold 128. Every block uses at least one slot, and the last block of the last sequence of every micro-batch uses all 32.
All inputs are finite; a program needn't handle non-finite values.
Results may differ from a plain program's by a relative error of at most 0.003.
The roundings to bfloat16 on the way count: a program that leaves them out, or rounds other values in their place, can miss the bound.
Values may be sent and summed in bfloat16 or wider, within the bound.
A program may use at most 432 MiB of HBM per device.

v0:
```python
import jax
import jax.numpy as jnp
from jax import lax
from jax.sharding import PartitionSpec as P

D = 1024
H = 16
HD = 64
ROT = 16
FF = 4096
PIC = 256
STEP = 10


NORM_EPS = 1e-05
CLIP_LEVEL = 1.0
BETA_FIRST = 0.9
BETA_SECOND = 0.95
ADAM_EPS = 1e-08
DECAY_RATE = 0.01
RATE_IN = 0.01
RATE_BACK = 0.05
RATE_SMALL = 0.3
RATE_HEAD = 0.01
RATE_EMBED = 0.3


def combined_all(part, axis, combine):
    gathered = jax.tree.map(lambda a: lax.all_gather(a, axis), part)

    def take(source):
        return jax.tree.map(lambda a: lax.dynamic_index_in_dim(a, source, 0, False), gathered)

    return lax.fori_loop(
        1, lax.axis_size(axis), lambda source, state: combine(state, take(source)), take(0)
    )


def norm_rows(values, gain_vec, shift_vec):
    centred = values - jnp.mean(values, axis=-1, keepdims=True)
    spread = jnp.mean(centred * centred, axis=-1, keepdims=True)
    return centred * lax.rsqrt(spread + NORM_EPS) * gain_vec + shift_vec


def rotate(head_rows, place_vec):
    half_rot = ROT // 2
    exponent = jnp.arange(half_rot).astype(jnp.float32) * (2.0 / ROT)
    angles = place_vec[:, None] * jnp.exp(-exponent * jnp.log(10000.0))
    cosine = jnp.cos(angles)[:, None, :]
    sine_part = jnp.sin(angles)[:, None, :]
    front_part = head_rows[..., :half_rot]
    back_part = head_rows[..., half_rot:ROT]
    return jnp.concatenate(
        [
            front_part * cosine - back_part * sine_part,
            back_part * cosine + front_part * sine_part,
            head_rows[..., ROT:],
        ],
        axis=-1,
    )


def split_small(gain_parts):
    marks = [0, D, 2 * D, 3 * D, 4 * D, 5 * D, 6 * D, 9 * D, 9 * D + FF, 10 * D + FF]
    return tuple((gain_parts[marks[number] : marks[number + 1]] for number in range(9)))


def gelu_exact(values):
    return jax.nn.gelu(values, approximate=False)


def combine_totals(earlier, later_part):
    highest = jnp.maximum(earlier[0], later_part[0])
    totals = earlier[1] * jnp.exp(earlier[0] - highest) + later_part[1] * jnp.exp(
        later_part[0] - highest
    )
    return (highest, totals, earlier[2] + later_part[2])


def allowed_mask(query_places, key_places, span_start):
    inside_query = (query_places >= span_start) & (query_places < span_start + PIC)
    inside_key = (key_places >= span_start) & (key_places < span_start + PIC)
    return (key_places[None, :] <= query_places[:, None]) | inside_query[:, None] & inside_key[
        None, :
    ]


def masked_scores(queries, keys_all, allowed):
    raw_scores = jnp.einsum(
        "qhd,khd->hqk", queries, keys_all, preferred_element_type=jnp.float32
    ) * HD ** (-0.5)
    return jnp.where(allowed[None], raw_scores, -1e30)


def adamw(weight, gradient, moment, square, rate_value):
    moment = BETA_FIRST * moment + (1.0 - BETA_FIRST) * gradient
    square = BETA_SECOND * square + (1.0 - BETA_SECOND) * gradient * gradient
    moment_hat = moment / (1.0 - BETA_FIRST**STEP)
    square_hat = square / (1.0 - BETA_SECOND**STEP)
    weight = weight - rate_value * (
        moment_hat / (jnp.sqrt(square_hat) + ADAM_EPS) + DECAY_RATE * weight
    )
    return (weight, moment, square)


def on_device(
    token_ids,
    pic_start,
    comp_pos,
    comp_tgt,
    proj_in,
    proj_back,
    small_params,
    head_table,
    embed_table,
    first_in,
    second_in,
    first_back,
    second_back,
    first_small,
    second_small,
    first_head,
    second_head,
    first_embed,
    second_embed,
):
    seq_dev = token_ids.shape[2]
    micro_count = token_ids.shape[0]
    vocab_dev = head_table.shape[1]
    rep_count = lax.axis_size("rep")
    seq_len = seq_dev * rep_count
    rep_at = lax.axis_index("rep")
    shard_at = lax.axis_index("shard")
    used_own = comp_pos[:, 0, :] < seq_dev
    marked = jnp.where(used_own, comp_tgt[:, 0, :], -1)
    ids_group, tgt_group = (
        lax.all_gather(token_ids[:, 0, :], "shard", axis=1, tiled=True),
        lax.all_gather(marked, "shard", axis=1, tiled=True),
    )
    in_low = proj_in.astype(jnp.bfloat16)
    back_low = proj_back.astype(jnp.bfloat16)
    small_low = small_params.astype(jnp.bfloat16)
    head_low = head_table.astype(jnp.bfloat16)
    table_low = embed_table.astype(jnp.bfloat16)
    own_places = rep_at * seq_dev + jnp.arange(seq_dev)
    key_places = jnp.arange(seq_len)
    own_float = own_places.astype(jnp.float32)
    vocab_ids = jnp.arange(vocab_dev)
    grad_in = jnp.zeros((D, 3 * D + FF), jnp.float32)
    grad_back = jnp.zeros((D + FF, D), jnp.float32)
    grad_small = jnp.zeros((10 * D + FF,), jnp.float32)
    grad_head = jnp.zeros(head_table.shape, jnp.float32)
    grad_embed = jnp.zeros(embed_table.shape, jnp.float32)
    loss_sum = jnp.zeros((), jnp.float32)
    count_sum = jnp.zeros((), jnp.float32)
    for micro_at in range(micro_count):
        wide_in, wide_back, wide_small = (
            lax.all_gather(in_low, "shard", axis=0, tiled=True),
            lax.all_gather(back_low, "shard", axis=0, tiled=True),
            lax.all_gather(small_low, "shard", axis=0, tiled=True),
        )
        (
            gain_one,
            shift_one,
            gain_two,
            shift_two,
            gain_last,
            shift_last,
            bias_qkv,
            bias_hidden,
            bias_out,
        ) = split_small(wide_small.astype(jnp.float32))
        columns = jnp.take(table_low, ids_group[micro_at], axis=1)
        arrived = lax.all_to_all(columns, "shard", split_axis=1, concat_axis=0, tiled=True)
        residual = arrived.T.astype(jnp.float32)
        normed_one = norm_rows(residual, gain_one, shift_one)
        normed_two = norm_rows(residual, gain_two, shift_two)
        low_one = normed_one.astype(jnp.bfloat16)
        low_two = normed_two.astype(jnp.bfloat16)
        projected = (
            jnp.dot(low_one, wide_in[:, : 3 * D], preferred_element_type=jnp.float32) + bias_qkv
        )
        queries = rotate(projected[:, :D].reshape(seq_dev, H, HD), own_float).astype(jnp.bfloat16)
        key_rows = (
            rotate(projected[:, D : 2 * D].reshape(seq_dev, H, HD), own_float)
            .astype(jnp.bfloat16)
            .reshape(seq_dev, D)
        )
        value_rows = projected[:, 2 * D :].astype(jnp.bfloat16)
        keys_all, values_all = (
            lax.all_gather(key_rows, "rep", axis=0, tiled=True),
            lax.all_gather(value_rows, "rep", axis=0, tiled=True),
        )
        keys_all = keys_all.reshape(seq_len, H, HD)
        values_all = values_all.reshape(seq_len, H, HD)
        allowed = allowed_mask(own_places, key_places, pic_start[micro_at, 0])
        scores = masked_scores(queries, keys_all, allowed)
        highest = jnp.max(scores, axis=-1, keepdims=True)
        exponent = jnp.exp(scores - highest)
        totals = jnp.sum(exponent, axis=-1, keepdims=True)
        logsum = highest + jnp.log(totals)
        attn_probs = (exponent / totals).astype(jnp.bfloat16)
        attended = (
            jnp.einsum("hqk,khd->qhd", attn_probs, values_all, preferred_element_type=jnp.float32)
            .reshape(seq_dev, D)
            .astype(jnp.bfloat16)
        )
        hidden_pre = (
            jnp.dot(low_two, wide_in[:, 3 * D :], preferred_element_type=jnp.float32) + bias_hidden
        )
        activation = gelu_exact(hidden_pre).astype(jnp.bfloat16)
        joined = jnp.concatenate([attended, activation], axis=1)
        after_add = (
            residual + jnp.dot(joined, wide_back, preferred_element_type=jnp.float32) + bias_out
        )
        final_rows = norm_rows(after_add, gain_last, shift_last)
        places = comp_pos[micro_at, 0]
        used_slots = (places < seq_dev).astype(jnp.float32)
        picked = (
            jnp.take(final_rows, jnp.minimum(places, seq_dev - 1), axis=0) * used_slots[:, None]
        ).astype(jnp.bfloat16)
        rows_all = lax.all_gather(picked, "shard", axis=0, tiled=True)
        logits = jnp.dot(rows_all, head_low, preferred_element_type=jnp.float32)
        targets = tgt_group[micro_at]
        matches = (targets - shard_at * vocab_dev)[:, None] == vocab_ids[None, :]
        row_top = jnp.max(logits, axis=1)
        row_total = jnp.sum(jnp.exp(logits - row_top[:, None]), axis=1)
        row_target = jnp.sum(jnp.where(matches, logits, 0.0), axis=1)
        row_top, row_total, row_target = combined_all(
            (row_top, row_total, row_target), "shard", combine_totals
        )
        logsum_rows = row_top + jnp.log(row_total)
        counted = (targets >= 0).astype(jnp.float32)
        loss_sum = loss_sum + jnp.sum((logsum_rows - row_target) * counted)
        count_sum = count_sum + jnp.sum(counted)
        d_logits = (
            (jnp.exp(logits - logsum_rows[:, None]) - matches.astype(jnp.float32))
            * counted[:, None]
        ).astype(jnp.bfloat16)
        grad_head = grad_head + jnp.einsum(
            "rd,rv->dv", rows_all, d_logits, preferred_element_type=jnp.float32
        )
        d_picked = lax.psum_scatter(
            jnp.einsum("rv,dv->rd", d_logits, head_low, preferred_element_type=jnp.float32),
            "shard",
            scatter_dimension=0,
            tiled=True,
        )
        d_final = jnp.zeros((seq_dev, D), jnp.float32).at[places].add(d_picked, mode="drop")
        back_in, back_back = (
            lax.all_gather(in_low, "shard", axis=0, tiled=True),
            lax.all_gather(back_low, "shard", axis=0, tiled=True),
        )
        _, pull_last = jax.vjp(norm_rows, after_add, gain_last, shift_last)
        d_after, d_gain_last, d_shift_last = pull_last(d_final)
        d_branch = d_after.astype(jnp.bfloat16)
        grad_back = grad_back + jnp.einsum(
            "sc,sd->cd", joined, d_branch, preferred_element_type=jnp.float32
        )
        d_joined = jnp.einsum("sd,cd->sc", d_branch, back_back, preferred_element_type=jnp.float32)
        d_attended = d_joined[:, :D].astype(jnp.bfloat16).reshape(seq_dev, H, HD)
        _, pull_gelu = jax.vjp(gelu_exact, hidden_pre)
        d_hidden = pull_gelu(d_joined[:, D:])[0].astype(jnp.bfloat16)
        probs_again = jnp.exp(masked_scores(queries, keys_all, allowed) - logsum)
        d_probs = jnp.einsum(
            "qhd,khd->hqk", d_attended, values_all, preferred_element_type=jnp.float32
        )
        d_scores = (
            probs_again * (d_probs - jnp.sum(probs_again * d_probs, axis=-1, keepdims=True))
        ).astype(jnp.bfloat16)
        d_queries = jnp.einsum(
            "hqk,khd->qhd", d_scores, keys_all, preferred_element_type=jnp.float32
        ) * HD ** (-0.5)
        low_probs = probs_again.astype(jnp.bfloat16)
        d_keys = jnp.einsum(
            "hqk,qhd->khd", d_scores, queries, preferred_element_type=jnp.float32
        ) * HD ** (-0.5)
        d_values = jnp.einsum(
            "hqk,qhd->khd", low_probs, d_attended, preferred_element_type=jnp.float32
        )
        key_grads = lax.psum_scatter(
            jnp.concatenate(
                [
                    d_keys.reshape(seq_dev * lax.axis_size("rep"), D),
                    d_values.reshape(seq_dev * lax.axis_size("rep"), D),
                ],
                axis=1,
            ),
            "rep",
            scatter_dimension=0,
            tiled=True,
        )
        d_key_rows = rotate(key_grads[:, :D].reshape(seq_dev, H, HD), -own_float).reshape(
            seq_dev, D
        )
        d_query_rows = rotate(d_queries, -own_float).reshape(seq_dev, D)
        d_projected = jnp.concatenate([d_query_rows, d_key_rows, key_grads[:, D:]], axis=1).astype(
            jnp.bfloat16
        )
        grad_in = grad_in + jnp.concatenate(
            [
                jnp.einsum("sd,sc->dc", low_one, d_projected, preferred_element_type=jnp.float32),
                jnp.einsum("sd,sc->dc", low_two, d_hidden, preferred_element_type=jnp.float32),
            ],
            axis=1,
        )
        d_normed_one = jnp.einsum(
            "sc,dc->sd", d_projected, back_in[:, : 3 * D], preferred_element_type=jnp.float32
        )
        d_normed_two = jnp.einsum(
            "sc,dc->sd", d_hidden, back_in[:, 3 * D :], preferred_element_type=jnp.float32
        )
        _, pull_one = jax.vjp(norm_rows, residual, gain_one, shift_one)
        d_resid_one, d_gain_one, d_shift_one = pull_one(d_normed_one)
        _, pull_two = jax.vjp(norm_rows, residual, gain_two, shift_two)
        d_resid_two, d_gain_two, d_shift_two = pull_two(d_normed_two)
        d_residual = (d_after + d_resid_one + d_resid_two).astype(jnp.bfloat16)
        returned = lax.all_to_all(d_residual.T, "shard", split_axis=0, concat_axis=1, tiled=True)
        grad_embed = grad_embed.at[:, ids_group[micro_at]].add(returned.astype(jnp.float32))
        grad_small = grad_small + jnp.concatenate(
            [
                d_gain_one,
                d_shift_one,
                d_gain_two,
                d_shift_two,
                d_gain_last,
                d_shift_last,
                jnp.sum(d_projected.astype(jnp.float32), axis=0),
                jnp.sum(d_hidden.astype(jnp.float32), axis=0),
                jnp.sum(d_branch.astype(jnp.float32), axis=0),
            ]
        )
    shard_in, shard_back, shard_small = (
        lax.psum_scatter(grad_in, "shard", scatter_dimension=0, tiled=True),
        lax.psum_scatter(grad_back, "shard", scatter_dimension=0, tiled=True),
        lax.psum_scatter(grad_small, "shard", scatter_dimension=0, tiled=True),
    )
    summed = lax.psum(
        (shard_in, shard_back, shard_small, grad_head, grad_embed, loss_sum, count_sum), "rep"
    )
    local_square = (
        jnp.sum(summed[0] * summed[0])
        + jnp.sum(summed[1] * summed[1])
        + jnp.sum(summed[2] * summed[2])
        + jnp.sum(summed[3] * summed[3])
        + jnp.sum(summed[4] * summed[4])
    )
    norm_value = jnp.sqrt(lax.psum(local_square, "shard"))
    factor = CLIP_LEVEL / jnp.maximum(norm_value, CLIP_LEVEL)
    next_in, moment_in, square_in = adamw(proj_in, summed[0] * factor, first_in, second_in, RATE_IN)
    next_back, moment_back, square_back = adamw(
        proj_back, summed[1] * factor, first_back, second_back, RATE_BACK
    )
    next_small, moment_small, square_small = adamw(
        small_params, summed[2] * factor, first_small, second_small, RATE_SMALL
    )
    next_head, moment_head, square_head = adamw(
        head_table, summed[3] * factor, first_head, second_head, RATE_HEAD
    )
    next_embed, moment_embed, square_embed = adamw(
        embed_table, summed[4] * factor, first_embed, second_embed, RATE_EMBED
    )
    return (
        jnp.stack([summed[5], summed[6]]),
        norm_value.reshape(1),
        next_in,
        moment_in,
        square_in,
        next_back,
        moment_back,
        square_back,
        next_small,
        moment_small,
        square_small,
        next_head,
        moment_head,
        square_head,
        next_embed,
        moment_embed,
        square_embed,
    )


def solution(mesh):
    placed = (
        P(None, "shard", "rep"),
        P(None, "shard"),
        P(None, "shard", "rep"),
        P(None, "shard", "rep"),
        P("shard", None),
        P("shard", None),
        P("shard"),
        P(None, "shard"),
        P("shard", None),
        P("shard", None),
        P("shard", None),
        P("shard", None),
        P("shard", None),
        P("shard"),
        P("shard"),
        P(None, "shard"),
        P(None, "shard"),
        P("shard", None),
        P("shard", None),
    )
    return jax.shard_map(
        on_device,
        mesh=mesh,
        in_specs=placed,
        out_specs=(
            P(),
            P(),
            P("shard", None),
            P("shard", None),
            P("shard", None),
            P("shard", None),
            P("shard", None),
            P("shard", None),
            P("shard"),
            P("shard"),
            P("shard"),
            P(None, "shard"),
            P(None, "shard"),
            P(None, "shard"),
            P("shard", None),
            P("shard", None),
            P("shard", None),
        ),
        check_vma=False,
    )
```

profile of v0, /device:TPU:0, one launch (start us, length us, event | category | flops | bytes accessed | tf_op | source)
XLA Modules:
  0.0 2981.0 jit_solution(18372402167705680473)
XLA Ops:
  10.8 26.1 copy.149
  36.8 14.8 convert_element_type.247
  51.6 22.5 all-gather.1
  88.2 10.4 gather_fusion.2
  106.5 36.8 %all-gather.8 = bf16[8,1,1792]{2,1,0:T(2,128)(2,1)S(1)} all-gather(bf16[1,1,1792]{2,1,0:T(2,128)(2,1)S(1)} %reshape.857), channel_id=1, replica_groups=mesh['rep'=4,'shard'=8] {'shard'}, dimensions={0}, use_global_device_ids=true | all-gather | bytes 32256 | tf_op jit(solution)/shard_map/all_gather | solution.py:160
  144.2 76.3 %all-gather.22.cloned.1.call-done = bf16[1024,7168]{1,0:T(8,128)(2,1)} async-done(((bf16[128,7168]{1,0:T(8,128)(2,1)}), bf16[1024,7168]{1,0:T(8,128)(2,1)}) %all-gather.22.cloned.1.call-update) | async-done | bytes 14680080 | tf_op jit(solution)/shard_map/all_gather | solution.py:158
  241.9 13.6 convert_element_type.269
  256.5 31.0 %all-gather = s32[2,1,256]{0,1,2:T(1,128)S(1)} all-gather(s32[2,1,32]{0,1,2:T(1,128)S(1)} %copy.148), channel_id=2, replica_groups=mesh['rep'=4,'shard'=8] {'shard'}, dimensions={2}, use_global_device_ids=true | all-gather | bytes 2304 | tf_op jit(solution)/shard_map/all_gather | solution.py:138
  299.7 20.3 subtract_reduce_fusion
  322.2 9.6 multiply_convert_fusion.5
  331.8 10.6 multiply_convert_fusion.4
  353.7 69.8 %all-gather.28.cloned.1.call-done = bf16[5120,1024]{1,0:T(8,128)(2,1)} async-done(((bf16[640,1024]{1,0:T(8,128)(2,1)}), bf16[5120,1024]{1,0:T(8,128)(2,1)}) %all-gather.28.cloned.1.call-update) | async-done | bytes 10485776 | tf_op jit(solution)/shard_map/all_gather | solution.py:159
  429.7 10.9 all-gather.32.cloned.1.call-done
  446.0 13.3 all-gather.30.cloned.1.call-done
  472.0 31.5 %all_gather.92 = bf16[256,1024]{1,0:T(8,128)(2,1)S(1)} all-gather(bf16[32,1024]{1,0:T(8,128)(2,1)S(1)} %fusion.75), channel_id=1, replica_groups=mesh['rep'=4,'shard'=8] {'shard'}, dimensions={0}, use_global_device_ids=true | all-gather | bytes 589824 | tf_op jit(solution)/shard_map/all_gather | solution.py:222
  513.2 20.4 all-gather.13
  533.6 16.4 all-gather.14
  550.0 18.3 all-gather.12
  569.0 31.3 %all_gather.83 = bf16[256,1024]{1,0:T(8,128)(2,1)S(1)} all-gather(bf16[32,1024]{1,0:T(8,128)(2,1)S(1)} %fusion.76), channel_id=1, replica_groups=mesh['rep'=4,'shard'=8] {'shard'}, dimensions={0}, use_global_device_ids=true | all-gather | bytes 589824 | tf_op jit(solution)/shard_map/all_gather | solution.py:222
  610.0 16.5 all-gather.10
  626.5 18.1 all-gather.11
  644.6 16.5 all-gather.9
  662.3 11.2 fusion.109
  674.9 11.4 fusion.108
  686.5 48.2 %reduce-scatter.11.cloned.1.call-done = f32[32,1024]{1,0:T(8,128)} async-done(((f32[256,1024]{1,0:T(8,128)}), f32[32,1024]{1,0:T(8,128)}) %reduce-scatter.11.cloned.1.call-update) | async-done | bytes 131088 | tf_op jit(solution)/shard_map/reduce_scatter | solution.py:243
  736.1 65.5 %reduce-scatter.7.cloned.1.call-done = f32[32,1024]{1,0:T(8,128)} async-done(((f32[256,1024]{1,0:T(8,128)}), f32[32,1024]{1,0:T(8,128)}) %reduce-scatter.7.cloned.1.call-update) | async-done | bytes 131088 | tf_op jit(solution)/shard_map/reduce_scatter | solution.py:243
  848.8 11.9 fusion.64
  860.7 13.7 convolution_add_fusion.1
  905.6 10.8 reduce-scatter.9.cloned.1.call-done
  936.9 30.4 %maximum_add_fusion = f32[1024,7168]{1,0:T(8,128)} fusion(f32[1024,4096]{1,0:T(8,128)} %fusion.100, f32[1024,3072]{1,0:T(8,128)} %fusion.99, f32[1024,4096]{1,0:T(8,128)} %fusion.102, f32[1024,3072]{1,0:T(8,128)} %fusion.101), kind=kLoop, calls=%fused_computation.18 | loop fusion | flops 22020096 | bytes 88080384 | tf_op jit(solution)/shard_map/add | solution.py:300
  968.1 15.8 fusion.107
  1008.5 15.4 all-to-all-done.2
  1027.3 18.4 convolution_add_fusion
  1045.8 16.7 scatter_custom_fusion.2
  1062.6 23.4 scatter_fusion
  1086.0 191.7 %reduce-scatter.17.cloned.1.call-done = f32[640,1024]{1,0:T(8,128)} async-done(((f32[5120,1024]{1,0:T(8,128)}), f32[640,1024]{1,0:T(8,128)}) %reduce-scatter.17.cloned.1.call-update) | async-done | bytes 2621456 | tf_op jit(solution)/shard_map/reduce_scatter | solution.py:335
  1277.7 467.0 %reduce-scatter.15.cloned.1.call-done = f32[128,7168]{1,0:T(8,128)} async-done(((f32[1024,7168]{1,0:T(8,128)}), f32[128,7168]{1,0:T(8,128)}) %reduce-scatter.15.cloned.1.call-update) | async-done | bytes 3670032 | tf_op jit(solution)/shard_map/reduce_scatter | solution.py:334
  1744.7 25.9 copy.164
  1770.7 26.0 copy.165
  1801.3 35.5 %all-reduce = f32[14336]{0:T(1024)S(1)} all-reduce(f32[14336]{0:T(1024)S(1)} %add.589), channel_id=16, replica_groups=mesh['rep'=4,'shard'=8] {'shard'}, use_global_device_ids=true, to_apply=%region_64.67.clone | all-reduce | flops 14336 | bytes 114688
  1846.4 854.2 %all-reduce.5.cloned.1.call-done = (f32[128,7168]{1,0:T(8,128)}, f32[640,1024]{1,0:T(8,128)}, f32[1024,6288]{0,1:T(8,128)}, f32[128,50304]{0,1:T(8,128)}) async-done(((f32[128,7168]{1,0:T(8,128)}, f32[640,1024]{1,0:T(8,128)}, f32[1024,6288]{0,1:T(8,128)}, f32[128,50304]{0,1:T(8,128)}), (f32[128,7168]{1,0:T(8,128)}, f32[640,1024]{1,0:T(8,128)}, f32[1024,6288]{0,1:T(8,128)}, ...) | async-done | bytes 57802768 | tf_op jit(solution)/shard_map/psum | solution.py:338
  2705.6 12.8 multiply_reduce_fusion.1
  2733.7 22.0 psum.63
  2756.5 60.9 %multiply_subtract_fusion = (f32[128,50304]{0,1:T(8,128)}, f32[128,50304]{0,1:T(8,128)}, f32[128,50304]{0,1:T(8,128)}) fusion(f32[128,50304]{0,1:T(8,128)} %copy.149, f32[128,50304]{0,1:T(8,128)} %get-tuple-element.546, f32[]{:T(128)S(6)} %div.228, f32[128,50304]{0,1:T(8,128)} %copy.164, f32[128,50304]{0,1:T(8,128)} %copy.165), kind=kLoop, calls=%fused_computation.21 | loop fusion | flops 103022592 | bytes 180289536 | tf_op jit(solution)/shard_map/sub | solution.py:100
  2817.4 25.8 copy.168
  2843.2 25.8 copy.169
  2869.1 25.8 copy.170
  2894.9 61.7 %multiply_subtract_fusion.1 = (f32[1024,6288]{0,1:T(8,128)}, f32[1024,6288]{0,1:T(8,128)}, f32[1024,6288]{0,1:T(8,128)}) fusion(f32[1024,6288]{0,1:T(8,128)} %param.34, f32[1024,6288]{0,1:T(8,128)} %get-tuple-element.545, f32[]{:T(128)S(6)} %div.228, f32[1024,6288]{0,1:T(8,128)} %param.42, f32[1024,6288]{0,1:T(8,128)} %param.43), kind=kLoop, calls=%fused_computation.23 | loop fusion | flops 103022592 | bytes 180289536 | tf_op jit(solution)/shard_map/sub | solution.py:100
  (548 shorter events, 292.6 us)
Async XLA Ops:
  7.2 213.4 %all-gather.22.cloned.1.call-start = ((), (), s32[]{:S(2)}) async-start(), calls=%async_computation.10 | async-start | bytes 16515072 | tf_op jit(solution)/shard_map/all_gather | solution.py:158
  84.8 14.8 all-to-all-start
  99.6 43.9 %all-to-all-start.1 = ((bf16[128,8,128]{0,2,1:T(8,128)(2,1)}), bf16[128,8,128]{0,2,1:T(8,128)(2,1)S(1)}, u32[]{:S(2)}, u32[]{:S(2)}) async-start(bf16[128,8,128]{0,2,1:T(8,128)(2,1)} %bitcast.33), calls=%async_computation.1 | async-start | bytes 524288 | tf_op jit(solution)/shard_map/all_to_all | solution.py:174
  105.8 236.6 %all-gather.26.cloned.1.call-start = ((), (), s32[]{:S(2)}) async-start(), calls=%async_computation.12 | async-start | bytes 1310720 | tf_op jit(solution)/shard_map/all_gather | solution.py:191
  143.4 83.4 %copy-start.61 = (f32[1024]{0:T(1024)}, f32[1024]{0:T(1024)S(1)}, u32[]{:S(2)}) copy-start(f32[1024]{0:T(1024)S(1)} %get-tuple-element.622) | copy-start | bytes 12292
  143.5 83.4 %copy-start.63 = (f32[1024]{0:T(1024)}, f32[1024]{0:T(1024)S(1)}, u32[]{:S(2)}) copy-start(f32[1024]{0:T(1024)S(1)} %get-tuple-element.621) | copy-start | bytes 12292
  143.7 178.5 %copy-start.82 = (f32[128]{0:T(128)}, f32[128]{0:T(128)S(1)}, u32[]{:S(2)}) copy-start(f32[128]{0:T(128)S(1)} %broadcast_multiply_fusion.3) | copy-start | bytes 1540
  143.9 80.5 %copy-start.111 = (f32[128]{0:T(128)}, f32[128]{0:T(128)S(1)}, u32[]{:S(2)}) copy-start(f32[128]{0:T(128)S(1)} %multiply_reduce_fusion.21) | copy-start | bytes 1540
  144.0 187.9 %copy-start.80 = (f32[128]{0:T(128)}, f32[128]{0:T(128)S(1)}, u32[]{:S(2)}) copy-start(f32[128]{0:T(128)S(1)} %broadcast_multiply_fusion.1) | copy-start | bytes 1540
  144.2 80.3 %copy-start.113 = (f32[128]{0:T(128)}, f32[128]{0:T(128)S(1)}, u32[]{:S(2)}) copy-start(f32[128]{0:T(128)S(1)} %multiply_reduce_fusion.19) | copy-start | bytes 1540
  144.2 178.0 %copy-start.86 = (f32[128]{0:T(128)}, f32[128]{0:T(128)S(1)}, u32[]{:S(2)}) copy-start(f32[128]{0:T(128)S(1)} %fusion.86) | copy-start | bytes 1540
  144.2 187.6 %copy-start.84 = (f32[128]{0:T(128)}, f32[128]{0:T(128)S(1)}, u32[]{:S(2)}) copy-start(f32[128]{0:T(128)S(1)} %fusion.88) | copy-start | bytes 1540
  235.0 112.8 %all-gather.24.cloned.1.call-start = ((), (), s32[]{:S(2)}) async-start(), calls=%async_computation.11 | async-start | bytes 1310720 | tf_op jit(solution)/shard_map/all_gather | solution.py:192
  236.9 186.7 %all-gather.28.cloned.1.call-start = ((), (), s32[]{:S(2)}) async-start(), calls=%async_computation.13 | async-start | bytes 11796480 | tf_op jit(solution)/shard_map/all_gather | solution.py:159
  240.0 200.7 %all-gather.32.cloned.1.call-start = ((), (), s32[]{:S(2)}) async-start(), calls=%async_computation.15 | async-start | bytes 1310720 | tf_op jit(solution)/shard_map/all_gather | solution.py:191
  256.4 203.0 %all-gather.30.cloned.1.call-start = ((), (), s32[]{:S(2)}) async-start(), calls=%async_computation.14 | async-start | bytes 1310720 | tf_op jit(solution)/shard_map/all_gather | solution.py:192
  297.0 365.3 %copy-start.107 = (f32[256]{0:T(256)}, f32[256]{0:T(256)S(1)}, u32[]{:S(2)}) copy-start(f32[256]{0:T(256)S(1)} %convert_element_type.286) | copy-start | bytes 3076
  297.0 377.8 %copy-start.109 = (f32[256]{0:T(256)}, f32[256]{0:T(256)S(1)}, u32[]{:S(2)}) copy-start(f32[256]{0:T(256)S(1)} %convert_element_type.285) | copy-start | bytes 3076
  320.0 342.4 %copy-start.88 = (s32[256]{0:T(256)}, s32[256]{0:T(256)S(1)}, u32[]{:S(2)}) copy-start(s32[256]{0:T(256)S(1)} %get-tuple-element.496) | copy-start | bytes 3076
  320.0 354.9 %copy-start.99 = (s32[256]{0:T(256)}, s32[256]{0:T(256)S(1)}, u32[]{:S(2)}) copy-start(s32[256]{0:T(256)S(1)} %get-tuple-element.497) | copy-start | bytes 3076
  320.2 120.5 %copy-start.49 = (bf16[128,16,48]{0,2,1:T(8,128)(2,1)}, bf16[128,16,48]{0,2,1:T(8,128)(2,1)S(1)}, u32[]{:S(2)}) copy-start(bf16[128,16,48]{0,2,1:T(8,128)(2,1)S(1)} %slice.443) | copy-start | bytes 589828
  322.1 412.6 %reduce-scatter.11.cloned.1.call-start = ((), (), s32[]{:S(2)}) async-start(), calls=%async_computation.18 | async-start | bytes 1179648 | tf_op jit(solution)/shard_map/reduce_scatter | solution.py:243
  353.7 75.8 %copy-start.57 = (bf16[128,1024]{1,0:T(8,128)(2,1)}, bf16[128,1024]{1,0:T(8,128)(2,1)S(1)}, u32[]{:S(2)}) copy-start(bf16[128,1024]{1,0:T(8,128)(2,1)S(1)} %copy.154) | copy-start | bytes 786436
  533.6 73.8 %copy-start.72 = (f32[8,1,256]{2,1,0:T(1,128)}, f32[8,1,256]{2,1,0:T(1,128)S(1)}, u32[]{:S(2)}) copy-start(f32[8,1,256]{2,1,0:T(1,128)S(1)} %all-gather.13) | copy-start | bytes 24580
  550.0 57.3 %copy-start.71 = (f32[8,1,256]{2,1,0:T(1,128)}, f32[8,1,256]{2,1,0:T(1,128)S(1)}, u32[]{:S(2)}) copy-start(f32[8,1,256]{2,1,0:T(1,128)S(1)} %all-gather.14) | copy-start | bytes 24580
  568.3 39.1 %copy-start.73 = (f32[8,1,256]{2,1,0:T(1,128)}, f32[8,1,256]{2,1,0:T(1,128)S(1)}, u32[]{:S(2)}) copy-start(f32[8,1,256]{2,1,0:T(1,128)S(1)} %all-gather.12) | copy-start | bytes 24580
  607.4 53.6 %slice-start = ((f32[8,1,256]{2,1,0:T(1,128)}), f32[1,1,256]{2,1,0:T(1,128)S(1)}, s32[]{:S(2)}) async-start(f32[8,1,256]{2,1,0:T(1,128)} %copy-done.71), calls=%async_computation.23 | async-start | bytes 2048 | tf_op jit(solution)/shard_map/jit(dynamic_index_in_dim)/dynamic_slice | solution.py:32
  607.4 53.6 %slice-start.1 = ((f32[8,1,256]{2,1,0:T(1,128)}), f32[1,1,256]{2,1,0:T(1,128)S(1)}, s32[]{:S(2)}) async-start(f32[8,1,256]{2,1,0:T(1,128)} %copy-done.72), calls=%async_computation.24 | async-start | bytes 2048 | tf_op jit(solution)/shard_map/jit(dynamic_index_in_dim)/dynamic_slice | solution.py:32
  607.4 53.6 %slice-start.2 = ((f32[8,1,256]{2,1,0:T(1,128)}), f32[1,1,256]{2,1,0:T(1,128)S(1)}, s32[]{:S(2)}) async-start(f32[8,1,256]{2,1,0:T(1,128)} %copy-done.73), calls=%async_computation.25 | async-start | bytes 2048 | tf_op jit(solution)/shard_map/jit(dynamic_index_in_dim)/dynamic_slice | solution.py:32
  673.6 128.1 %reduce-scatter.7.cloned.1.call-start = ((), (), s32[]{:S(2)}) async-start(), calls=%async_computation.16 | async-start | bytes 1179648 | tf_op jit(solution)/shard_map/reduce_scatter | solution.py:243
  686.2 216.8 %reduce-scatter.13.cloned.1.call-start = ((), (), s32[]{:S(2)}) async-start(), calls=%async_computation.19 | async-start | bytes 5242880 | tf_op jit(solution)/shard_map/reduce_scatter | solution.py:281
  825.0 91.4 %reduce-scatter.9.cloned.1.call-start = ((), (), s32[]{:S(2)}) async-start(), calls=%async_computation.17 | async-start | bytes 5242880 | tf_op jit(solution)/shard_map/reduce_scatter | solution.py:281
  848.8 428.9 %reduce-scatter.17.cloned.1.call-start = ((), (), s32[]{:S(2)}) async-start(), calls=%async_computation.21 | async-start | bytes 23592960 | tf_op jit(solution)/shard_map/reduce_scatter | solution.py:335
  874.5 870.2 %reduce-scatter.15.cloned.1.call-start = ((), (), s32[]{:S(2)}) async-start(), calls=%async_computation.20 | async-start | bytes 33030144 | tf_op jit(solution)/shard_map/reduce_scatter | solution.py:334
  1000.6 23.2 all-to-all-start.2
  1023.8 38.7 %all-to-all-start.3 = ((bf16[8,128,128]{1,2,0:T(8,128)(2,1)}), bf16[8,128,128]{1,2,0:T(8,128)(2,1)S(1)}, u32[]{:S(2)}, u32[]{:S(2)}) async-start(bf16[8,128,128]{1,2,0:T(8,128)(2,1)} %copy_bitcast_fusion), calls=%async_computation.9 | async-start | bytes 524288 | tf_op jit(solution)/shard_map/all_to_all | solution.py:318
  1027.3 1673.4 %all-reduce.5.cloned.1.call-start = ((), (), s32[]{:S(2)}) async-start(), calls=%async_computation.22 | async-start | bytes 115605504 | tf_op jit(solution)/shard_map/psum | solution.py:338
  1770.7 30.5 %copy-start.94 = (f32[1024]{0:T(1024)S(1)}, f32[1024]{0:T(1024)}, u32[]{:S(2)}) copy-start(f32[1024]{0:T(1024)} %get-tuple-element.566) | copy-start | bytes 12292
  1770.7 30.6 %copy-start.91 = (f32[1024]{0:T(1024)S(1)}, f32[1024]{0:T(1024)}, u32[]{:S(2)}) copy-start(f32[1024]{0:T(1024)} %get-tuple-element.480) | copy-start | bytes 12292
  1770.7 30.6 %copy-start.90 = (f32[1024]{0:T(1024)S(1)}, f32[1024]{0:T(1024)}, u32[]{:S(2)}) copy-start(f32[1024]{0:T(1024)} %get-tuple-element.495) | copy-start | bytes 12292
  1770.7 30.6 %copy-start.69 = (f32[4096]{0:T(1024)S(1)}, f32[4096]{0:T(1024)}, u32[]{:S(2)}) copy-start(f32[4096]{0:T(1024)} %get-tuple-element.572) | copy-start | bytes 49156
  1770.7 30.6 %copy-start.95 = (f32[1024]{0:T(1024)S(1)}, f32[1024]{0:T(1024)}, u32[]{:S(2)}) copy-start(f32[1024]{0:T(1024)} %get-tuple-element.570) | copy-start | bytes 12292
  1845.8 859.9 %copy-start.78 = (f32[1792]{0:T(1024)}, f32[1792]{0:T(1024)S(1)}, u32[]{:S(2)}) copy-start(f32[1792]{0:T(1024)S(1)} %get-tuple-element.542) | copy-start | bytes 21508
  2894.9 61.7 %copy-start.77 = (f32[1792]{0:T(1024)S(1)}, f32[1792]{0:T(1024)}, u32[]{:S(2)}) copy-start(f32[1792]{0:T(1024)} %param.33) | copy-start | bytes 21508
  2894.9 61.7 %copy-start.79 = (f32[1792]{0:T(1024)S(1)}, f32[1792]{0:T(1024)}, u32[]{:S(2)}) copy-start(f32[1792]{0:T(1024)} %copy-done.78) | copy-start | bytes 21508
  2894.9 61.7 %copy-start.105 = (f32[1792]{0:T(1024)S(1)}, f32[1792]{0:T(1024)}, u32[]{:S(2)}) copy-start(f32[1792]{0:T(1024)} %param.40) | copy-start | bytes 21508
  2894.9 61.8 %copy-start.106 = (f32[1792]{0:T(1024)S(1)}, f32[1792]{0:T(1024)}, u32[]{:S(2)}) copy-start(f32[1792]{0:T(1024)} %param.41) | copy-start | bytes 21508
  2894.9 62.4 %copy-start.12 = (f32[640,1024]{1,0:T(8,128)S(1)}, f32[640,1024]{1,0:T(8,128)}, u32[]{:S(2)}) copy-start(f32[640,1024]{1,0:T(8,128)} %get-tuple-element.544) | copy-start | bytes 7864324
  (98 other events, 851.1 us)
Sparse Core Ops, SparseCore 0:
  10.9 209.6 all-gather.21
  235.1 15.9 all-gather.25
  253.2 16.7 all-gather.23
  272.6 150.9 all-gather.27
  425.5 15.0 all-gather.31
  442.6 16.6 all-gather.29
  673.7 61.0 reduce-scatter.10
  739.1 62.4 reduce-scatter.6
  825.1 43.5 reduce-scatter.12
  871.8 44.5 reduce-scatter.8
  920.8 356.8 reduce-scatter.16
  1281.4 463.1 reduce-scatter.14
  1748.1 952.5 all-reduce.4
where the time goes:
time: 2990 us; the launch traced here: 2980 us
  waiting for transfers between devices  1820 us (61%)
  other arithmetic  346 us (12%)
  blocking collectives  326 us (11%)
  matrix products  223 us (7%)
  local copies, waits for them, and re-layouts  216 us (7%)
    psum x1, waiting for transfers between devices, on_device(): lax.psum((shard_in, shard_back, shard_small, grad_head, grad_embed, loss_...  854 us
    reduce_scatter x1, waiting for transfers between devices, on_device(): lax.psum_scatter(grad_in, 'shard', scatter_dimension=0, tiled=True)  467 us
    reduce_scatter x1, waiting for transfers between devices, on_device(): lax.psum_scatter(grad_back, 'shard', scatter_dimension=0, tiled=True)  192 us
    unnamed x283, local copies, waits for them, and re-layouts  175 us
    sub x5, other arithmetic, adamw(): weight - rate_value * (moment_hat / (jnp.sqrt(square_hat) + ADAM_EPS) + D...  138 us
    reduce_scatter x2, waiting for transfers between devices, on_device(): lax.psum_scatter(jnp.einsum('rv,dv->rd', d_logits, head_low, preferred_el...  114 us
    all_gather x6, blocking collectives, combined_all(): gathered = jax.tree.map(lambda a: lax.all_gather(a, axis), part)  106 us
    all_gather x1, waiting for transfers between devices, on_device(): lax.all_gather(in_low, 'shard', axis=0, tiled=True)  76.3 us
  transfers between devices with their start and end apart: 17, of which 11 were waited for; matrix products, arithmetic and copies ran while one was open for 15% of the time, Pallas kernels for 0%

commit v1 on v0

--- a/solution.py
+++ b/solution.py
@@ -1,6 +1,10 @@
+import functools
+
 import jax
 import jax.numpy as jnp
 from jax import lax
+from jax.experimental import pallas as pl
+from jax.experimental.pallas import tpu as pltpu
 from jax.sharding import PartitionSpec as P
 
 D = 1024
@@ -103,7 +107,7 @@
     return (weight, moment, square)
 
 
-def on_device(
+def any_mesh(
     token_ids,
     pic_start,
     comp_pos,
@@ -381,6 +385,1211 @@
     )
 
 
+MESH = pl.DeviceIdType.MESH
+RG = 4
+SG = 8
+
+
+def whereabouts():
+    rep = lax.axis_index("rep")
+    shard = lax.axis_index("shard")
+    core_twin = rep + 1 - 2 * lax.rem(rep, 2)
+    x_twin = lax.rem(rep + 2, RG)
+    y_twin = shard + 1 - 2 * lax.rem(shard, 2)
+    return rep, shard, core_twin, x_twin, y_twin
+
+
+def z_peer(shard, step):
+    return lax.rem(shard + 2 * step, SG)
+
+
+def shard_peer(shard, step):
+    return lax.rem(shard + step, SG)
+
+
+def greet(partners):
+    barrier = pltpu.get_barrier_semaphore()
+    for partner in partners:
+        pl.semaphore_signal(barrier, inc=1, device_id=partner, device_id_type=MESH)
+    pl.semaphore_wait(barrier, len(partners))
+
+
+def remote(src, dst, send_sem, recv_sem, partner):
+    return pltpu.make_async_remote_copy(
+        src_ref=src,
+        dst_ref=dst,
+        send_sem=send_sem,
+        recv_sem=recv_sem,
+        device_id=partner,
+        device_id_type=MESH,
+    )
+
+
+def comm_call(kernel, out_shape, scratch, number, args, spaces=None, out_spaces=None, limit=None):
+    any_spec = pl.BlockSpec(memory_space=pl.ANY)
+    vmem_spec = pl.BlockSpec(memory_space=pltpu.VMEM)
+    pick = {"a": any_spec, "v": vmem_spec}
+    spaces = spaces or "a" * len(args)
+    out_spaces = out_spaces or "a" * len(out_shape)
+    return pl.pallas_call(
+        kernel,
+        out_shape=out_shape,
+        in_specs=[pick[space] for space in spaces],
+        out_specs=[pick[space] for space in out_spaces],
+        scratch_shapes=scratch,
+        compiler_params=pltpu.CompilerParams(
+            collective_id=number, has_side_effects=True, vmem_limit_bytes=limit
+        ),
+    )(*args)
+
+
+def facts_kernel(ints, smalls, ints_all, smalls_all, send_int, recv_int, send_small, recv_small, send_rep, recv_rep, own):
+    rep, shard, _, _, _ = whereabouts()
+    shard_peers = [(rep, shard_peer(shard, step)) for step in range(1, SG)]
+    rep_peers = [(lax.rem(rep + step, RG), shard) for step in range(1, RG)]
+    greet(shard_peers + rep_peers)
+    copies = []
+    for at, peer in enumerate(shard_peers):
+        copies.append(remote(ints, ints_all.at[rep, shard], send_int.at[at], recv_int.at[at], peer))
+        copies[-1].start()
+    small_copies = []
+    for at, peer in enumerate(shard_peers):
+        small_copies.append(remote(smalls, smalls_all.at[shard], send_small.at[at], recv_small.at[at], peer))
+        small_copies[-1].start()
+    keep_int = pltpu.make_async_copy(ints, ints_all.at[rep, shard], own.at[0])
+    keep_small = pltpu.make_async_copy(smalls, smalls_all.at[shard], own.at[1])
+    keep_int.start()
+    keep_small.start()
+    keep_int.wait()
+    for copy in copies:
+        copy.wait()
+    rep_copies = []
+    for at, peer in enumerate(rep_peers):
+        rep_copies.append(remote(ints_all.at[rep], ints_all.at[rep], send_rep.at[at], recv_rep.at[at], peer))
+        rep_copies[-1].start()
+    keep_small.wait()
+    for copy in small_copies + rep_copies:
+        copy.wait()
+
+
+def share_facts(ints, smalls, number):
+    dma = pltpu.SemaphoreType.DMA
+    return comm_call(
+        facts_kernel,
+        [
+            jax.ShapeDtypeStruct((RG, SG) + ints.shape, ints.dtype),
+            jax.ShapeDtypeStruct((SG,) + smalls.shape, smalls.dtype),
+        ],
+        [dma((SG - 1,))] * 4 + [dma((RG - 1,))] * 2 + [dma((2,))],
+        number,
+        (ints, smalls),
+        "vv",
+        "vv",
+    )
+
+
+def start_gather(source, out, slot, place, sems):
+    send_z, recv_z, send_y, recv_y, own = sems
+    rep, shard, _, _, y_twin = place
+    keep = pltpu.make_async_copy(source, slot(out, shard), own)
+    keep.start()
+    first_y = remote(source, slot(out, shard), send_y.at[0], recv_y.at[0], (rep, y_twin))
+    z_copies = [
+        remote(source, slot(out, shard), send_z.at[step - 1], recv_z.at[step - 1], (rep, z_peer(shard, step)))
+        for step in range(1, 4)
+    ]
+    for copy in z_copies:
+        copy.start()
+    first_y.start()
+    return keep, first_y, z_copies
+
+
+def finish_gather(started, out, slot, place, sems):
+    send_z, recv_z, send_y, recv_y, own = sems
+    rep, shard, _, _, y_twin = place
+    keep, first_y, z_copies = started
+    passed = []
+    for step in range(1, 4):
+        z_copies[step - 1].wait_recv()
+        came_from = z_peer(shard, SG // 2 - step)
+        passed.append(
+            remote(slot(out, came_from), slot(out, came_from), send_y.at[step], recv_y.at[step], (rep, y_twin))
+        )
+        passed[-1].start()
+    keep.wait()
+    for copy in z_copies:
+        copy.wait_send()
+    first_y.wait()
+    for copy in passed:
+        copy.wait()
+
+
+def gather_partners(place):
+    rep, shard, _, _, y_twin = place
+    return [(rep, z_peer(shard, step)) for step in range(1, 4)] + [(rep, y_twin)]
+
+
+GATHER_SEMS = [pltpu.SemaphoreType.DMA((3,)), pltpu.SemaphoreType.DMA((3,)), pltpu.SemaphoreType.DMA((4,)), pltpu.SemaphoreType.DMA((4,)), pltpu.SemaphoreType.DMA]
+
+
+def column_slot(out, index):
+    width = out.shape[1] // SG
+    return out.at[:, pl.ds(pl.multiple_of(index * width, width), width)]
+
+
+def row_slot(out, index):
+    height = out.shape[0] // SG
+    return out.at[pl.ds(pl.multiple_of(index * height, height), height)]
+
+
+def tile_user(tile):
+    return jnp.where(tile < SG, tile, (tile - SG) // 4)
+
+
+def tile_slot(tile):
+    return jnp.where(tile < SG, 0, 1 + lax.rem(tile - SG + SG, 4))
+
+
+def embed_kernel(rows, in_parts, back_tiles, out, in_all, back_all, *sems):
+    gather_sems = sems[:5]
+    send_in, recv_in, send_back, recv_back, own_in, send_pair, recv_pair = sems[5:]
+    place = whereabouts()
+    rep, shard, core_twin, _, _ = place
+    half = lax.rem(rep, 2)
+    greet([(rep, shard_peer(shard, step)) for step in range(1, SG)] + [(core_twin, shard)])
+    started = start_gather(rows, out, column_slot, place, gather_sems)
+    in_copies = []
+    for step in range(1, SG):
+        peer = shard_peer(shard, step)
+        in_copies.append(
+            remote(in_parts.at[peer, half], in_all.at[shard, half], send_in.at[step - 1], recv_in.at[step - 1], (rep, peer))
+        )
+        in_copies[-1].start()
+    keep_in = pltpu.make_async_copy(in_parts.at[shard, half], in_all.at[shard, half], own_in)
+    keep_in.start()
+    moves = []
+    for at in range(5):
+        tile = 5 * shard + at
+        user = tile_user(tile)
+        slot = tile_slot(tile)
+        there = remote(back_tiles.at[at, half], back_all.at[slot, half], send_back.at[at], recv_back.at[slot], (rep, user))
+        here = pltpu.make_async_copy(back_tiles.at[at, half], back_all.at[slot, half], recv_back.at[slot])
+
+        @pl.when(user == shard)
+        def _():
+            here.start()
+
+        @pl.when(user != shard)
+        def _():
+            there.start()
+
+        moves.append((user, there))
+    finish_gather(started, out, column_slot, place, gather_sems)
+    keep_in.wait()
+    for copy in in_copies:
+        copy.wait()
+    for slot in range(5):
+        pltpu.make_async_copy(back_tiles.at[0, half], back_all.at[slot, half], recv_back.at[slot]).wait()
+    pair_in = remote(in_all.at[:, half], in_all.at[:, half], send_pair.at[0], recv_pair.at[0], (core_twin, shard))
+    pair_back = remote(back_all.at[:, half], back_all.at[:, half], send_pair.at[1], recv_pair.at[1], (core_twin, shard))
+    pair_in.start()
+    pair_back.start()
+    for user, there in moves:
+
+        @pl.when(user != shard)
+        def _():
+            there.wait_send()
+
+    pair_in.wait()
+    pair_back.wait()
+
+
+def share_embedding(rows, in_parts, back_tiles, number):
+    dma = pltpu.SemaphoreType.DMA
+    return comm_call(
+        embed_kernel,
+        [
+            jax.ShapeDtypeStruct((rows.shape[0], SG * rows.shape[1]), rows.dtype),
+            jax.ShapeDtypeStruct(in_parts.shape, in_parts.dtype),
+            jax.ShapeDtypeStruct(back_tiles.shape, back_tiles.dtype),
+        ],
+        GATHER_SEMS + [dma((SG - 1,))] * 2 + [dma((5,))] * 2 + [dma] + [dma((2,))] * 2,
+        number,
+        (rows, in_parts, back_tiles),
+    )
+
+
+def gather_kernel(rows, out, *sems):
+    place = whereabouts()
+    greet(gather_partners(place))
+    started = start_gather(rows, out, row_slot, place, sems)
+    finish_gather(started, out, row_slot, place, sems)
+
+
+def shard_gather(rows, number):
+    return comm_call(
+        gather_kernel,
+        [jax.ShapeDtypeStruct((SG * rows.shape[0], rows.shape[1]), rows.dtype)],
+        GATHER_SEMS,
+        number,
+        (rows,),
+        "v",
+        "v",
+    )[0]
+
+
+def stats_kernel(stats, out, send, recv):
+    rep, shard, _, _, _ = whereabouts()
+    peers = [(rep, shard_peer(shard, step)) for step in range(1, SG)]
+    greet(peers)
+    copies = [remote(stats, out.at[shard], send.at[at], recv.at[at], peer) for at, peer in enumerate(peers)]
+    for copy in copies:
+        copy.start()
+    out[shard] = stats[...]
+    for copy in copies:
+        copy.wait()
+
+
+def shard_stats(stats, number):
+    dma = pltpu.SemaphoreType.DMA
+    return comm_call(
+        stats_kernel,
+        [jax.ShapeDtypeStruct((SG,) + stats.shape, stats.dtype)],
+        [dma((SG - 1,)), dma((SG - 1,))],
+        number,
+        (stats,),
+        "v",
+        "v",
+    )[0]
+
+
+def sum_sems():
+    dma = pltpu.SemaphoreType.DMA
+    return [dma((4,)), dma((4,)), dma((3,)), dma((3,))]
+
+
+def sum_buffers(chunk):
+    return [pltpu.VMEM((4,) + chunk, jnp.float32), pltpu.VMEM((4,) + chunk, jnp.float32), pltpu.VMEM((3,) + chunk, jnp.float32)]
+
+
+def start_sum(parts, place, buffers, sems):
+    rep, shard, _, _, y_twin = place
+    from_y, own_sum, from_z = buffers
+    send_y, recv_y, send_z, recv_z = sems
+    y_copies = {}
+    for step in (2, 1, 3, 0):
+        y_copies[step] = remote(
+            parts.at[z_peer(y_twin, step)], from_y.at[step], send_y.at[step], recv_y.at[step], (rep, y_twin)
+        )
+        y_copies[step].start()
+    return y_copies
+
+
+def finish_sum(y_copies, parts, out, place, buffers, sems, post=None):
+    rep, shard, _, _, y_twin = place
+    from_y, own_sum, from_z = buffers
+    send_y, recv_y, send_z, recv_z = sems
+    z_copies = []
+    for step in (2, 1, 3):
+        y_copies[step].wait_recv()
+        own_sum[step] = parts[z_peer(shard, step)] + from_y[step]
+        z_copies.append(
+            remote(own_sum.at[step], from_z.at[step - 1], send_z.at[step - 1], recv_z.at[step - 1], (rep, z_peer(shard, step)))
+        )
+        z_copies[-1].start()
+    y_copies[0].wait_recv()
+    total = parts[shard] + from_y[0]
+    for copy in z_copies:
+        copy.wait_recv()
+    out[...] = total + from_z[0] + from_z[1] + from_z[2]
+    for step in range(4):
+        y_copies[step].wait_send()
+    for copy in z_copies:
+        copy.wait_send()
+
+
+def sum_kernel(parts, out, from_y, own_sum, from_z, *sems):
+    place = whereabouts()
+    greet(gather_partners(place))
+    buffers = (from_y, own_sum, from_z)
+    y_copies = start_sum(parts, place, buffers, sems)
+    finish_sum(y_copies, parts, out, place, buffers, sems)
+
+
+def shard_sum(parts, number):
+    chunk = parts.shape[1:]
+    return comm_call(
+        sum_kernel,
+        [jax.ShapeDtypeStruct(chunk, jnp.float32)],
+        sum_buffers(chunk) + sum_sems(),
+        number,
+        (parts,),
+        "v",
+        "v",
+        40 << 20,
+    )[0]
+
+
+def picked_kernel(parts, rows, facts, out, rows_all, facts_all, from_y, own_sum, from_z, *sems):
+    place = whereabouts()
+    rep, shard, core_twin, x_twin, _ = place
+    sum_sem = sems[:4]
+    send_row, recv_row, send_fact, recv_fact, own = sems[4:]
+    rep_peers = [(lax.rem(rep + step, RG), shard) for step in range(1, RG)]
+    greet(gather_partners(place) + rep_peers)
+    buffers = (from_y, own_sum, from_z)
+    y_copies = start_sum(parts, place, buffers, sum_sem)
+    keep = pltpu.make_async_copy(rows, rows_all.at[rep], own)
+    keep.start()
+    to_x = remote(rows, rows_all.at[rep], send_row.at[0], recv_row.at[0], (x_twin, shard))
+    to_core = remote(rows, rows_all.at[rep], send_row.at[1], recv_row.at[1], (core_twin, shard))
+    to_x.start()
+    to_core.start()
+    fact_copies = [
+        remote(facts, facts_all.at[rep], send_fact.at[at], recv_fact.at[at], peer) for at, peer in enumerate(rep_peers)
+    ]
+    for copy in fact_copies:
+        copy.start()
+    facts_all[rep] = facts[...]
+    finish_sum(y_copies, parts, out, place, buffers, sum_sem)
+    to_x.wait_recv()
+    passed = remote(rows_all.at[x_twin], rows_all.at[x_twin], send_row.at[2], recv_row.at[2], (core_twin, shard))
+    passed.start()
+    keep.wait()
+    to_x.wait_send()
+    to_core.wait()
+    for copy in fact_copies:
+        copy.wait()
+    passed.wait()
+
+
+def sum_and_share(parts, rows, facts, number):
+    dma = pltpu.SemaphoreType.DMA
+    chunk = parts.shape[1:]
+    return comm_call(
+        picked_kernel,
+        [
+            jax.ShapeDtypeStruct(chunk, jnp.float32),
+            jax.ShapeDtypeStruct((RG,) + rows.shape, rows.dtype),
+            jax.ShapeDtypeStruct((RG,) + facts.shape, facts.dtype),
+        ],
+        sum_buffers(chunk) + sum_sems() + [dma((3,))] * 4 + [dma],
+        number,
+        (parts, rows, facts),
+        "vvv",
+        "vvv",
+        40 << 20,
+    )
+
+
+def branch_kernel(rows, pieces, out, features, *sems):
+    place = whereabouts()
+    rep, shard, _, _, _ = place
+    send, recv = sems[5:]
+    peers = [(rep, shard_peer(shard, step)) for step in range(1, SG)]
+    greet(peers)
+    started = start_gather(rows, out, row_slot, place, sems[:5])
+    copies = []
+    for at, peer in enumerate(peers):
+        copies.append(remote(pieces.at[peer[1]], features.at[shard], send.at[at], recv.at[at], peer))
+        copies[-1].start()
+    features[shard] = pieces[shard]
+    finish_gather(started, out, row_slot, place, sems[:5])
+    for copy in copies:
+        copy.wait()
+
+
+def share_branch(rows, pieces, number):
+    dma = pltpu.SemaphoreType.DMA
+    return comm_call(
+        branch_kernel,
+        [jax.ShapeDtypeStruct((SG * rows.shape[0], rows.shape[1]), rows.dtype), jax.ShapeDtypeStruct(pieces.shape, pieces.dtype)],
+        GATHER_SEMS + [dma((SG - 1,))] * 2,
+        number,
+        (rows, pieces),
+        "vv",
+        "vv",
+    )
+
+
+def layer_kernel(parts, stats, grad_in, grad_back, smalls, out, stats_all, sum_in, sum_back, smalls_out,
+                 from_y, own_sum, from_z, pair_in, pair_back, half_in, half_back, far_in, far_back, small_rep, small_sum, small_shard, *sems):
+    place = whereabouts()
+    rep, shard, core_twin, x_twin, _ = place
+    sum_sem = sems[:4]
+    send_stat, recv_stat, send_pair, recv_pair, send_far, recv_far, send_rep, recv_rep, send_small, recv_small = sems[4:]
+    shard_peers = [(rep, shard_peer(shard, step)) for step in range(1, SG)]
+    rep_peers = [(lax.rem(rep + step, RG), shard) for step in range(1, RG)]
+    greet(shard_peers + rep_peers)
+    buffers = (from_y, own_sum, from_z)
+    rep_copies = [
+        remote(smalls, small_rep.at[at], send_rep.at[at], recv_rep.at[at], peer) for at, peer in enumerate(rep_peers)
+    ]
+    for copy in rep_copies:
+        copy.start()
+    core_far = lax.rem(core_twin + 2, RG)
+    pair_copies = [
+        remote(grad_in.at[core_far], pair_in.at[1], send_pair.at[0], recv_pair.at[0], (core_twin, shard)),
+        remote(grad_back.at[core_far], pair_back.at[1], send_pair.at[1], recv_pair.at[1], (core_twin, shard)),
+        remote(grad_in.at[core_twin], pair_in.at[0], send_pair.at[2], recv_pair.at[2], (core_twin, shard)),
+        remote(grad_back.at[core_twin], pair_back.at[0], send_pair.at[3], recv_pair.at[3], (core_twin, shard)),
+    ]
+    for copy in pair_copies:
+        copy.start()
+    y_copies = start_sum(parts, place, buffers, sum_sem)
+    stat_copies = [
+        remote(stats, stats_all.at[shard], send_stat.at[at], recv_stat.at[at], peer) for at, peer in enumerate(shard_peers)
+    ]
+    for copy in stat_copies:
+        copy.start()
+    stats_all[shard] = stats[...]
+    pair_copies[0].wait()
+    pair_copies[1].wait()
+    half_in[...] = grad_in[x_twin] + pair_in[1]
+    half_back[...] = grad_back[x_twin] + pair_back[1]
+    far_copies = [
+        remote(half_in, far_in, send_far.at[0], recv_far.at[0], (x_twin, shard)),
+        remote(half_back, far_back, send_far.at[1], recv_far.at[1], (x_twin, shard)),
+    ]
+    for copy in far_copies:
+        copy.start()
+    for copy in rep_copies:
+        copy.wait()
+    small_sum[...] = smalls[...] + small_rep[0] + small_rep[1] + small_rep[2]
+    small_copies = [
+        remote(small_sum.at[peer[1]], small_shard.at[at], send_small.at[at], recv_small.at[at], peer)
+        for at, peer in enumerate(shard_peers)
+    ]
+    for copy in small_copies:
+        copy.start()
+    finish_sum(y_copies, parts, out, place, buffers, sum_sem)
+    pair_copies[2].wait()
+    pair_copies[3].wait()
+    for copy in far_copies:
+        copy.wait()
+    sum_in[...] = grad_in[rep] + pair_in[0] + far_in[...]
+    sum_back[...] = grad_back[rep] + pair_back[0] + far_back[...]
+    for copy in stat_copies + small_copies:
+        copy.wait()
+    total = small_sum[shard]
+    for at in range(SG - 1):
+        total = total + small_shard[at]
+    smalls_out[...] = total
+
+
+def layer_sums(parts, stats, grad_in, grad_back, smalls, number):
+    dma = pltpu.SemaphoreType.DMA
+    chunk = parts.shape[1:]
+    quarter_in, quarter_back, piece = grad_in.shape[1:], grad_back.shape[1:], smalls.shape[1:]
+    vmem = lambda shape: pltpu.VMEM(shape, jnp.float32)
+    shape = lambda dims: jax.ShapeDtypeStruct(dims, jnp.float32)
+    return comm_call(
+        layer_kernel,
+        [shape(chunk), shape((SG,) + stats.shape), shape(quarter_in), shape(quarter_back), shape(piece)],
+        sum_buffers(chunk)
+        + [vmem((2,) + quarter_in), vmem((2,) + quarter_back), vmem(quarter_in), vmem(quarter_back), vmem(quarter_in), vmem(quarter_back)]
+        + [vmem((3,) + smalls.shape), vmem(smalls.shape), vmem((SG - 1,) + piece)]
+        + sum_sems()
+        + [dma((SG - 1,))] * 2 + [dma((4,))] * 2 + [dma((2,))] * 2 + [dma((3,))] * 2 + [dma((SG - 1,))] * 2,
+        number,
+        (parts, stats, grad_in, grad_back, smalls),
+        "vvvvv",
+        "vvvvv",
+        62 << 20,
+    )
+
+
+def return_kernel(rows, sum_in, sum_back, rows_all, in_all, back_all, *sems):
+    place = whereabouts()
+    rep, shard, core_twin, x_twin, _ = place
+    (send_row, recv_row, own, send_in, recv_in, send_back, recv_back, send_far, recv_far, send_pair, recv_pair) = sems
+    greet([(rep, shard_peer(shard, step)) for step in range(1, SG)] + [(core_twin, shard), (x_twin, shard)])
+    in_copies = []
+    for step in range(1, SG):
+        peer = shard_peer(shard, step)
+        in_copies.append(
+            remote(sum_in.at[peer], in_all.at[rep, shard], send_in.at[step - 1], recv_in.at[step - 1], (rep, peer))
+        )
+        in_copies[-1].start()
+    keep_in = pltpu.make_async_copy(sum_in.at[shard], in_all.at[rep, shard], own.at[1])
+    keep_in.start()
+    moves = []
+    for slot in range(5):
+        tile = jnp.where(slot == 0, shard, SG + 4 * shard + slot - 1)
+        owner = tile // 5
+        at = lax.rem(tile, 5)
+        there = remote(sum_back.at[slot], back_all.at[rep, at], send_back.at[slot], recv_back.at[at], (rep, owner))
+        here = pltpu.make_async_copy(sum_back.at[slot], back_all.at[rep, at], recv_back.at[at])
+
+        @pl.when(owner == shard)
+        def _():
+            here.start()
+
+        @pl.when(owner != shard)
+        def _():
+            there.start()
+
+        moves.append((owner, there))
+    keep = pltpu.make_async_copy(rows, rows_all.at[rep], own.at[0])
+    keep.start()
+    to_x = remote(rows, rows_all.at[rep], send_row.at[0], recv_row.at[0], (x_twin, shard))
+    to_core = remote(rows, rows_all.at[rep], send_row.at[1], recv_row.at[1], (core_twin, shard))
+    to_x.start()
+    to_core.start()
+    keep_in.wait()
+    for copy in in_copies:
+        copy.wait()
+    in_far = remote(in_all.at[rep], in_all.at[rep], send_far.at[0], recv_far.at[0], (x_twin, shard))
+    in_pair = remote(in_all.at[rep], in_all.at[rep], send_pair.at[0], recv_pair.at[0], (core_twin, shard))
+    in_far.start()
+    in_pair.start()
+    for at in range(5):
+        pltpu.make_async_copy(sum_back.at[0], back_all.at[rep, at], recv_back.at[at]).wait()
+    back_far = remote(back_all.at[rep], back_all.at[rep], send_far.at[1], recv_far.at[1], (x_twin, shard))
+    back_pair = remote(back_all.at[rep], back_all.at[rep], send_pair.at[1], recv_pair.at[1], (core_twin, shard))
+    back_far.start()
+    back_pair.start()
+    to_x.wait_recv()
+    passed = remote(rows_all.at[x_twin], rows_all.at[x_twin], send_row.at[2], recv_row.at[2], (core_twin, shard))
+    passed.start()
+    in_far.wait_recv()
+    in_passed = remote(in_all.at[x_twin], in_all.at[x_twin], send_pair.at[2], recv_pair.at[2], (core_twin, shard))
+    in_passed.start()
+    back_far.wait_recv()
+    back_passed = remote(back_all.at[x_twin], back_all.at[x_twin], send_pair.at[3], recv_pair.at[3], (core_twin, shard))
+    back_passed.start()
+    for owner, there in moves:
+
+        @pl.when(owner != shard)
+        def _():
+            there.wait_send()
+
+    keep.wait()
+    to_x.wait_send()
+    to_core.wait()
+    in_far.wait_send()
+    back_far.wait_send()
+    for copy in (in_pair, back_pair, passed, in_passed, back_passed):
+        copy.wait()
+
+
+def return_sums(rows, sum_in, sum_back, number):
+    dma = pltpu.SemaphoreType.DMA
+    shape = lambda dims, like: jax.ShapeDtypeStruct(dims, like.dtype)
+    return comm_call(
+        return_kernel,
+        [shape((RG,) + rows.shape, rows), shape((RG,) + sum_in.shape, sum_in), shape((RG,) + sum_back.shape, sum_back)],
+        [dma((3,))] * 2 + [dma((2,))] + [dma((SG - 1,))] * 2 + [dma((5,))] * 2 + [dma((2,))] * 2 + [dma((4,))] * 2,
+        number,
+        (rows, sum_in, sum_back),
+    )
+
+
+GROUP_HEADS = H // SG
+HEAD_COLS = GROUP_HEADS * HD
+UNITS = FF // SG
+OWN_COLS = 3 * HEAD_COLS + UNITS
+VOCAB_BLOCK = 512
+TABLE_BLOCK = 4096
+EMBED_BLOCK = 2048
+EMBED_PART = 512
+TOKEN_CHUNK = 128
+VMEM_LIMIT = 60 << 20
+
+
+def transposed_dot(left, right):
+    return lax.dot_general(left, right, (((1,), (1,)), ((), ())), preferred_element_type=jnp.float32)
+
+
+def first_dot(left, right):
+    return lax.dot_general(left, right, (((0,), (0,)), ((), ())), preferred_element_type=jnp.float32)
+
+
+def plain_dot(left, right):
+    return jnp.dot(left, right, preferred_element_type=jnp.float32)
+
+
+def table_kernel(ids, table, rows, turned, rows_wide):
+    at = pl.program_id(0)
+    block = table[...].astype(jnp.bfloat16).astype(jnp.float32)
+    width = block.shape[1]
+    turned[pl.ds(pl.multiple_of(at * width, width), width), :] = block.T
+
+    @pl.when(at == pl.num_programs(0) - 1)
+    def _():
+        @pl.loop(0, rows.shape[0] // 16)
+        def _(group):
+            for lane in range(16):
+                token = group * 16 + lane
+                rows_wide[pl.ds(token, 1), :] = turned[pl.ds(ids[token], 1), :]
+
+        rows[...] = rows_wide[...].astype(jnp.bfloat16)
+
+
+def embedding_rows(ids, table):
+    feats, vocab = table.shape
+    blocks = pl.cdiv(vocab, TABLE_BLOCK)
+    return pl.pallas_call(
+        table_kernel,
+        grid=(blocks,),
+        in_specs=[
+            pl.BlockSpec(memory_space=pltpu.SMEM),
+            pl.BlockSpec((feats, TABLE_BLOCK), lambda at: (0, at)),
+        ],
+        out_specs=pl.BlockSpec((ids.shape[0], feats), lambda at: (0, 0)),
+        out_shape=jax.ShapeDtypeStruct((ids.shape[0], feats), jnp.bfloat16),
+        scratch_shapes=[
+            pltpu.VMEM((blocks * TABLE_BLOCK, feats), jnp.float32),
+            pltpu.VMEM((ids.shape[0], feats), jnp.float32),
+        ],
+        compiler_params=pltpu.CompilerParams(vmem_limit_bytes=VMEM_LIMIT),
+    )(ids, table)
+
+
+def vocab_rows(vocab, block):
+    at = pl.program_id(0)
+    places = at * VOCAB_BLOCK + lax.broadcasted_iota(jnp.int32, block.shape, 0)
+    return places, jnp.where(places < vocab, block, jnp.zeros_like(block))
+
+
+def top_kernel(vocab, rows, targets, head, stats, head_out, top, total, target):
+    at = pl.program_id(0)
+
+    @pl.when(at == 0)
+    def _():
+        top[...] = jnp.full_like(top, -1e30)
+        total[...] = jnp.zeros_like(total)
+        target[...] = jnp.zeros_like(target)
+
+    low = head[...].astype(jnp.bfloat16)
+    head_out[...] = low
+    logits = transposed_dot(low, rows[...])
+    places = at * VOCAB_BLOCK + lax.broadcasted_iota(jnp.int32, logits.shape, 0)
+    valid = places < vocab
+    masked = jnp.where(valid, logits, -1e30)
+    highest = jnp.maximum(top[...], jnp.max(masked, axis=0, keepdims=True))
+    weights = jnp.where(valid, jnp.exp(masked - highest), 0.0)
+    total[...] = total[...] * jnp.exp(top[...] - highest) + jnp.sum(weights, axis=0, keepdims=True)
+    top[...] = highest
+    hits = (places == targets[...]) & valid
+    target[...] += jnp.sum(jnp.where(hits, logits, 0.0), axis=0, keepdims=True)
+
+    @pl.when(at == pl.num_programs(0) - 1)
+    def _():
+        stats[...] = jnp.zeros_like(stats)
+        stats[0:1, :] = top[...]
+        stats[1:2, :] = total[...]
+        stats[2:3, :] = target[...]
+
+
+def logit_stats(rows, targets, head):
+    vocab, depth = head.shape
+    count = rows.shape[0]
+    line = pltpu.VMEM((1, count), jnp.float32)
+    return pl.pallas_call(
+        functools.partial(top_kernel, vocab),
+        grid=(pl.cdiv(vocab, VOCAB_BLOCK),),
+        in_specs=[
+            pl.BlockSpec((count, depth), lambda at: (0, 0)),
+            pl.BlockSpec((1, count), lambda at: (0, 0)),
+            pl.BlockSpec((VOCAB_BLOCK, depth), lambda at: (at, 0)),
+        ],
+        out_specs=[
+            pl.BlockSpec((8, count), lambda at: (0, 0)),
+            pl.BlockSpec((VOCAB_BLOCK, depth), lambda at: (at, 0)),
+        ],
+        out_shape=[
+            jax.ShapeDtypeStruct((8, count), jnp.float32),
+            jax.ShapeDtypeStruct(head.shape, jnp.bfloat16),
+        ],
+        scratch_shapes=[line, line, line],
+        compiler_params=pltpu.CompilerParams(vmem_limit_bytes=VMEM_LIMIT),
+    )(rows, targets, head)
+
+
+def logit_grads(vocab, low, rows, logsum, targets, counted):
+    logits = transposed_dot(low, rows)
+    places = pl.program_id(0) * VOCAB_BLOCK + lax.broadcasted_iota(jnp.int32, logits.shape, 0)
+    hits = (places == targets).astype(jnp.float32)
+    grads = (jnp.exp(logits - logsum) - hits) * counted
+    return jnp.where(places < vocab, grads, 0.0).astype(jnp.bfloat16)
+
+
+def rows_kernel(vocab, rows, facts, targets, head, out):
+    @pl.when(pl.program_id(0) == 0)
+    def _():
+        out[...] = jnp.zeros_like(out)
+
+    _, low = vocab_rows(vocab, head[...])
+    grads = logit_grads(vocab, low, rows[...], facts[0:1, :], targets[...], facts[1:2, :])
+    out[...] += first_dot(grads, low)
+
+
+def picked_grads(rows, facts, targets, head):
+    vocab, depth = head.shape
+    count = rows.shape[0]
+    return pl.pallas_call(
+        functools.partial(rows_kernel, vocab),
+        grid=(pl.cdiv(vocab, VOCAB_BLOCK),),
+        in_specs=[
+            pl.BlockSpec((count, depth), lambda at: (0, 0)),
+            pl.BlockSpec((8, count), lambda at: (0, 0)),
+            pl.BlockSpec((1, count), lambda at: (0, 0)),
+            pl.BlockSpec((VOCAB_BLOCK, depth), lambda at: (at, 0)),
+        ],
+        out_specs=pl.BlockSpec((count, depth), lambda at: (0, 0)),
+        out_shape=jax.ShapeDtypeStruct((count, depth), jnp.float32),
+        compiler_params=pltpu.CompilerParams(vmem_limit_bytes=VMEM_LIMIT),
+    )(rows, facts, targets, head)
+
+
+def head_kernel(vocab, rows, facts, targets, head, out, squares):
+    @pl.when(pl.program_id(0) == 0)
+    def _():
+        squares[...] = jnp.zeros_like(squares)
+
+    _, low = vocab_rows(vocab, head[...])
+    groups = rows.shape[0]
+    total = None
+    for group in range(groups):
+        grads = logit_grads(
+            vocab, low, rows[group], facts[group, 0:1, :], targets[group, 0:1, :], facts[group, 1:2, :]
+        )
+        term = plain_dot(grads, rows[group])
+        total = term if total is None else total + term
+    out[...] = total
+    squares[0:1, :] += jnp.sum(total * total, axis=0, keepdims=True)
+
+
+def head_grads(rows, facts, targets, head):
+    vocab, depth = head.shape
+    groups, count, _ = rows.shape
+    return pl.pallas_call(
+        functools.partial(head_kernel, vocab),
+        grid=(pl.cdiv(vocab, VOCAB_BLOCK),),
+        in_specs=[
+            pl.BlockSpec((groups, count, depth), lambda at: (0, 0, 0)),
+            pl.BlockSpec((groups, 8, count), lambda at: (0, 0, 0)),
+            pl.BlockSpec((groups, 8, count), lambda at: (0, 0, 0)),
+            pl.BlockSpec((VOCAB_BLOCK, depth), lambda at: (at, 0)),
+        ],
+        out_specs=[
+            pl.BlockSpec((VOCAB_BLOCK, depth), lambda at: (at, 0)),
+            pl.BlockSpec((8, depth), lambda at: (0, 0)),
+        ],
+        out_shape=[
+            jax.ShapeDtypeStruct(head.shape, jnp.float32),
+            jax.ShapeDtypeStruct((8, depth), jnp.float32),
+        ],
+        compiler_params=pltpu.CompilerParams(vmem_limit_bytes=VMEM_LIMIT),
+    )(rows, facts, targets, head)
+
+
+def embed_grad_kernel(starts, ids, rows, out, squares):
+    at = pl.program_id(0)
+    parts = EMBED_BLOCK // EMBED_PART
+
+    @pl.when(at == 0)
+    def _():
+        squares[...] = jnp.zeros_like(squares)
+
+    for part in range(parts):
+        begin = starts[at * parts + part]
+        end = starts[at * parts + part + 1]
+        base = at * EMBED_BLOCK + part * EMBED_PART
+        places = base + lax.broadcasted_iota(jnp.int32, (TOKEN_CHUNK, EMBED_PART), 1)
+
+        def add(chunk, total):
+            here = pl.ds(pl.multiple_of(chunk * TOKEN_CHUNK, TOKEN_CHUNK), TOKEN_CHUNK)
+            hits = (ids[here, :] == places).astype(jnp.bfloat16)
+            return total + first_dot(rows[here, :], hits)
+
+        total = lax.fori_loop(
+            begin // TOKEN_CHUNK,
+            (end + TOKEN_CHUNK - 1) // TOKEN_CHUNK,
+            add,
+            jnp.zeros((rows.shape[1], EMBED_PART), jnp.float32),
+        )
+        out[:, part * EMBED_PART : (part + 1) * EMBED_PART] = total
+        squares[...] += total * total
+
+
+def embed_grads(starts, ids, rows, vocab):
+    count, feats = rows.shape
+    return pl.pallas_call(
+        embed_grad_kernel,
+        grid=(pl.cdiv(vocab, EMBED_BLOCK),),
+        in_specs=[
+            pl.BlockSpec(memory_space=pltpu.SMEM),
+            pl.BlockSpec((count, 1), lambda at: (0, 0)),
+            pl.BlockSpec((count, feats), lambda at: (0, 0)),
+        ],
+        out_specs=[
+            pl.BlockSpec((feats, EMBED_BLOCK), lambda at: (0, at)),
+            pl.BlockSpec((feats, EMBED_PART), lambda at: (0, 0)),
+        ],
+        out_shape=[
+            jax.ShapeDtypeStruct((feats, vocab), jnp.float32),
+            jax.ShapeDtypeStruct((feats, EMBED_PART), jnp.float32),
+        ],
+        compiler_params=pltpu.CompilerParams(vmem_limit_bytes=VMEM_LIMIT),
+    )(starts, ids, rows)
+
+
+def turn_tables(places):
+    half_rot = ROT // 2
+    lane = jnp.arange(HEAD_COLS) % HD
+    exponent = (lane % half_rot).astype(jnp.float32) * (2.0 / ROT)
+    angles = places[:, None] * jnp.exp(-exponent * jnp.log(10000.0))[None, :]
+    cosine, sine = jnp.cos(angles), jnp.sin(angles)
+    lane = lane[None, :]
+    return (
+        jnp.where(lane < ROT, cosine, 1.0),
+        jnp.where(lane < half_rot, -sine, 0.0),
+        jnp.where((lane >= half_rot) & (lane < ROT), sine, 0.0),
+    )
+
+
+def turn(rows, tables, sign):
+    half_rot = ROT // 2
+    own, after, before = tables
+    return (
+        rows * own
+        + sign * jnp.roll(rows, -half_rot, axis=-1) * after
+        + sign * jnp.roll(rows, half_rot, axis=-1) * before
+    )
+
+
+def centred_rows(values):
+    centred = values - jnp.mean(values, axis=-1, keepdims=True)
+    spread = jnp.mean(centred * centred, axis=-1, keepdims=True)
+    scale = lax.rsqrt(spread + NORM_EPS)
+    return centred * scale, scale
+
+
+def group_plan(
+    token_ids,
+    pic_start,
+    comp_pos,
+    comp_tgt,
+    proj_in,
+    proj_back,
+    small_params,
+    head_table,
+    embed_table,
+    first_in,
+    second_in,
+    first_back,
+    second_back,
+    first_small,
+    second_small,
+    first_head,
+    second_head,
+    first_embed,
+    second_embed,
+):
+    bf16 = jnp.bfloat16
+    rep_at = lax.axis_index("rep")
+    shard_at = lax.axis_index("shard")
+    micro, _, seq_dev = token_ids.shape
+    slots = comp_pos.shape[2]
+    seq_len = seq_dev * RG
+    lines = micro * SG // RG
+    blocks = lines * RG
+    own_blocks = blocks // SG
+    tokens = lines * seq_len
+    slot_count = blocks * slots
+    own_slots = own_blocks * slots
+    vocab_dev = head_table.shape[1]
+    vocab = embed_table.shape[1]
+    quarter = D // SG // RG
+
+    place_line = jnp.concatenate([comp_pos[:, 0, :].reshape(-1), comp_tgt[:, 0, :].reshape(-1)])
+    span_line = jnp.concatenate([pic_start[:, 0], jnp.zeros((seq_dev - micro,), jnp.int32)])
+    ints = jnp.concatenate(
+        [token_ids[:, 0, :], place_line[None], span_line[None], jnp.zeros((4, seq_dev), jnp.int32)]
+    )
+    small_low = small_params.astype(bf16).astype(jnp.float32).reshape(-1, 128)
+    small_rows = small_low.shape[0]
+    smalls = jnp.pad(small_low, ((0, 16 - small_rows), (0, 0)))
+    ints_all, smalls_all = share_facts(ints, smalls, 1)
+    wide_small = smalls_all[:, :small_rows].reshape(-1)
+    (
+        gain_one,
+        shift_one,
+        gain_two,
+        shift_two,
+        gain_last,
+        shift_last,
+        bias_qkv,
+        bias_hidden,
+        bias_out,
+    ) = split_small(wide_small)
+    head_cols = [
+        lax.dynamic_slice(bias_qkv, (part * D + shard_at * HEAD_COLS,), (HEAD_COLS,)) for part in range(3)
+    ]
+    own_hidden = lax.dynamic_slice(bias_hidden, (shard_at * UNITS,), (UNITS,))
+
+    by_group = ints_all.reshape(RG, RG, SG // RG, 8, seq_dev)
+    ids_all = jnp.transpose(by_group[:, :, :, :micro], (1, 3, 2, 0, 4)).reshape(RG, tokens)
+    slot_facts = jnp.transpose(
+        by_group[:, :, :, 2].reshape(RG, RG, SG // RG, 2, micro, slots), (3, 1, 4, 2, 0, 5)
+    ).reshape(2, RG, slot_count)
+    used_all = slot_facts[0] < seq_dev
+    targets_all = jnp.where(used_all, slot_facts[1] - shard_at * vocab_dev, -1)
+    counted_all = used_all.astype(jnp.float32)
+    ids_group = lax.dynamic_index_in_dim(ids_all, rep_at, 0, False)
+    pos_group = lax.dynamic_index_in_dim(slot_facts[0], rep_at, 0, False)
+    targets_group = lax.dynamic_index_in_dim(targets_all, rep_at, 0, False)
+    counted_group = lax.dynamic_index_in_dim(counted_all, rep_at, 0, False)
+    spans = lax.dynamic_index_in_dim(by_group[0, :, :, 3, :micro], rep_at, 0, False).T.reshape(lines)
+
+    flat_ids = ids_all.reshape(-1)
+    sorted_ids, order = lax.sort((flat_ids, jnp.arange(flat_ids.shape[0], dtype=jnp.int32)), num_keys=1)
+    edges = jnp.arange(pl.cdiv(vocab, EMBED_BLOCK) * (EMBED_BLOCK // EMBED_PART) + 1) * EMBED_PART
+    starts = jnp.sum((flat_ids[None, :] < edges[:, None]).astype(jnp.int32), axis=1)
+
+    rows = embedding_rows(ids_group, embed_table)
+    in_low = proj_in.astype(bf16)
+    qkv_parts = in_low[:, : 3 * D].reshape(D // SG, 3, SG, HEAD_COLS)
+    in_parts = jnp.concatenate(
+        [
+            jnp.transpose(qkv_parts, (2, 0, 1, 3)).reshape(SG, D // SG, 3 * HEAD_COLS),
+            jnp.transpose(in_low[:, 3 * D :].reshape(D // SG, SG, UNITS), (1, 0, 2)),
+        ],
+        axis=2,
+    ).reshape(SG, 2, D // SG // 2, OWN_COLS)
+    back_tiles = proj_back.astype(bf16).reshape(5, 2, 64, D)
+    residual_low, in_all, back_all = share_embedding(rows, in_parts, back_tiles, 2)
+    own_in = in_all.reshape(D, OWN_COLS)
+    own_back = back_all.reshape(5 * 128, D)
+
+    residual = residual_low.astype(jnp.float32)
+    unit_rows, unit_scale = centred_rows(residual)
+    low_one = (unit_rows * gain_one + shift_one).astype(bf16)
+    low_two = (unit_rows * gain_two + shift_two).astype(bf16)
+    pick = (pos_group.reshape(blocks, slots, 1) == jnp.arange(seq_dev)[None, None, :]).astype(bf16)
+
+    def pick_rows(values):
+        blocked = values.reshape(blocks, seq_dev, values.shape[1])
+        return jnp.einsum("bst,btd->bsd", pick, blocked, preferred_element_type=jnp.float32).reshape(
+            slot_count, values.shape[1]
+        )
+
+    def put_rows(values):
+        blocked = values.reshape(blocks, slots, values.shape[1])
+        return jnp.einsum("bst,bsd->btd", pick, blocked, preferred_element_type=jnp.float32).reshape(
+            tokens, values.shape[1]
+        )
+
+    picked_one = pick_rows(low_one).astype(bf16)
+    picked_two = pick_rows(low_two).astype(bf16)
+    slot_places = (
+        (jnp.arange(blocks) % RG * seq_dev)[:, None] + jnp.minimum(pos_group.reshape(blocks, slots), seq_dev - 1)
+    ).reshape(-1)
+    key_places = jnp.arange(seq_len)
+    query_turn = turn_tables(slot_places.astype(jnp.float32))
+    key_turn = turn_tables(key_places.astype(jnp.float32))
+    key_turn = tuple(jnp.tile(table, (lines, 1)) for table in key_turn)
+    queries = turn(plain_dot(picked_one, own_in[:, :HEAD_COLS]) + head_cols[0], query_turn, 1.0).astype(bf16)
+    key_values = plain_dot(low_one, own_in[:, HEAD_COLS : 3 * HEAD_COLS])
+    keys = turn(key_values[:, :HEAD_COLS] + head_cols[1], key_turn, 1.0).astype(bf16)
+    values = (key_values[:, HEAD_COLS:] + head_cols[2]).astype(bf16)
+    line_slots = slot_count // lines
+    queries = queries.reshape(lines, line_slots, GROUP_HEADS, HD)
+    keys = keys.reshape(lines, seq_len, GROUP_HEADS, HD)
+    values = values.reshape(lines, seq_len, GROUP_HEADS, HD)
+    query_at = slot_places.reshape(lines, line_slots, 1)
+    key_at = key_places[None, None, :]
+    span_at = spans.reshape(lines, 1, 1)
+    in_query = (query_at >= span_at) & (query_at < span_at + PIC)
+    in_key = (key_at >= span_at) & (key_at < span_at + PIC)
+    allowed = ((key_at <= query_at) | (in_query & in_key))[:, None]
+    scores = jnp.einsum("nqhd,nkhd->nhqk", queries, keys, preferred_element_type=jnp.float32) * HD ** (-0.5)
+    scores = jnp.where(allowed, scores, -1e30)
+    highest = jnp.max(scores, axis=-1, keepdims=True)
+    exponent = jnp.exp(scores - highest)
+    probs = exponent / jnp.sum(exponent, axis=-1, keepdims=True)
+    low_probs = probs.astype(bf16)
+    attended = (
+        jnp.einsum("nhqk,nkhd->nqhd", low_probs, values, preferred_element_type=jnp.float32)
+        .reshape(slot_count, HEAD_COLS)
+        .astype(bf16)
+    )
+    hidden_pre = plain_dot(picked_two, own_in[:, 3 * HEAD_COLS :]) + own_hidden
+    activation = gelu_exact(hidden_pre).astype(bf16)
+    joined = jnp.concatenate([attended, activation], axis=1)
+    branch_parts = plain_dot(joined, own_back).reshape(SG, own_slots, D)
+    branch = shard_sum(branch_parts, 3)
+
+    own_pick = lax.dynamic_slice_in_dim(pick, shard_at * own_blocks, own_blocks, 0)
+    own_residual = lax.dynamic_slice_in_dim(residual_low, shard_at * own_blocks * seq_dev, own_blocks * seq_dev, 0)
+    own_residual = jnp.einsum(
+        "bst,btd->bsd", own_pick, own_residual.reshape(own_blocks, seq_dev, D), preferred_element_type=jnp.float32
+    ).reshape(own_slots, D)
+    own_used = lax.dynamic_slice_in_dim(counted_group, shard_at * own_slots, own_slots, 0)
+    after_add = own_residual + branch + bias_out
+    final_rows, pull_last = jax.vjp(norm_rows, after_add, gain_last, shift_last)
+    picked = (final_rows * own_used[:, None]).astype(bf16)
+    rows_group = shard_gather(picked, 4)
+
+    head_turned = head_table.T
+    stats, head_low = logit_stats(rows_group, targets_group[None], head_turned)
+    stats_all = shard_stats(stats, 5)
+    tops = stats_all[:, 0]
+    top = jnp.max(tops, axis=0)
+    logsum = top + jnp.log(jnp.sum(stats_all[:, 1] * jnp.exp(tops - top), axis=0))
+    row_target = jnp.sum(stats_all[:, 2], axis=0)
+    facts = jnp.concatenate(
+        [logsum[None], counted_group[None], row_target[None], jnp.zeros((5, slot_count), jnp.float32)]
+    )
+    picked_parts = picked_grads(rows_group, facts, targets_group[None], head_low)
+    d_picked, rows_all, facts_all = sum_and_share(
+        picked_parts.reshape(SG, own_slots, D), rows_group, facts, 6
+    )
+    loss_sum = jnp.sum((facts_all[:, 0] - facts_all[:, 2]) * facts_all[:, 1])
+    count_sum = jnp.sum(facts_all[:, 1])
+    targets_wide = jnp.broadcast_to(targets_all[:, None, :], (RG, 8, slot_count))
+    grad_head, head_squares = head_grads(rows_all, facts_all, targets_wide, head_low)
+
+    d_after, d_gain_last, d_shift_last = pull_last(d_picked)
+    d_branch_own = d_after.astype(bf16)
+    d_bias_out = jnp.sum(d_branch_own.astype(jnp.float32), axis=0)
+    pieces = jnp.transpose(d_after.reshape(own_slots, SG, D // SG), (1, 0, 2))
+    d_branch, after_pieces = share_branch(d_branch_own, pieces, 7)
+    d_after_feats = after_pieces.reshape(slot_count, D // SG)
+
+    d_joined = transposed_dot(d_branch, own_back)
+    grad_back = first_dot(joined, d_branch)
+    d_attended = d_joined[:, :HEAD_COLS].astype(bf16).reshape(lines, line_slots, GROUP_HEADS, HD)
+    _, pull_gelu = jax.vjp(gelu_exact, hidden_pre)
+    d_hidden = pull_gelu(d_joined[:, HEAD_COLS:])[0].astype(bf16)
+    d_probs = jnp.einsum("nqhd,nkhd->nhqk", d_attended, values, preferred_element_type=jnp.float32)
+    d_scores = (probs * (d_probs - jnp.sum(probs * d_probs, axis=-1, keepdims=True))).astype(bf16)
+    d_queries = jnp.einsum("nhqk,nkhd->nqhd", d_scores, keys, preferred_element_type=jnp.float32) * HD ** (-0.5)
+    d_keys = jnp.einsum("nhqk,nqhd->nkhd", d_scores, queries, preferred_element_type=jnp.float32) * HD ** (-0.5)
+    d_values = jnp.einsum("nhqk,nqhd->nkhd", low_probs, d_attended, preferred_element_type=jnp.float32)
+    d_query_rows = turn(d_queries.reshape(slot_count, HEAD_COLS), query_turn, -1.0).astype(bf16)
+    d_key_rows = turn(d_keys.reshape(tokens, HEAD_COLS), key_turn, -1.0).astype(bf16)
+    d_key_values = jnp.concatenate([d_key_rows, d_values.reshape(tokens, HEAD_COLS).astype(bf16)], axis=1)
+    grad_in = jnp.concatenate(
+        [first_dot(picked_one, d_query_rows), first_dot(low_one, d_key_values), first_dot(picked_two, d_hidden)],
+        axis=1,
+    )
+    d_projected = jnp.concatenate([put_rows(d_query_rows).astype(bf16), d_key_values], axis=1)
+    d_hidden_rows = put_rows(d_hidden).astype(bf16)
+    d_normed_one = transposed_dot(d_projected, own_in[:, : 3 * HEAD_COLS])
+    d_normed_two = transposed_dot(d_hidden_rows, own_in[:, 3 * HEAD_COLS :])
+    d_unit = d_normed_one * gain_one + d_normed_two * gain_two
+    norm_stats = jnp.stack([jnp.sum(d_unit, axis=1), jnp.sum(d_unit * unit_rows, axis=1)])
+    norm_stats = jnp.pad(norm_stats, ((0, 6), (0, 0)))
+    unit_parts = jnp.transpose(d_unit.reshape(tokens, SG, D // SG), (1, 0, 2))
+
+    def whole(columns, length):
+        start = shard_at * columns.shape[0]
+        return lax.dynamic_update_slice(jnp.zeros((length,), jnp.float32), columns, (start,))
+
+    d_bias_parts = [
+        jnp.sum(d_query_rows.astype(jnp.float32), axis=0),
+        jnp.sum(d_key_rows.astype(jnp.float32), axis=0),
+        jnp.sum(d_key_values[:, HEAD_COLS:].astype(jnp.float32), axis=0),
+    ]
+    grad_small = jnp.concatenate(
+        [
+            jnp.sum(d_normed_one * unit_rows, axis=0),
+            jnp.sum(d_normed_one, axis=0),
+            jnp.sum(d_normed_two * unit_rows, axis=0),
+            jnp.sum(d_normed_two, axis=0),
+            d_gain_last,
+            d_shift_last,
+            *[whole(part, D) for part in d_bias_parts],
+            whole(jnp.sum(d_hidden.astype(jnp.float32), axis=0), FF),
+            d_bias_out,
+        ]
+    )
+    grad_small = jnp.pad(grad_small.reshape(SG, small_rows, 128), ((0, 0), (0, 16 - small_rows), (0, 0)))
+    in_quarters = jnp.transpose(grad_in.reshape(SG, RG, quarter, OWN_COLS), (1, 0, 2, 3))
+    back_quarters = jnp.transpose(grad_back.reshape(5, RG, 32, D), (1, 0, 2, 3))
+    d_unit_feats, norm_stats_all, in_sum, back_sum, small_sum = layer_sums(
+        unit_parts, norm_stats, in_quarters, back_quarters, grad_small, 8
+    )
+
+    norm_sums = jnp.sum(norm_stats_all, axis=0)
+    own_unit = lax.dynamic_slice_in_dim(residual_low, shard_at * (D // SG), D // SG, 1).astype(jnp.float32)
+    row_mean = jnp.mean(residual, axis=-1, keepdims=True)
+    own_unit = (own_unit - row_mean) * unit_scale
+    d_rows = (
+        d_unit_feats - norm_sums[0][:, None] / D - own_unit * (norm_sums[1][:, None] / D)
+    ) * unit_scale
+    d_after_rows = jnp.einsum(
+        "bst,bsd->btd",
+        pick.astype(jnp.float32),
+        d_after_feats.reshape(blocks, slots, D // SG),
+        precision=lax.Precision.HIGHEST,
+    ).reshape(tokens, D // SG)
+    d_rows = (d_after_rows + d_rows).astype(bf16)
+    d_rows_all, in_grads, back_grads = return_sums(d_rows, in_sum, back_sum, 9)
+    d_sorted = jnp.take(d_rows_all.reshape(RG * tokens, D // SG), order, axis=0)
+    grad_embed, embed_squares = embed_grads(starts, sorted_ids[:, None], d_sorted, vocab)
+
+    in_grads = jnp.transpose(in_grads, (0, 2, 1, 3)).reshape(D // SG, SG, OWN_COLS)
+    qkv_grads = jnp.transpose(
+        in_grads[:, :, : 3 * HEAD_COLS].reshape(D // SG, SG, 3, HEAD_COLS), (0, 2, 1, 3)
+    ).reshape(D // SG, 3 * D)
+    grad_in = jnp.concatenate([qkv_grads, in_grads[:, :, 3 * HEAD_COLS :].reshape(D // SG, FF)], axis=1)
+    grad_back = jnp.transpose(back_grads, (1, 0, 2, 3)).reshape(proj_back.shape)
+    grad_small = small_sum[:small_rows].reshape(-1)
+
+    local_square = (
+        jnp.sum(grad_in * grad_in)
+        + jnp.sum(grad_back * grad_back)
+        + jnp.sum(grad_small * grad_small)
+        + jnp.sum(head_squares)
+        + jnp.sum(embed_squares)
+    )
+    squares_all = shard_stats(jnp.broadcast_to(local_square, (8, 128)), 10)
+    norm_value = jnp.sqrt(jnp.sum(squares_all[:, 0, 0]))
+    factor = CLIP_LEVEL / jnp.maximum(norm_value, CLIP_LEVEL)
+    next_in, moment_in, square_in = adamw(proj_in, grad_in * factor, first_in, second_in, RATE_IN)
+    next_back, moment_back, square_back = adamw(
+        proj_back, grad_back * factor, first_back, second_back, RATE_BACK
+    )
+    next_small, moment_small, square_small = adamw(
+        small_params, grad_small * factor, first_small, second_small, RATE_SMALL
+    )
+    next_head, moment_head, square_head = adamw(
+        head_table, grad_head.T * factor, first_head, second_head, RATE_HEAD
+    )
+    next_embed, moment_embed, square_embed = adamw(
+        embed_table, grad_embed * factor, first_embed, second_embed, RATE_EMBED
+    )
+    return (
+        jnp.stack([loss_sum, count_sum]),
+        norm_value.reshape(1),
+        next_in,
+        moment_in,
+        square_in,
+        next_back,
+        moment_back,
+        square_back,
+        next_small,
+        moment_small,
+        square_small,
+        next_head,
+        moment_head,
+        square_head,
+        next_embed,
+        moment_embed,
+        square_embed,
+    )
+
+
+def select_plan(mesh):
+    if mesh.shape["rep"] == RG and mesh.shape["shard"] == SG:
+        return group_plan
+    return any_mesh
+
+
 def solution(mesh):
     placed = (
         P(None, "shard", "rep"),
@@ -404,7 +1613,7 @@
         P("shard", None),
     )
     return jax.shard_map(
-        on_device,
+        select_plan(mesh),
         mesh=mesh,
         in_specs=placed,
         out_specs=(

time: 2990 us -> 1070 us (0.36)
  waiting for transfers between devices: 1820 us -> 0 us
  Pallas kernels: 0 us -> 622 us
  blocking collectives: 326 us -> 0 us
  matrix products: 223 us -> 56.6 us
  other arithmetic: 346 us -> 227 us
  local copies, waits for them, and re-layouts: 216 us -> 149 us
    psum x1 -> x0, waiting for transfers between devices: 854 us -> none  [on_device(): lax.psum((shard_in, shard_back, shard_small, grad_head, grad_embed, loss_...]
    reduce_scatter x6 -> x0, waiting for transfers between devices: 783 us -> none  [the longest x1 467 us: on_device(): lax.psum_scatter(grad_in, 'shard', scatter_dimension=0, tiled=True)]
    pallas_call x0 -> x15, Pallas kernels: none -> 622 us  [the longest x10 440 us: comm_call(): pl.pallas_call(kernel, out_shape=out_shape, in_specs=[pick[space] for spa...]
    all_gather x11 -> x0, blocking collectives: 259 us -> none  [the longest x6 106 us: combined_all(): gathered = jax.tree.map(lambda a: lax.all_gather(a, axis), part)]
    all_gather x6 -> x0, waiting for transfers between devices: 170 us -> none  [the longest x1 76.3 us: on_device(): lax.all_gather(in_low, 'shard', axis=0, tiled=True)]
    dot_general x36 -> x22, matrix products: 223 us -> 53.4 us  [the longest x3 16.5 us: transposed_dot(): lax.dot_general(left, right, (((1,), (1,)), ((), ())), preferred_element_...]
    unnamed x283 -> x200, local copies, waits for them, and re-layouts: 175 us -> 28 us
    scatter-add x4 -> x0, other arithmetic: 42.8 us -> none  [the longest x2 40.2 us: on_device(): grad_embed.at[:, ids_group[micro_at]].add(returned.astype(jnp.float32))]
  transfers between devices with their start and end apart: 17 -> 0, of which waited for: 11 -> 0; matrix products, arithmetic and copies ran while one was open for 15% -> 0% of each run, Pallas kernels for 0% -> 0%
where the time goes in v1:
time: 1070 us; the launch traced here: 1060 us
  Pallas kernels  622 us (58%)
  other arithmetic  227 us (21%)
  local copies, waits for them, and re-layouts  149 us (14%)
  matrix products  56.6 us (5%)
    pallas_call x10, Pallas kernels, comm_call(): pl.pallas_call(kernel, out_shape=out_shape, in_specs=[pick[space] for spa...  440 us
    sub x5, other arithmetic, adamw(): weight - rate_value * (moment_hat / (jnp.sqrt(square_hat) + ADAM_EPS) + D...  137 us
    pallas_call x1, Pallas kernels, head_grads(): pl.pallas_call(functools.partial(head_kernel, vocab), grid=(pl.cdiv(vocab...  65.9 us
    pallas_call x1, Pallas kernels, embed_grads(): pl.pallas_call(embed_grad_kernel, grid=(pl.cdiv(vocab, EMBED_BLOCK),), in...  53.6 us
    gather x1, local copies, waits for them, and re-layouts, group_plan(): d_sorted = jnp.take(d_rows_all.reshape(RG * tokens, D // SG), order, axis=0)  29.5 us
    unnamed x200, local copies, waits for them, and re-layouts  28 us
    pallas_call x1, Pallas kernels, picked_grads(): pl.pallas_call(functools.partial(rows_kernel, vocab), grid=(pl.cdiv(vocab...  23.3 us
    pallas_call x1, Pallas kernels, logit_stats(): pl.pallas_call(functools.partial(top_kernel, vocab), grid=(pl.cdiv(vocab,...  22.3 us

profile of v1, /device:TPU:0, one launch (start us, length us, event | category | flops | bytes accessed | tf_op | source)
XLA Modules:
  0.0 1061.2 jit_solution(11776286313309164628)
XLA Ops:
  7.5 13.5 %shard_map.314 = (s32[4,8,8,128]{3,2,1,0:T(8,128)}, f32[8,16,128]{2,1,0:T(8,128)}) custom-call(s32[8,128]{1,0:T(8,128)} %add_add_fusion.1.ints, f32[16,128]{1,0:T(8,128)} %pad_convert_fusion.smalls), custom_call_target="tpu_custom_call" | custom-call | tf_op jit(solution)/shard_map/pallas_call | solution.py:434
  22.6 17.1 %shard_map.315.rows = bf16[2048,128]{1,0:T(8,128)(2,1)} custom-call(s32[2048]{0:T(1024)} %bitcast.301, f32[128,50304]{1,0:T(8,128)} %table.1), custom_call_target="tpu_custom_call" | custom-call | tf_op jit(solution)/shard_map/pallas_call | solution.py:1032
  46.1 82.8 %shard_map.316 = (bf16[2048,1024]{1,0:T(8,128)(2,1)}, bf16[8,2,64,896]{3,2,1,0:T(8,128)(2,1)}, bf16[5,2,64,1024]{3,2,1,0:T(8,128)(2,1)}) custom-call(bf16[2048,128]{1,0:T(8,128)(2,1)} %shard_map.315.rows, bf16[8,2,64,896]{3,2,1,0:T(8,128)(2,1)} %pad_maximum_fusion.1.in_parts, bf16[5,2,64,1024]{3,2,1,0:T(8,128)(2,1)} %bitcast.256), custom_call_target="tpu_custom_call" | custom-call | tf_op jit(solution)/shard_map/pallas_call | solution.py:434
  128.9 3.0 convert_reduce_fusion
  134.4 6.1 fusion.12
  142.5 2.9 convolution_convert_fusion.2
  162.8 3.3 fusion.205
  170.0 2.9 convolution_convert_fusion.1
  173.0 5.5 multiply_convert_fusion.1
  179.6 48.2 %shard_map.317 = f32[64,1024]{1,0:T(8,128)S(1)} custom-call(f32[8,64,1024]{2,1,0:T(8,128)S(1)} %fusion.212.parts), custom_call_target="tpu_custom_call" | custom-call | tf_op jit(solution)/shard_map/pallas_call | solution.py:434
  231.1 22.3 %shard_map.318.rows = bf16[512,1024]{1,0:T(8,128)(2,1)} custom-call(bf16[64,1024]{1,0:T(8,128)(2,1)} %multiply_convert_fusion.2.rows), custom_call_target="tpu_custom_call" | custom-call | tf_op jit(solution)/shard_map/pallas_call | solution.py:434
  254.0 22.3 %shard_map.319 = (f32[8,512]{1,0:T(8,128)}, bf16[6288,1024]{1,0:T(8,128)(2,1)}) custom-call(bf16[512,1024]{1,0:T(8,128)(2,1)} %shard_map.318.rows, s32[1,512]{1,0:T(1,128)} %constant_dynamic-slice_fusion.1.targets, f32[6288,1024]{1,0:T(8,128)} %bitcast.231), custom_call_target="tpu_custom_call" | custom-call | tf_op jit(solution)/shard_map/pallas_call | solution.py:1089
  276.3 9.5 shard_map.320
  287.8 23.3 %shard_map.321 = f32[512,1024]{1,0:T(8,128)} custom-call(bf16[512,1024]{1,0:T(8,128)(2,1)} %shard_map.318.rows, f32[8,512]{1,0:T(8,128)} %maximum_maximum_fusion.facts, s32[1,512]{1,0:T(1,128)} %constant_dynamic-slice_fusion.1.targets, bf16[6288,1024]{1,0:T(8,128)(2,1)} %get-tuple-element.49.head), custom_call_target="tpu_custom_call" | custom-call | tf_op jit(solution)/shard_map/pallas_call | solution.py:1131
  312.7 34.2 %shard_map.322 = (f32[64,1024]{1,0:T(8,128)S(1)}, bf16[4,512,1024]{2,1,0:T(8,128)(2,1)S(1)}, f32[4,8,512]{2,1,0:T(8,128)S(1)}) custom-call(f32[8,64,1024]{2,1,0:T(8,128)S(1)} %bitcast.229, bf16[512,1024]{1,0:T(8,128)(2,1)S(1)} %copy-done, f32[8,512]{1,0:T(8,128)S(1)} %copy-done.3), custom_call_target="tpu_custom_call" | custom-call | tf_op jit(solution)/shard_map/pallas_call | solution.py:434
  350.2 65.9 %shard_map.326 = (f32[6288,1024]{1,0:T(8,128)}, f32[8,1024]{1,0:T(8,128)}) custom-call(bf16[4,512,1024]{2,1,0:T(8,128)(2,1)} %copy-done.2, f32[4,8,512]{2,1,0:T(8,128)} %copy-done.4, s32[4,8,512]{2,1,0:T(8,128)} %broadcast_in_dim.214.targets, bf16[6288,1024]{1,0:T(8,128)(2,1)} %get-tuple-element.49.head), custom_call_target="tpu_custom_call" | custom-call | tf_op jit(solution)/shard_map/pallas_call | solution.py:1167
  420.5 23.4 %shard_map.323 = (bf16[512,1024]{1,0:T(8,128)(2,1)}, f32[8,64,128]{2,1,0:T(8,128)}) custom-call(bf16[64,1024]{1,0:T(8,128)(2,1)} %get-tuple-element.96.rows, f32[8,64,128]{2,1,0:T(8,128)} %bitcast.280), custom_call_target="tpu_custom_call" | custom-call | tf_op jit(solution)/shard_map/pallas_call | solution.py:434
  444.0 2.7 fusion.213
  456.8 3.0 concatenate.110
  459.8 2.9 concatenate.111
  465.1 2.9 convert_reduce_fusion.4
  475.9 2.6 convolution_convert_fusion.4
  478.7 2.7 convert_reduce_fusion.3
  481.9 7.5 fusion.210
  489.4 9.2 copy.181
  498.6 3.0 convert_reduce_fusion.2
  502.8 6.4 fusion.211
  509.2 9.2 copy.182
  518.4 12.0 %fusion.179 = (f32[2048]{0:T(1024)}, f32[2048]{0:T(1024)}, f32[1024]{0:T(1024)S(1)}, f32[1024]{0:T(1024)S(1)}, f32[2048,1024]{1,0:T(8,128)}) fusion(f32[2048]{0:T(1024)} %copy-done.44, f32[2048]{0:T(1024)S(1)} %broadcast_multiply_fusion.1, bf16[2048,1024]{1,0:T(8,128)(2,1)} %get-tuple-element.44, f32[2048,1024]{1,0:T(8,128)} %copy.182, ...), kind=kLoop, calls=%fused_computation.348 | loop fusion | flops 27256832 | bytes 29409280 | tf_op jit(solution)/shard_map/reduce_sum | solution.py:1484
  547.9 3.5 fusion.36
  554.5 5.0 copy.188
  559.5 4.3 copy.295
  567.1 9.1 copy.183
  576.2 9.1 copy.184
  585.3 133.1 %shard_map.324 = (f32[2048,128]{1,0:T(8,128)}, f32[8,8,2048]{2,1,0:T(8,128)}, f32[8,32,896]{2,1,0:T(8,128)}, f32[5,32,1024]{2,1,0:T(8,128)}, f32[16,128]{1,0:T(8,128)}) custom-call(f32[8,2048,128]{2,1,0:T(8,128)} %bitcast.232, f32[8,2048]{1,0:T(8,128)} %select_maximum_fusion.stats, f32[4,8,32,896]{3,2,1,0:T(8,128)} %bitcast.239, ...), custom_call_target="tpu_custom_call" | custom-call | tf_op jit(solution)/shard_map/pallas_call | solution.py:434
  720.6 4.3 fusion.40.rows
  724.9 56.0 %shard_map.325 = (bf16[4,2048,128]{2,1,0:T(8,128)(2,1)}, f32[4,8,32,896]{3,2,1,0:T(8,128)}, f32[4,5,32,1024]{3,2,1,0:T(8,128)}) custom-call(bf16[2048,128]{1,0:T(8,128)(2,1)} %fusion.40.rows, f32[8,32,896]{2,1,0:T(8,128)} %get-tuple-element.56.sum_in, f32[5,32,1024]{2,1,0:T(8,128)} %get-tuple-element.57.sum_back), custom_call_target="tpu_custom_call" | custom-call | tf_op jit(solution)/shard_map/pallas_call | solution.py:434
  780.9 4.2 copy.195
  795.5 6.2 sort.15
  801.7 29.5 %gather_fusion = bf16[8192,128]{1,0:T(8,128)(2,1)} fusion(bf16[8192,128]{1,0:T(8,128)(2,1)S(1)} %bitcast.230, s32[8192]{0:T(1024)S(1)} %fusion.142), kind=kCustom, calls=%fused_computation | custom fusion | bytes 4227072 | tf_op jit(solution)/shard_map/jit(_take)/gather | solution.py:1532
  831.2 6.6 broadcast_select_fusion.rows
  837.8 2.7 copy.196.ids
  841.5 53.6 %shard_map.327 = (f32[128,50304]{1,0:T(8,128)}, f32[128,512]{1,0:T(8,128)}) custom-call(s32[101]{0:T(128)} %convert_reduce_fusion.1.starts, s32[8192,1]{1,0:T(8,128)} %copy.196.ids, bf16[8192,128]{1,0:T(8,128)(2,1)} %broadcast_select_fusion.rows), custom_call_target="tpu_custom_call" | custom-call | tf_op jit(solution)/shard_map/pallas_call | solution.py:1219
  898.0 16.6 %shard_map.328 = f32[8,8,128]{2,1,0:T(8,128)} custom-call(f32[8,128]{1,0:T(8,128)} %broadcast_in_dim.219.stats), custom_call_target="tpu_custom_call" | custom-call | tf_op jit(solution)/shard_map/pallas_call | solution.py:434
  916.7 61.0 %multiply_subtract_fusion = (f32[128,50304]{1,0:T(8,128)}, f32[128,50304]{1,0:T(8,128)}, f32[128,50304]{1,0:T(8,128)}) fusion(f32[128,50304]{1,0:T(8,128)} %table.1, f32[128,50304]{1,0:T(8,128)} %get-tuple-element.68, f32[]{:T(128)S(6)} %div.134, f32[128,50304]{1,0:T(8,128)} %param.36, f32[128,50304]{1,0:T(8,128)} %param.37), kind=kLoop, calls=%fused_computation.8 | loop fusion | flops 103022592 | bytes 180289536 | tf_op jit(solution)/shard_map/sub | solution.py:104
  977.6 61.7 %multiply_subtract_fusion.1 = (f32[1024,6288]{0,1:T(8,128)}, f32[1024,6288]{0,1:T(8,128)}, f32[1024,6288]{0,1:T(8,128)}) fusion(f32[1024,6288]{0,1:T(8,128)} %param.26, f32[6288,1024]{1,0:T(8,128)} %get-tuple-element.67, f32[]{:T(128)S(6)} %div.134, f32[1024,6288]{0,1:T(8,128)} %param.34, f32[1024,6288]{0,1:T(8,128)} %param.35), kind=kLoop, calls=%fused_computation.10 | loop fusion | flops 103022592 | bytes 180289536 | tf_op jit(solution)/shard_map/sub | solution.py:104
  1042.7 6.9 multiply_subtract_fusion.3
  1049.7 6.6 multiply_subtract_fusion.2
  (382 shorter events, 123.9 us)
Async XLA Ops:
  22.6 17.1 %copy-start.10 = (f32[128,7168]{1,0:T(8,128)S(1)}, f32[128,7168]{1,0:T(8,128)}, u32[]{:S(2)}) copy-start(f32[128,7168]{1,0:T(8,128)} %param.23) | copy-start | bytes 11010052
  128.9 4.9 copy-start.48
  133.8 6.8 copy-start.44
  133.8 11.6 %copy-start.41 = (f32[14336]{0:T(1024)}, f32[14336]{0:T(1024)S(1)}, u32[]{:S(2)}) copy-start(f32[14336]{0:T(1024)S(1)} %reshape.777) | copy-start | bytes 172036
  134.4 6.1 copy-start.51
  134.4 6.1 copy-start.52
  134.4 95.9 %copy-start.46 = (f32[1024]{0:T(1024)}, f32[1024]{0:T(1024)S(1)}, u32[]{:S(2)}) copy-start(f32[1024]{0:T(1024)S(1)} %get-tuple-element.142) | copy-start | bytes 12292
  142.4 5.8 copy-start.58
  151.9 5.2 copy-start.16
  152.5 4.7 copy-start.18
  159.9 9.7 copy-start.30
  160.0 9.6 copy-start.34
  172.9 5.6 copy-start.23
  173.0 5.6 copy-start.31
  178.6 50.6 %copy-start.61 = (f32[1024]{0:T(1024)S(1)}, f32[1024]{0:T(1024)}, u32[]{:S(2)}) copy-start(f32[1024]{0:T(1024)} %get-tuple-element.144) | copy-start | bytes 12292
  179.6 50.5 %copy-start.43 = (s32[1,4,2,2,4,32]{5,4,3,2,1,0:T(4,128)S(1)}, s32[1,4,2,2,4,32]{5,4,3,2,1,0:T(4,128)}, u32[]{:S(2)}) copy-start(s32[1,4,2,2,4,32]{5,4,3,2,1,0:T(4,128)} %get-tuple-element.140) | copy-start | bytes 24580
  179.6 50.8 %copy-start.60 = (f32[1024]{0:T(1024)S(1)}, f32[1024]{0:T(1024)}, u32[]{:S(2)}) copy-start(f32[1024]{0:T(1024)} %get-tuple-element.143) | copy-start | bytes 12292
  229.3 47.0 %copy-start.21 = (f32[64,1024]{1,0:T(8,128)}, f32[64,1024]{1,0:T(8,128)S(1)}, u32[]{:S(2)}) copy-start(f32[64,1024]{1,0:T(8,128)S(1)} %get-tuple-element.109) | copy-start | bytes 786436
  229.4 46.9 %copy-start.65 = (f32[64]{0:T(128)}, f32[64]{0:T(128)S(1)}, u32[]{:S(2)}) copy-start(f32[64]{0:T(128)S(1)} %broadcast_multiply_fusion.2) | copy-start | bytes 772
  229.6 46.7 %copy-start.69 = (f32[64]{0:T(128)}, f32[64]{0:T(128)S(1)}, u32[]{:S(2)}) copy-start(f32[64]{0:T(128)S(1)} %fusion.170) | copy-start | bytes 772
  230.2 46.1 %copy-start.49 = (s32[4,512]{1,0:T(4,128)}, s32[4,512]{1,0:T(4,128)S(1)}, u32[]{:S(2)}) copy-start(s32[4,512]{1,0:T(4,128)S(1)} %get-tuple-element.106) | copy-start | bytes 24580
  287.8 23.3 %copy-start = (bf16[512,1024]{1,0:T(8,128)(2,1)S(1)}, bf16[512,1024]{1,0:T(8,128)(2,1)}, u32[]{:S(2)}) copy-start(bf16[512,1024]{1,0:T(8,128)(2,1)} %shard_map.318.rows) | copy-start | bytes 3145732
  287.8 23.3 %copy-start.3 = (f32[8,512]{1,0:T(8,128)S(1)}, f32[8,512]{1,0:T(8,128)}, u32[]{:S(2)}) copy-start(f32[8,512]{1,0:T(8,128)} %maximum_maximum_fusion.facts) | copy-start | bytes 49156
  287.8 61.7 %copy-start.50 = (s32[4,512]{1,0:T(4,128)S(1)}, s32[4,512]{1,0:T(4,128)}, u32[]{:S(2)}) copy-start(s32[4,512]{1,0:T(4,128)} %copy-done.49) | copy-start | bytes 24580
  350.1 67.3 %copy-start.22 = (f32[64,1024]{1,0:T(8,128)S(1)}, f32[64,1024]{1,0:T(8,128)}, u32[]{:S(2)}) copy-start(f32[64,1024]{1,0:T(8,128)} %copy-done.21) | copy-start | bytes 786436
  350.1 67.3 %copy-start.47 = (f32[1024]{0:T(1024)S(1)}, f32[1024]{0:T(1024)}, u32[]{:S(2)}) copy-start(f32[1024]{0:T(1024)} %copy-done.46) | copy-start | bytes 12292
  350.1 67.3 %copy-start.66 = (f32[64]{0:T(128)S(1)}, f32[64]{0:T(128)}, u32[]{:S(2)}) copy-start(f32[64]{0:T(128)} %copy-done.65) | copy-start | bytes 772
  350.1 67.3 %copy-start.70 = (f32[64]{0:T(128)S(1)}, f32[64]{0:T(128)}, u32[]{:S(2)}) copy-start(f32[64]{0:T(128)} %copy-done.69) | copy-start | bytes 772
  350.2 68.1 %copy-start.87 = (f32[64]{0:T(128)S(1)}, f32[64]{0:T(128)}, u32[]{:S(2)}) copy-start(f32[64]{0:T(128)} %copy-done.86) | copy-start | bytes 772
  418.4 29.6 %copy-start.72 = (f32[4,2,128]{2,1,0:T(2,128)S(1)}, f32[4,2,128]{2,1,0:T(2,128)}, u32[]{:S(2)}) copy-start(f32[4,2,128]{2,1,0:T(2,128)} %copy-done.71) | copy-start | bytes 12292
  456.8 8.3 copy-start.25
  467.9 7.9 copy-start.82
  518.4 12.6 %copy-start.64 = (f32[1024]{0:T(1024)S(1)}, f32[1024]{0:T(1024)}, u32[]{:S(2)}) copy-start(f32[1024]{0:T(1024)} %get-tuple-element.170) | copy-start | bytes 12292
  518.4 13.8 %copy-start.73 = (f32[1024]{0:T(1024)S(1)}, f32[1024]{0:T(1024)}, u32[]{:S(2)}) copy-start(f32[1024]{0:T(1024)} %get-tuple-element.172) | copy-start | bytes 12292
  518.4 14.4 %copy-start.63 = (f32[1024]{0:T(1024)S(1)}, f32[1024]{0:T(1024)}, u32[]{:S(2)}) copy-start(f32[1024]{0:T(1024)} %get-tuple-element.73) | copy-start | bytes 12292
  518.4 15.0 %copy-start.62 = (f32[1024]{0:T(1024)S(1)}, f32[1024]{0:T(1024)}, u32[]{:S(2)}) copy-start(f32[1024]{0:T(1024)} %get-tuple-element.75) | copy-start | bytes 12292
  559.5 4.3 copy-start.88
  585.3 134.2 %copy-start.40 = (f32[8,64,128]{2,1,0:T(8,128)S(1)}, f32[8,64,128]{2,1,0:T(8,128)}, u32[]{:S(2)}) copy-start(f32[8,64,128]{2,1,0:T(8,128)} %get-tuple-element.52) | copy-start | bytes 786436
  585.3 135.3 %copy-start.45 = (f32[2048]{0:T(1024)S(1)}, f32[2048]{0:T(1024)}, u32[]{:S(2)}) copy-start(f32[2048]{0:T(1024)} %copy-done.44) | copy-start | bytes 24580
  789.5 6.0 copy-start.39
  789.5 12.1 %copy-start.5 = (bf16[4,2048,128]{2,1,0:T(8,128)(2,1)S(1)}, bf16[4,2048,128]{2,1,0:T(8,128)(2,1)}, u32[]{:S(2)}) copy-start(bf16[4,2048,128]{2,1,0:T(8,128)(2,1)} %get-tuple-element.65) | copy-start | bytes 6291460
  977.6 61.7 %copy-start.53 = (f32[1792]{0:T(1024)S(1)}, f32[1792]{0:T(1024)}, u32[]{:S(2)}) copy-start(f32[1792]{0:T(1024)} %param.25) | copy-start | bytes 21508
  977.6 61.7 %copy-start.67 = (f32[1792]{0:T(1024)S(1)}, f32[1792]{0:T(1024)}, u32[]{:S(2)}) copy-start(f32[1792]{0:T(1024)} %param.32) | copy-start | bytes 21508
  977.6 61.7 %copy-start.68 = (f32[1792]{0:T(1024)S(1)}, f32[1792]{0:T(1024)}, u32[]{:S(2)}) copy-start(f32[1792]{0:T(1024)} %param.33) | copy-start | bytes 21508
  977.6 62.3 %copy-start.15 = (f32[4,5,32,1024]{3,2,1,0:T(8,128)S(1)}, f32[4,5,32,1024]{3,2,1,0:T(8,128)}, u32[]{:S(2)}) copy-start(f32[4,5,32,1024]{3,2,1,0:T(8,128)} %get-tuple-element.59) | copy-start | bytes 7864324
  1042.7 6.9 copy-start.8
  1042.7 6.9 copy-start.11
  1042.7 6.9 copy-start.26
  (43 other events, 97.0 us)

commit v2 on v1

--- a/solution.py
+++ b/solution.py
@@ -425,67 +425,25 @@
     )
 
 
-def comm_call(kernel, out_shape, scratch, number, args, spaces=None, out_spaces=None, limit=None):
-    any_spec = pl.BlockSpec(memory_space=pl.ANY)
-    vmem_spec = pl.BlockSpec(memory_space=pltpu.VMEM)
-    pick = {"a": any_spec, "v": vmem_spec}
+def comm_call(kernel, out_shape, scratch, number, args, spaces=None, out_spaces=None, limit=None, grid=()):
+    pick = {
+        "a": pl.BlockSpec(memory_space=pl.ANY),
+        "v": pl.BlockSpec(memory_space=pltpu.VMEM),
+    }
+    choose = lambda space: pick[space] if isinstance(space, str) else space
     spaces = spaces or "a" * len(args)
     out_spaces = out_spaces or "a" * len(out_shape)
     return pl.pallas_call(
         kernel,
+        grid=grid,
         out_shape=out_shape,
-        in_specs=[pick[space] for space in spaces],
-        out_specs=[pick[space] for space in out_spaces],
+        in_specs=[choose(space) for space in spaces],
+        out_specs=[choose(space) for space in out_spaces],
         scratch_shapes=scratch,
         compiler_params=pltpu.CompilerParams(
             collective_id=number, has_side_effects=True, vmem_limit_bytes=limit
         ),
     )(*args)
-
-
-def facts_kernel(ints, smalls, ints_all, smalls_all, send_int, recv_int, send_small, recv_small, send_rep, recv_rep, own):
-    rep, shard, _, _, _ = whereabouts()
-    shard_peers = [(rep, shard_peer(shard, step)) for step in range(1, SG)]
-    rep_peers = [(lax.rem(rep + step, RG), shard) for step in range(1, RG)]
-    greet(shard_peers + rep_peers)
-    copies = []
-    for at, peer in enumerate(shard_peers):
-        copies.append(remote(ints, ints_all.at[rep, shard], send_int.at[at], recv_int.at[at], peer))
-        copies[-1].start()
-    small_copies = []
-    for at, peer in enumerate(shard_peers):
-        small_copies.append(remote(smalls, smalls_all.at[shard], send_small.at[at], recv_small.at[at], peer))
-        small_copies[-1].start()
-    keep_int = pltpu.make_async_copy(ints, ints_all.at[rep, shard], own.at[0])
-    keep_small = pltpu.make_async_copy(smalls, smalls_all.at[shard], own.at[1])
-    keep_int.start()
-    keep_small.start()
-    keep_int.wait()
-    for copy in copies:
-        copy.wait()
-    rep_copies = []
-    for at, peer in enumerate(rep_peers):
-        rep_copies.append(remote(ints_all.at[rep], ints_all.at[rep], send_rep.at[at], recv_rep.at[at], peer))
-        rep_copies[-1].start()
-    keep_small.wait()
-    for copy in small_copies + rep_copies:
-        copy.wait()
-
-
-def share_facts(ints, smalls, number):
-    dma = pltpu.SemaphoreType.DMA
-    return comm_call(
-        facts_kernel,
-        [
-            jax.ShapeDtypeStruct((RG, SG) + ints.shape, ints.dtype),
-            jax.ShapeDtypeStruct((SG,) + smalls.shape, smalls.dtype),
-        ],
-        [dma((SG - 1,))] * 4 + [dma((RG - 1,))] * 2 + [dma((2,))],
-        number,
-        (ints, smalls),
-        "vv",
-        "vv",
-    )
 
 
 def start_gather(source, out, slot, place, sems):
@@ -532,11 +490,6 @@
 GATHER_SEMS = [pltpu.SemaphoreType.DMA((3,)), pltpu.SemaphoreType.DMA((3,)), pltpu.SemaphoreType.DMA((4,)), pltpu.SemaphoreType.DMA((4,)), pltpu.SemaphoreType.DMA]
 
 
-def column_slot(out, index):
-    width = out.shape[1] // SG
-    return out.at[:, pl.ds(pl.multiple_of(index * width, width), width)]
-
-
 def row_slot(out, index):
     height = out.shape[0] // SG
     return out.at[pl.ds(pl.multiple_of(index * height, height), height)]
@@ -550,72 +503,197 @@
     return jnp.where(tile < SG, 0, 1 + lax.rem(tile - SG + SG, 4))
 
 
-def embed_kernel(rows, in_parts, back_tiles, out, in_all, back_all, *sems):
-    gather_sems = sems[:5]
-    send_in, recv_in, send_back, recv_back, own_in, send_pair, recv_pair = sems[5:]
-    place = whereabouts()
-    rep, shard, core_twin, _, _ = place
+def entry_kernel(
+    ints, smalls, in_parts, back_tiles, table,
+    ints_out, smalls_out, out, in_all, back_all,
+    ints_all, smalls_all, turned, wide, low, ids,
+    send_int, recv_int, send_small, recv_small, send_rep, recv_rep,
+    send_in, recv_in, send_back, recv_back, send_pair, recv_pair,
+    send_z, recv_z, send_y, recv_y, own,
+):
+    at = pl.program_id(0)
+    rep, shard, core_twin, _, y_twin = whereabouts()
     half = lax.rem(rep, 2)
-    greet([(rep, shard_peer(shard, step)) for step in range(1, SG)] + [(core_twin, shard)])
-    started = start_gather(rows, out, column_slot, place, gather_sems)
-    in_copies = []
-    for step in range(1, SG):
-        peer = shard_peer(shard, step)
-        in_copies.append(
-            remote(in_parts.at[peer, half], in_all.at[shard, half], send_in.at[step - 1], recv_in.at[step - 1], (rep, peer))
-        )
-        in_copies[-1].start()
-    keep_in = pltpu.make_async_copy(in_parts.at[shard, half], in_all.at[shard, half], own_in)
-    keep_in.start()
-    moves = []
-    for at in range(5):
-        tile = 5 * shard + at
-        user = tile_user(tile)
-        slot = tile_slot(tile)
-        there = remote(back_tiles.at[at, half], back_all.at[slot, half], send_back.at[at], recv_back.at[slot], (rep, user))
-        here = pltpu.make_async_copy(back_tiles.at[at, half], back_all.at[slot, half], recv_back.at[slot])
-
-        @pl.when(user == shard)
-        def _():
-            here.start()
-
-        @pl.when(user != shard)
-        def _():
-            there.start()
-
-        moves.append((user, there))
-    finish_gather(started, out, column_slot, place, gather_sems)
-    keep_in.wait()
-    for copy in in_copies:
-        copy.wait()
-    for slot in range(5):
-        pltpu.make_async_copy(back_tiles.at[0, half], back_all.at[slot, half], recv_back.at[slot]).wait()
-    pair_in = remote(in_all.at[:, half], in_all.at[:, half], send_pair.at[0], recv_pair.at[0], (core_twin, shard))
-    pair_back = remote(back_all.at[:, half], back_all.at[:, half], send_pair.at[1], recv_pair.at[1], (core_twin, shard))
-    pair_in.start()
-    pair_back.start()
-    for user, there in moves:
-
-        @pl.when(user != shard)
-        def _():
-            there.wait_send()
-
-    pair_in.wait()
-    pair_back.wait()
-
-
-def share_embedding(rows, in_parts, back_tiles, number):
+    shard_peers = [(rep, shard_peer(shard, step)) for step in range(1, SG)]
+    rep_peers = [(lax.rem(rep + step, RG), shard) for step in range(1, RG)]
+    lines = low.shape[0]
+    tokens = low.shape[1]
+
+    def int_copies():
+        return [
+            remote(ints, ints_all.at[rep, shard], send_int.at[k], recv_int.at[k], peer)
+            for k, peer in enumerate(shard_peers)
+        ]
+
+    def small_copies():
+        return [
+            remote(smalls, smalls_all.at[shard], send_small.at[k], recv_small.at[k], peer)
+            for k, peer in enumerate(shard_peers)
+        ]
+
+    def rep_copies():
+        return [
+            remote(ints_all.at[rep], ints_all.at[rep], send_rep.at[k], recv_rep.at[k], peer)
+            for k, peer in enumerate(rep_peers)
+        ]
+
+    def in_copies():
+        return [
+            remote(in_parts.at[peer[1], half], in_all.at[shard, half], send_in.at[k], recv_in.at[k], peer)
+            for k, peer in enumerate(shard_peers)
+        ]
+
+    def own_in():
+        return pltpu.make_async_copy(in_parts.at[shard, half], in_all.at[shard, half], own.at[0])
+
+    def back_move(k):
+        tile = 5 * shard + k
+        user, slot = tile_user(tile), tile_slot(tile)
+        there = remote(
+            back_tiles.at[k, half], back_all.at[slot, half], send_back.at[k], recv_back.at[slot], (rep, user)
+        )
+        return user, slot, there
+
+    @pl.when(at == 0)
+    def _():
+        greet(shard_peers + rep_peers)
+        for copy in int_copies() + small_copies() + in_copies():
+            copy.start()
+        own_in().start()
+        for k in range(5):
+            user, slot, there = back_move(k)
+            here = pltpu.make_async_copy(back_tiles.at[k, half], back_all.at[slot, half], recv_back.at[slot])
+            pl.when(user == shard)(here.start)
+            pl.when(user != shard)(there.start)
+        ints_all[rep, shard] = ints[...]
+        smalls_all[shard] = smalls[...]
+
+    block = table[...].astype(jnp.bfloat16).astype(jnp.float32)
+    width = block.shape[1]
+    turned[pl.ds(pl.multiple_of(at * width, width), width), :] = block.T
+
+    @pl.when(at == 4)
+    def _():
+        for copy in int_copies():
+            copy.wait()
+        for copy in rep_copies():
+            copy.start()
+
+    @pl.when(at == pl.num_programs(0) - 1)
+    def _():
+        for copy in rep_copies():
+            copy.wait()
+        to_scalars = pltpu.make_async_copy(ints_all.at[:, pl.ds(2 * rep, 2)], ids, own.at[1])
+        to_scalars.start()
+        to_scalars.wait()
+
+        def slot(index, line):
+            return out.at[
+                pl.ds(line * tokens, tokens),
+                pl.ds(pl.multiple_of(index * low.shape[2], low.shape[2]), low.shape[2]),
+            ]
+
+        def line_copies(line):
+            z_copies = [
+                remote(low.at[line], slot(shard, line), send_z.at[line, k - 1], recv_z.at[line, k - 1], (rep, z_peer(shard, k)))
+                for k in range(1, 4)
+            ]
+            first_y = remote(low.at[line], slot(shard, line), send_y.at[line, 0], recv_y.at[line, 0], (rep, y_twin))
+            keep = pltpu.make_async_copy(low.at[line], slot(shard, line), own.at[2 + line])
+            return z_copies, first_y, keep
+
+        started = []
+        for line in range(lines):
+            micro, member = line // 2, line % 2
+            for block_at in range(RG):
+
+                @pl.loop(0, 16)
+                def _(group):
+                    for k in range(8):
+                        lane = group * 8 + k
+                        wide[pl.ds(block_at * 128 + lane, 1), :] = turned[
+                            pl.ds(ids[block_at, member, micro, lane], 1), :
+                        ]
+
+            low[line] = wide[...].astype(jnp.bfloat16)
+            z_copies, first_y, keep = line_copies(line)
+            for copy in z_copies + [first_y, keep]:
+                copy.start()
+            started.append((z_copies, first_y, keep))
+        passed = []
+        for line in range(lines):
+            for k in range(1, 4):
+                started[line][0][k - 1].wait_recv()
+                came_from = z_peer(shard, 4 - k)
+                copy = remote(
+                    slot(came_from, line), slot(came_from, line), send_y.at[line, k], recv_y.at[line, k], (rep, y_twin)
+                )
+                copy.start()
+                passed.append(copy)
+        own_in().wait()
+        for copy in in_copies():
+            copy.wait()
+        for k in range(5):
+            pltpu.make_async_copy(back_tiles.at[0, half], back_all.at[k, half], recv_back.at[k]).wait()
+        pair_in = remote(in_all.at[:, half], in_all.at[:, half], send_pair.at[0], recv_pair.at[0], (core_twin, shard))
+        pair_back = remote(back_all.at[:, half], back_all.at[:, half], send_pair.at[1], recv_pair.at[1], (core_twin, shard))
+        pair_in.start()
+        pair_back.start()
+        for copy in small_copies():
+            copy.wait()
+        ints_out[...] = ints_all[...]
+        smalls_out[...] = smalls_all[...]
+        for k in range(5):
+            user, _, there = back_move(k)
+            pl.when(user != shard)(there.wait_send)
+        for z_copies, first_y, keep in started:
+            keep.wait()
+            first_y.wait()
+            for copy in z_copies:
+                copy.wait_send()
+        for copy in passed:
+            copy.wait()
+        pair_in.wait()
+        pair_back.wait()
+
+
+def share_entry(ints, smalls, in_parts, back_tiles, table, tokens, number):
     dma = pltpu.SemaphoreType.DMA
+    feats, vocab = table.shape
+    blocks = pl.cdiv(vocab, TABLE_BLOCK)
+    lines = 4
+    per_line = tokens // lines
     return comm_call(
-        embed_kernel,
+        entry_kernel,
         [
-            jax.ShapeDtypeStruct((rows.shape[0], SG * rows.shape[1]), rows.dtype),
+            jax.ShapeDtypeStruct((RG, SG) + ints.shape, ints.dtype),
+            jax.ShapeDtypeStruct((SG,) + smalls.shape, smalls.dtype),
+            jax.ShapeDtypeStruct((tokens, SG * feats), jnp.bfloat16),
             jax.ShapeDtypeStruct(in_parts.shape, in_parts.dtype),
             jax.ShapeDtypeStruct(back_tiles.shape, back_tiles.dtype),
         ],
-        GATHER_SEMS + [dma((SG - 1,))] * 2 + [dma((5,))] * 2 + [dma] + [dma((2,))] * 2,
+        [
+            pltpu.VMEM((RG, SG) + ints.shape, ints.dtype),
+            pltpu.VMEM((SG,) + smalls.shape, smalls.dtype),
+            pltpu.VMEM((blocks * TABLE_BLOCK, feats), jnp.float32),
+            pltpu.VMEM((per_line, feats), jnp.float32),
+            pltpu.VMEM((lines, per_line, feats), jnp.bfloat16),
+            pltpu.SMEM((RG, 2) + ints.shape, jnp.int32),
+        ]
+        + [dma((SG - 1,))] * 4
+        + [dma((RG - 1,))] * 2
+        + [dma((SG - 1,))] * 2
+        + [dma((5,))] * 2
+        + [dma((2,))] * 2
+        + [dma((lines, 3))] * 2
+        + [dma((lines, 4))] * 2
+        + [dma((2 + lines,))],
         number,
-        (rows, in_parts, back_tiles),
+        (ints, smalls, in_parts, back_tiles, table),
+        ["v", "v", "a", "a", pl.BlockSpec((feats, TABLE_BLOCK), lambda at: (0, at))],
+        "vvaaa",
+        VMEM_LIMIT,
+        (blocks,),
     )
 
 
@@ -812,165 +890,199 @@
     )
 
 
-def layer_kernel(parts, stats, grad_in, grad_back, smalls, out, stats_all, sum_in, sum_back, smalls_out,
-                 from_y, own_sum, from_z, pair_in, pair_back, half_in, half_back, far_in, far_back, small_rep, small_sum, small_shard, *sems):
-    place = whereabouts()
-    rep, shard, core_twin, x_twin, _ = place
-    sum_sem = sems[:4]
-    send_stat, recv_stat, send_pair, recv_pair, send_far, recv_far, send_rep, recv_rep, send_small, recv_small = sems[4:]
+def layer_kernel(
+    vocab, parts, stats, grad_in, grad_back, smalls, rows, facts, targets, head,
+    out, stats_out, sum_in, sum_back, smalls_out, head_out, squares,
+    stats_all, from_y, own_sum, from_z, pair_in, pair_back, half_in, half_back, far_in, far_back, small_rep, small_sum, small_shard,
+    send_y, recv_y, send_z, recv_z, send_stat, recv_stat, send_pair, recv_pair, send_far, recv_far,
+    send_rep, recv_rep, send_small, recv_small,
+):
+    at = pl.program_id(0)
+    last = pl.num_programs(0) - 1
+    rep, shard, core_twin, x_twin, y_twin = whereabouts()
+    core_far = lax.rem(core_twin + 2, RG)
     shard_peers = [(rep, shard_peer(shard, step)) for step in range(1, SG)]
     rep_peers = [(lax.rem(rep + step, RG), shard) for step in range(1, RG)]
-    greet(shard_peers + rep_peers)
-    buffers = (from_y, own_sum, from_z)
-    rep_copies = [
-        remote(smalls, small_rep.at[at], send_rep.at[at], recv_rep.at[at], peer) for at, peer in enumerate(rep_peers)
-    ]
-    for copy in rep_copies:
-        copy.start()
-    core_far = lax.rem(core_twin + 2, RG)
-    pair_copies = [
-        remote(grad_in.at[core_far], pair_in.at[1], send_pair.at[0], recv_pair.at[0], (core_twin, shard)),
-        remote(grad_back.at[core_far], pair_back.at[1], send_pair.at[1], recv_pair.at[1], (core_twin, shard)),
-        remote(grad_in.at[core_twin], pair_in.at[0], send_pair.at[2], recv_pair.at[2], (core_twin, shard)),
-        remote(grad_back.at[core_twin], pair_back.at[0], send_pair.at[3], recv_pair.at[3], (core_twin, shard)),
-    ]
-    for copy in pair_copies:
-        copy.start()
-    y_copies = start_sum(parts, place, buffers, sum_sem)
-    stat_copies = [
-        remote(stats, stats_all.at[shard], send_stat.at[at], recv_stat.at[at], peer) for at, peer in enumerate(shard_peers)
-    ]
-    for copy in stat_copies:
-        copy.start()
-    stats_all[shard] = stats[...]
-    pair_copies[0].wait()
-    pair_copies[1].wait()
-    half_in[...] = grad_in[x_twin] + pair_in[1]
-    half_back[...] = grad_back[x_twin] + pair_back[1]
-    far_copies = [
-        remote(half_in, far_in, send_far.at[0], recv_far.at[0], (x_twin, shard)),
-        remote(half_back, far_back, send_far.at[1], recv_far.at[1], (x_twin, shard)),
-    ]
-    for copy in far_copies:
-        copy.start()
-    for copy in rep_copies:
-        copy.wait()
-    small_sum[...] = smalls[...] + small_rep[0] + small_rep[1] + small_rep[2]
-    small_copies = [
-        remote(small_sum.at[peer[1]], small_shard.at[at], send_small.at[at], recv_small.at[at], peer)
-        for at, peer in enumerate(shard_peers)
-    ]
-    for copy in small_copies:
-        copy.start()
-    finish_sum(y_copies, parts, out, place, buffers, sum_sem)
-    pair_copies[2].wait()
-    pair_copies[3].wait()
-    for copy in far_copies:
-        copy.wait()
-    sum_in[...] = grad_in[rep] + pair_in[0] + far_in[...]
-    sum_back[...] = grad_back[rep] + pair_back[0] + far_back[...]
-    for copy in stat_copies + small_copies:
-        copy.wait()
-    total = small_sum[shard]
-    for at in range(SG - 1):
-        total = total + small_shard[at]
-    smalls_out[...] = total
-
-
-def layer_sums(parts, stats, grad_in, grad_back, smalls, number):
+
+    def rep_copies():
+        return [
+            remote(smalls, small_rep.at[k], send_rep.at[k], recv_rep.at[k], peer) for k, peer in enumerate(rep_peers)
+        ]
+
+    def pair_copies(which, slot):
+        pairs = ((grad_in, pair_in), (grad_back, pair_back))
+        return [
+            remote(
+                source.at[which], target.at[slot], send_pair.at[2 * slot + k], recv_pair.at[2 * slot + k],
+                (core_twin, shard),
+            )
+            for k, (source, target) in enumerate(pairs)
+        ]
+
+    def y_copy(step):
+        return remote(parts.at[z_peer(y_twin, step)], from_y.at[step], send_y.at[step], recv_y.at[step], (rep, y_twin))
+
+    def z_copy(step):
+        return remote(
+            own_sum.at[step], from_z.at[step - 1], send_z.at[step - 1], recv_z.at[step - 1], (rep, z_peer(shard, step))
+        )
+
+    def stat_copies():
+        return [
+            remote(stats, stats_all.at[shard], send_stat.at[k], recv_stat.at[k], peer)
+            for k, peer in enumerate(shard_peers)
+        ]
+
+    def far_copies():
+        return [
+            remote(half_in, far_in, send_far.at[0], recv_far.at[0], (x_twin, shard)),
+            remote(half_back, far_back, send_far.at[1], recv_far.at[1], (x_twin, shard)),
+        ]
+
+    def small_copies():
+        return [
+            remote(small_sum.at[peer[1]], small_shard.at[k], send_small.at[k], recv_small.at[k], peer)
+            for k, peer in enumerate(shard_peers)
+        ]
+
+    def pass_on(step):
+        y_copy(step).wait_recv()
+        own_sum[step] = parts[z_peer(shard, step)] + from_y[step]
+        z_copy(step).start()
+
+    @pl.when(at == 0)
+    def _():
+        greet(shard_peers + rep_peers)
+        for step in (2, 1, 3, 0):
+            y_copy(step).start()
+        for copy in pair_copies(core_far, 1) + pair_copies(core_twin, 0) + rep_copies() + stat_copies():
+            copy.start()
+        stats_all[shard] = stats[...]
+        squares[...] = jnp.zeros_like(squares)
+
+    @pl.when(at == 2)
+    def _():
+        for copy in pair_copies(core_far, 1):
+            copy.wait()
+        half_in[...] = grad_in[x_twin] + pair_in[1]
+        half_back[...] = grad_back[x_twin] + pair_back[1]
+        for copy in far_copies():
+            copy.start()
+        for copy in rep_copies():
+            copy.wait()
+        small_sum[...] = smalls[...] + small_rep[0] + small_rep[1] + small_rep[2]
+        for copy in small_copies():
+            copy.start()
+
+    pl.when(at == 5)(lambda: pass_on(2))
+    pl.when(at == 9)(lambda: pass_on(1))
+
+    _, low = vocab_rows(vocab, head[...])
+    total = None
+    for group in range(RG):
+        grads = logit_grads(
+            vocab, low, rows[group], facts[group, 0:1, :], targets[group, 0:1, :], facts[group, 1:2, :]
+        )
+        term = plain_dot(grads, rows[group])
+        total = term if total is None else total + term
+    head_out[...] = total
+    squares[0:1, :] += jnp.sum(total * total, axis=0, keepdims=True)
+
+    @pl.when(at == last)
+    def _():
+        pass_on(3)
+        for copy in pair_copies(core_twin, 0):
+            copy.wait()
+        for copy in far_copies():
+            copy.wait()
+        sum_in[...] = grad_in[rep] + pair_in[0] + far_in[...]
+        sum_back[...] = grad_back[rep] + pair_back[0] + far_back[...]
+        for copy in stat_copies() + small_copies():
+            copy.wait()
+        stats_out[...] = stats_all[...]
+        whole = small_sum[shard]
+        for k in range(SG - 1):
+            whole = whole + small_shard[k]
+        smalls_out[...] = whole
+        y_copy(0).wait_recv()
+        own = parts[shard] + from_y[0]
+        for step in (1, 2, 3):
+            z_copy(step).wait()
+        out[...] = own + from_z[0] + from_z[1] + from_z[2]
+        for step in range(4):
+            y_copy(step).wait_send()
+
+
+def layer_sums(parts, stats, grad_in, grad_back, smalls, rows, facts, targets, head, number):
     dma = pltpu.SemaphoreType.DMA
     chunk = parts.shape[1:]
     quarter_in, quarter_back, piece = grad_in.shape[1:], grad_back.shape[1:], smalls.shape[1:]
+    vocab, depth = head.shape
     vmem = lambda shape: pltpu.VMEM(shape, jnp.float32)
     shape = lambda dims: jax.ShapeDtypeStruct(dims, jnp.float32)
+    block = pl.BlockSpec((VOCAB_BLOCK, depth), lambda at: (at, 0))
     return comm_call(
-        layer_kernel,
-        [shape(chunk), shape((SG,) + stats.shape), shape(quarter_in), shape(quarter_back), shape(piece)],
-        sum_buffers(chunk)
+        functools.partial(layer_kernel, vocab),
+        [shape(chunk), shape((SG,) + stats.shape), shape(quarter_in), shape(quarter_back), shape(piece), shape(head.shape), shape((8, depth))],
+        [vmem((SG,) + stats.shape)]
+        + sum_buffers(chunk)
         + [vmem((2,) + quarter_in), vmem((2,) + quarter_back), vmem(quarter_in), vmem(quarter_back), vmem(quarter_in), vmem(quarter_back)]
         + [vmem((3,) + smalls.shape), vmem(smalls.shape), vmem((SG - 1,) + piece)]
         + sum_sems()
         + [dma((SG - 1,))] * 2 + [dma((4,))] * 2 + [dma((2,))] * 2 + [dma((3,))] * 2 + [dma((SG - 1,))] * 2,
         number,
-        (parts, stats, grad_in, grad_back, smalls),
-        "vvvvv",
-        "vvvvv",
+        (parts, stats, grad_in, grad_back, smalls, rows, facts, targets, head),
+        ["v"] * 8 + [block],
+        ["v"] * 5 + [block, "v"],
         62 << 20,
-    )
-
-
-def return_kernel(rows, sum_in, sum_back, rows_all, in_all, back_all, *sems):
-    place = whereabouts()
-    rep, shard, core_twin, x_twin, _ = place
-    (send_row, recv_row, own, send_in, recv_in, send_back, recv_back, send_far, recv_far, send_pair, recv_pair) = sems
-    greet([(rep, shard_peer(shard, step)) for step in range(1, SG)] + [(core_twin, shard), (x_twin, shard)])
-    in_copies = []
-    for step in range(1, SG):
-        peer = shard_peer(shard, step)
-        in_copies.append(
-            remote(sum_in.at[peer], in_all.at[rep, shard], send_in.at[step - 1], recv_in.at[step - 1], (rep, peer))
-        )
-        in_copies[-1].start()
-    keep_in = pltpu.make_async_copy(sum_in.at[shard], in_all.at[rep, shard], own.at[1])
-    keep_in.start()
-    moves = []
-    for slot in range(5):
-        tile = jnp.where(slot == 0, shard, SG + 4 * shard + slot - 1)
-        owner = tile // 5
-        at = lax.rem(tile, 5)
-        there = remote(sum_back.at[slot], back_all.at[rep, at], send_back.at[slot], recv_back.at[at], (rep, owner))
-        here = pltpu.make_async_copy(sum_back.at[slot], back_all.at[rep, at], recv_back.at[at])
-
-        @pl.when(owner == shard)
-        def _():
-            here.start()
-
-        @pl.when(owner != shard)
-        def _():
-            there.start()
-
-        moves.append((owner, there))
+        (pl.cdiv(vocab, VOCAB_BLOCK),),
+    )
+
+
+def return_kernel(
+    rows, sum_in, sum_back, rows_all, in_all, back_all, send_row, recv_row, own, send_in, recv_in, send_back, recv_back
+):
+    rep, shard, core_twin, x_twin, _ = whereabouts()
+    shard_peers = [(rep, shard_peer(shard, step)) for step in range(1, SG)]
+    greet(shard_peers + [(core_twin, shard), (x_twin, shard)])
     keep = pltpu.make_async_copy(rows, rows_all.at[rep], own.at[0])
     keep.start()
     to_x = remote(rows, rows_all.at[rep], send_row.at[0], recv_row.at[0], (x_twin, shard))
     to_core = remote(rows, rows_all.at[rep], send_row.at[1], recv_row.at[1], (core_twin, shard))
     to_x.start()
     to_core.start()
+    in_copies = [
+        remote(sum_in.at[peer[1]], in_all.at[shard], send_in.at[k], recv_in.at[k], peer)
+        for k, peer in enumerate(shard_peers)
+    ]
+    for copy in in_copies:
+        copy.start()
+    keep_in = pltpu.make_async_copy(sum_in.at[shard], in_all.at[shard], own.at[1])
+    keep_in.start()
+    moves = []
+    for slot in range(5):
+        tile = shard if slot == 0 else SG + 4 * shard + slot - 1
+        owner = tile // 5
+        at = lax.rem(tile, 5)
+        there = remote(sum_back.at[slot], back_all.at[at], send_back.at[slot], recv_back.at[at], (rep, owner))
+        here = pltpu.make_async_copy(sum_back.at[slot], back_all.at[at], recv_back.at[at])
+        pl.when(owner == shard)(here.start)
+        pl.when(owner != shard)(there.start)
+        moves.append((owner, there))
+    to_x.wait_recv()
+    passed = remote(rows_all.at[x_twin], rows_all.at[x_twin], send_row.at[2], recv_row.at[2], (core_twin, shard))
+    passed.start()
     keep_in.wait()
     for copy in in_copies:
         copy.wait()
-    in_far = remote(in_all.at[rep], in_all.at[rep], send_far.at[0], recv_far.at[0], (x_twin, shard))
-    in_pair = remote(in_all.at[rep], in_all.at[rep], send_pair.at[0], recv_pair.at[0], (core_twin, shard))
-    in_far.start()
-    in_pair.start()
     for at in range(5):
-        pltpu.make_async_copy(sum_back.at[0], back_all.at[rep, at], recv_back.at[at]).wait()
-    back_far = remote(back_all.at[rep], back_all.at[rep], send_far.at[1], recv_far.at[1], (x_twin, shard))
-    back_pair = remote(back_all.at[rep], back_all.at[rep], send_pair.at[1], recv_pair.at[1], (core_twin, shard))
-    back_far.start()
-    back_pair.start()
-    to_x.wait_recv()
-    passed = remote(rows_all.at[x_twin], rows_all.at[x_twin], send_row.at[2], recv_row.at[2], (core_twin, shard))
-    passed.start()
-    in_far.wait_recv()
-    in_passed = remote(in_all.at[x_twin], in_all.at[x_twin], send_pair.at[2], recv_pair.at[2], (core_twin, shard))
-    in_passed.start()
-    back_far.wait_recv()
-    back_passed = remote(back_all.at[x_twin], back_all.at[x_twin], send_pair.at[3], recv_pair.at[3], (core_twin, shard))
-    back_passed.start()
+        pltpu.make_async_copy(sum_back.at[0], back_all.at[at], recv_back.at[at]).wait()
     for owner, there in moves:
-
-        @pl.when(owner != shard)
-        def _():
-            there.wait_send()
-
+        pl.when(owner != shard)(there.wait_send)
     keep.wait()
     to_x.wait_send()
     to_core.wait()
-    in_far.wait_send()
-    back_far.wait_send()
-    for copy in (in_pair, back_pair, passed, in_passed, back_passed):
-        copy.wait()
+    passed.wait()
 
 
 def return_sums(rows, sum_in, sum_back, number):
@@ -978,11 +1090,54 @@
     shape = lambda dims, like: jax.ShapeDtypeStruct(dims, like.dtype)
     return comm_call(
         return_kernel,
-        [shape((RG,) + rows.shape, rows), shape((RG,) + sum_in.shape, sum_in), shape((RG,) + sum_back.shape, sum_back)],
-        [dma((3,))] * 2 + [dma((2,))] + [dma((SG - 1,))] * 2 + [dma((5,))] * 2 + [dma((2,))] * 2 + [dma((4,))] * 2,
+        [shape((RG,) + rows.shape, rows), shape(sum_in.shape, sum_in), shape(sum_back.shape, sum_back)],
+        [dma((3,))] * 2 + [dma((2,))] + [dma((SG - 1,))] * 2 + [dma((5,))] * 2,
         number,
         (rows, sum_in, sum_back),
     )
+
+
+def total_kernel(value, out, from_rep, half, from_shard, send_rep, recv_rep, send_shard, recv_shard):
+    rep, shard, _, _, _ = whereabouts()
+    shard_peers = [(rep, shard_peer(shard, step)) for step in range(1, SG)]
+    rep_peers = [(lax.rem(rep + step, RG), shard) for step in range(1, RG)]
+    greet(shard_peers + rep_peers)
+    copies = [
+        remote(value, from_rep.at[rep], send_rep.at[k], recv_rep.at[k], peer) for k, peer in enumerate(rep_peers)
+    ]
+    for copy in copies:
+        copy.start()
+    from_rep[rep] = value[...]
+    for copy in copies:
+        copy.wait()
+    half[...] = from_rep[0] + from_rep[1] + from_rep[2] + from_rep[3]
+    copies = [
+        remote(half, from_shard.at[shard], send_shard.at[k], recv_shard.at[k], peer)
+        for k, peer in enumerate(shard_peers)
+    ]
+    for copy in copies:
+        copy.start()
+    from_shard[shard] = half[...]
+    for copy in copies:
+        copy.wait()
+    total = from_shard[0]
+    for k in range(1, SG):
+        total = total + from_shard[k]
+    out[...] = total
+
+
+def total_everywhere(value, number):
+    dma = pltpu.SemaphoreType.DMA
+    return comm_call(
+        total_kernel,
+        [jax.ShapeDtypeStruct(value.shape, value.dtype)],
+        [pltpu.VMEM((RG,) + value.shape, value.dtype), pltpu.VMEM(value.shape, value.dtype), pltpu.VMEM((SG,) + value.shape, value.dtype)]
+        + [dma((RG - 1,))] * 2 + [dma((SG - 1,))] * 2,
+        number,
+        (value,),
+        "v",
+        "v",
+    )[0]
 
 
 GROUP_HEADS = H // SG
@@ -991,9 +1146,6 @@
 OWN_COLS = 3 * HEAD_COLS + UNITS
 VOCAB_BLOCK = 512
 TABLE_BLOCK = 4096
-EMBED_BLOCK = 2048
-EMBED_PART = 512
-TOKEN_CHUNK = 128
 VMEM_LIMIT = 60 << 20
 
 
@@ -1007,43 +1159,6 @@
 
 def plain_dot(left, right):
     return jnp.dot(left, right, preferred_element_type=jnp.float32)
-
-
-def table_kernel(ids, table, rows, turned, rows_wide):
-    at = pl.program_id(0)
-    block = table[...].astype(jnp.bfloat16).astype(jnp.float32)
-    width = block.shape[1]
-    turned[pl.ds(pl.multiple_of(at * width, width), width), :] = block.T
-
-    @pl.when(at == pl.num_programs(0) - 1)
-    def _():
-        @pl.loop(0, rows.shape[0] // 16)
-        def _(group):
-            for lane in range(16):
-                token = group * 16 + lane
-                rows_wide[pl.ds(token, 1), :] = turned[pl.ds(ids[token], 1), :]
-
-        rows[...] = rows_wide[...].astype(jnp.bfloat16)
-
-
-def embedding_rows(ids, table):
-    feats, vocab = table.shape
-    blocks = pl.cdiv(vocab, TABLE_BLOCK)
-    return pl.pallas_call(
-        table_kernel,
-        grid=(blocks,),
-        in_specs=[
-            pl.BlockSpec(memory_space=pltpu.SMEM),
-            pl.BlockSpec((feats, TABLE_BLOCK), lambda at: (0, at)),
-        ],
-        out_specs=pl.BlockSpec((ids.shape[0], feats), lambda at: (0, 0)),
-        out_shape=jax.ShapeDtypeStruct((ids.shape[0], feats), jnp.bfloat16),
-        scratch_shapes=[
-            pltpu.VMEM((blocks * TABLE_BLOCK, feats), jnp.float32),
-            pltpu.VMEM((ids.shape[0], feats), jnp.float32),
-        ],
-        compiler_params=pltpu.CompilerParams(vmem_limit_bytes=VMEM_LIMIT),
-    )(ids, table)
 
 
 def vocab_rows(vocab, block):
@@ -1116,13 +1231,19 @@
 
 
 def rows_kernel(vocab, rows, facts, targets, head, out):
-    @pl.when(pl.program_id(0) == 0)
+    at = pl.program_id(0)
+
+    @pl.when(at == 0)
     def _():
         out[...] = jnp.zeros_like(out)
 
     _, low = vocab_rows(vocab, head[...])
-    grads = logit_grads(vocab, low, rows[...], facts[0:1, :], targets[...], facts[1:2, :])
-    out[...] += first_dot(grads, low)
+    logits = transposed_dot(rows[...], low)
+    places = at * VOCAB_BLOCK + lax.broadcasted_iota(jnp.int32, logits.shape, 1)
+    hits = (places == targets[...]).astype(jnp.float32)
+    grads = (jnp.exp(logits - facts[:, 0:1]) - hits) * facts[:, 1:2]
+    grads = jnp.where(places < vocab, grads, 0.0).astype(jnp.bfloat16)
+    out[...] += plain_dot(grads, low)
 
 
 def picked_grads(rows, facts, targets, head):
@@ -1133,8 +1254,8 @@
         grid=(pl.cdiv(vocab, VOCAB_BLOCK),),
         in_specs=[
             pl.BlockSpec((count, depth), lambda at: (0, 0)),
-            pl.BlockSpec((8, count), lambda at: (0, 0)),
-            pl.BlockSpec((1, count), lambda at: (0, 0)),
+            pl.BlockSpec((count, 8), lambda at: (0, 0)),
+            pl.BlockSpec((count, 1), lambda at: (0, 0)),
             pl.BlockSpec((VOCAB_BLOCK, depth), lambda at: (at, 0)),
         ],
         out_specs=pl.BlockSpec((count, depth), lambda at: (0, 0)),
@@ -1143,97 +1264,55 @@
     )(rows, facts, targets, head)
 
 
-def head_kernel(vocab, rows, facts, targets, head, out, squares):
-    @pl.when(pl.program_id(0) == 0)
-    def _():
-        squares[...] = jnp.zeros_like(squares)
-
-    _, low = vocab_rows(vocab, head[...])
-    groups = rows.shape[0]
-    total = None
-    for group in range(groups):
-        grads = logit_grads(
-            vocab, low, rows[group], facts[group, 0:1, :], targets[group, 0:1, :], facts[group, 1:2, :]
-        )
-        term = plain_dot(grads, rows[group])
-        total = term if total is None else total + term
-    out[...] = total
-    squares[0:1, :] += jnp.sum(total * total, axis=0, keepdims=True)
-
-
-def head_grads(rows, facts, targets, head):
-    vocab, depth = head.shape
-    groups, count, _ = rows.shape
-    return pl.pallas_call(
-        functools.partial(head_kernel, vocab),
-        grid=(pl.cdiv(vocab, VOCAB_BLOCK),),
-        in_specs=[
-            pl.BlockSpec((groups, count, depth), lambda at: (0, 0, 0)),
-            pl.BlockSpec((groups, 8, count), lambda at: (0, 0, 0)),
-            pl.BlockSpec((groups, 8, count), lambda at: (0, 0, 0)),
-            pl.BlockSpec((VOCAB_BLOCK, depth), lambda at: (at, 0)),
-        ],
-        out_specs=[
-            pl.BlockSpec((VOCAB_BLOCK, depth), lambda at: (at, 0)),
-            pl.BlockSpec((8, depth), lambda at: (0, 0)),
-        ],
-        out_shape=[
-            jax.ShapeDtypeStruct(head.shape, jnp.float32),
-            jax.ShapeDtypeStruct((8, depth), jnp.float32),
-        ],
-        compiler_params=pltpu.CompilerParams(vmem_limit_bytes=VMEM_LIMIT),
-    )(rows, facts, targets, head)
-
-
-def embed_grad_kernel(starts, ids, rows, out, squares):
+def embed_grad_kernel(ids, rows, out, squares, table, wide):
     at = pl.program_id(0)
-    parts = EMBED_BLOCK // EMBED_PART
+    width = out.shape[1]
 
     @pl.when(at == 0)
     def _():
         squares[...] = jnp.zeros_like(squares)
-
-    for part in range(parts):
-        begin = starts[at * parts + part]
-        end = starts[at * parts + part + 1]
-        base = at * EMBED_BLOCK + part * EMBED_PART
-        places = base + lax.broadcasted_iota(jnp.int32, (TOKEN_CHUNK, EMBED_PART), 1)
-
-        def add(chunk, total):
-            here = pl.ds(pl.multiple_of(chunk * TOKEN_CHUNK, TOKEN_CHUNK), TOKEN_CHUNK)
-            hits = (ids[here, :] == places).astype(jnp.bfloat16)
-            return total + first_dot(rows[here, :], hits)
-
-        total = lax.fori_loop(
-            begin // TOKEN_CHUNK,
-            (end + TOKEN_CHUNK - 1) // TOKEN_CHUNK,
-            add,
-            jnp.zeros((rows.shape[1], EMBED_PART), jnp.float32),
-        )
-        out[:, part * EMBED_PART : (part + 1) * EMBED_PART] = total
-        squares[...] += total * total
-
-
-def embed_grads(starts, ids, rows, vocab):
+        wide[...] = rows[...].astype(jnp.float32)
+
+        @pl.loop(0, table.shape[0] // 512)
+        def _(part):
+            table[pl.ds(pl.multiple_of(part * 512, 512), 512), :] = jnp.zeros((512, table.shape[1]), jnp.float32)
+
+        @pl.loop(0, rows.shape[0] // 8)
+        def _(group):
+            for lane in range(8):
+                token = group * 8 + lane
+                here = pl.ds(ids[token], 1)
+                table[here, :] = table[here, :] + wide[pl.ds(token, 1), :]
+
+    block = table[pl.ds(pl.multiple_of(at * width, width), width), :]
+    out[...] = block.T
+    squares[...] += jnp.sum((block * block).reshape(width // 8, 8, block.shape[1]), axis=0)
+
+
+def embed_grads(ids, rows, vocab):
     count, feats = rows.shape
+    blocks = pl.cdiv(vocab, TABLE_BLOCK)
     return pl.pallas_call(
         embed_grad_kernel,
-        grid=(pl.cdiv(vocab, EMBED_BLOCK),),
+        grid=(blocks,),
         in_specs=[
             pl.BlockSpec(memory_space=pltpu.SMEM),
-            pl.BlockSpec((count, 1), lambda at: (0, 0)),
-            pl.BlockSpec((count, feats), lambda at: (0, 0)),
+            pl.BlockSpec(memory_space=pltpu.VMEM),
         ],
         out_specs=[
-            pl.BlockSpec((feats, EMBED_BLOCK), lambda at: (0, at)),
-            pl.BlockSpec((feats, EMBED_PART), lambda at: (0, 0)),
+            pl.BlockSpec((feats, TABLE_BLOCK), lambda at: (0, at)),
+            pl.BlockSpec((8, feats), lambda at: (0, 0)),
         ],
         out_shape=[
             jax.ShapeDtypeStruct((feats, vocab), jnp.float32),
-            jax.ShapeDtypeStruct((feats, EMBED_PART), jnp.float32),
+            jax.ShapeDtypeStruct((8, feats), jnp.float32),
+        ],
+        scratch_shapes=[
+            pltpu.VMEM((blocks * TABLE_BLOCK, feats), jnp.float32),
+            pltpu.VMEM((count, feats), jnp.float32),
         ],
         compiler_params=pltpu.CompilerParams(vmem_limit_bytes=VMEM_LIMIT),
-    )(starts, ids, rows)
+    )(ids, rows)
 
 
 def turn_tables(places):
@@ -1250,21 +1329,262 @@
     )
 
 
-def turn(rows, tables, sign):
-    half_rot = ROT // 2
-    own, after, before = tables
-    return (
-        rows * own
-        + sign * jnp.roll(rows, -half_rot, axis=-1) * after
-        + sign * jnp.roll(rows, half_rot, axis=-1) * before
-    )
-
-
 def centred_rows(values):
     centred = values - jnp.mean(values, axis=-1, keepdims=True)
     spread = jnp.mean(centred * centred, axis=-1, keepdims=True)
     scale = lax.rsqrt(spread + NORM_EPS)
     return centred * scale, scale
+
+
+def exact_dot(left, right):
+    return jnp.dot(left, right, precision=lax.Precision.HIGHEST, preferred_element_type=jnp.float32)
+
+
+def pick_matrix(places, tokens):
+    lane = lax.broadcasted_iota(jnp.int32, (places.shape[0], tokens), 1)
+    return (places == lane).astype(jnp.float32)
+
+
+def turn(rows, tables, sign):
+    half_rot = ROT // 2
+    own, after, before = tables
+    width = rows.shape[1]
+    return (
+        rows * own
+        + sign * (pltpu.roll(rows, width - half_rot, 1) * after)
+        + sign * (pltpu.roll(rows, half_rot, 1) * before)
+    )
+
+
+def head_lanes(rows, head):
+    lane = lax.broadcasted_iota(jnp.int32, rows.shape, 1)
+    return jnp.where(lane // HD == head, rows, jnp.zeros_like(rows))
+
+
+def head_probs(queries, keys, allowed, head):
+    scores = transposed_dot(head_lanes(queries, head), keys) * HD ** (-0.5)
+    scores = jnp.where(allowed, scores, -1e30)
+    exponent = jnp.exp(scores - jnp.max(scores, axis=-1, keepdims=True))
+    return exponent / jnp.sum(exponent, axis=-1, keepdims=True)
+
+
+def line_allowed(places, span, tokens):
+    keys = lax.broadcasted_iota(jnp.int32, (places.shape[0], tokens), 1)
+    in_query = (places >= span) & (places < span + PIC)
+    in_key = (keys >= span) & (keys < span + PIC)
+    return (keys <= places) | (in_query & in_key)
+
+
+def forward_kernel(
+    spans, residual, places, scales, bias, own, after, before, weights, back,
+    queries, keys, values, hidden, joined, picked_one, picked_two, picked_rows, branch,
+):
+    bf16 = jnp.bfloat16
+    tokens = residual.shape[0]
+    span = spans[pl.program_id(0)]
+    gain_one, shift_one = scales[0:1, :], scales[1:2, :]
+    gain_two, shift_two = scales[2:3, :], scales[3:4, :]
+    unit, _ = centred_rows(residual[...].astype(jnp.float32))
+    low_one = (unit * gain_one + shift_one).astype(bf16)
+    pick = pick_matrix(places[...], tokens)
+    rows = plain_dot(pick.astype(bf16), residual[...])
+    picked_rows[...] = rows.astype(bf16)
+    unit, _ = centred_rows(rows)
+    low_picked = (unit * gain_one + shift_one).astype(bf16)
+    picked_one[...] = low_picked
+    low_two = (unit * gain_two + shift_two).astype(bf16)
+    picked_two[...] = low_two
+    tables = (own[...], after[...], before[...])
+    picked_tables = tuple(exact_dot(pick, table) for table in tables)
+    two, three = 2 * HEAD_COLS, 3 * HEAD_COLS
+    query = plain_dot(low_picked, weights[:, :HEAD_COLS]) + bias[:, :HEAD_COLS]
+    query = turn(query, picked_tables, 1.0).astype(bf16)
+    queries[...] = query
+    key = plain_dot(low_one, weights[:, HEAD_COLS:two]) + bias[:, HEAD_COLS:two]
+    key = turn(key, tables, 1.0).astype(bf16)
+    keys[...] = key
+    value = (plain_dot(low_one, weights[:, two:three]) + bias[:, two:three]).astype(bf16)
+    values[...] = value
+    allowed = line_allowed(places[...], span, tokens)
+    attended = None
+    for head in range(GROUP_HEADS):
+        probs = head_probs(query, key, allowed, head).astype(bf16)
+        term = head_lanes(plain_dot(probs, value), head)
+        attended = term if attended is None else attended + term
+    joined[:, :HEAD_COLS] = attended.astype(bf16)
+    pre = plain_dot(low_two, weights[:, three:]) + bias[:, three:]
+    hidden[...] = pre
+    joined[:, HEAD_COLS:] = (0.5 * pre * (1.0 + lax.erf(pre * 0.5**0.5))).astype(bf16)
+    branch[...] = plain_dot(joined[...], back[...])
+
+
+def line_block(height, width):
+    return pl.BlockSpec((height, width), lambda line: (line, 0))
+
+
+def still(array):
+    return pl.BlockSpec(array.shape, lambda line: (0,) * array.ndim)
+
+
+def layer_forward(spans, residual, places, scales, bias, tables, weights, back):
+    lines = spans.shape[0]
+    tokens, slots = residual.shape[0] // lines, places.shape[0] // lines
+    depth = residual.shape[1]
+    bf16, f32 = jnp.bfloat16, jnp.float32
+    outs = [
+        (slots, HEAD_COLS, bf16),
+        (tokens, HEAD_COLS, bf16),
+        (tokens, HEAD_COLS, bf16),
+        (slots, UNITS, f32),
+        (slots, HEAD_COLS + UNITS, bf16),
+        (slots, depth, bf16),
+        (slots, depth, bf16),
+        (slots, depth, bf16),
+        (slots, depth, f32),
+    ]
+    return pl.pallas_call(
+        forward_kernel,
+        grid=(lines,),
+        in_specs=[
+            pl.BlockSpec(memory_space=pltpu.SMEM),
+            line_block(tokens, depth),
+            line_block(slots, 1),
+            still(scales),
+            still(bias),
+            *[still(table) for table in tables],
+            still(weights),
+            still(back),
+        ],
+        out_specs=[line_block(height, width) for height, width, _ in outs],
+        out_shape=[jax.ShapeDtypeStruct((lines * height, width), kind) for height, width, kind in outs],
+        compiler_params=pltpu.CompilerParams(vmem_limit_bytes=VMEM_LIMIT),
+    )(spans, residual, places, scales, bias, *tables, weights, back)
+
+
+def backward_kernel(
+    spans, residual, places, scales, own, after, before, weights, back,
+    queries, keys, values, hidden, joined, picked_one, picked_two, d_branch,
+    unit_parts, stats, grad_in, grad_back, grad_scales, grad_bias,
+):
+    bf16 = jnp.bfloat16
+    line = pl.program_id(0)
+    tokens = residual.shape[0]
+    span = spans[line]
+    gain_one, shift_one = scales[0:1, :], scales[1:2, :]
+    gain_two = scales[2:3, :]
+
+    @pl.when(line == 0)
+    def _():
+        for total in (grad_in, grad_back, grad_scales, grad_bias):
+            total[...] = jnp.zeros_like(total)
+
+    pick = pick_matrix(places[...], tokens)
+    tables = (own[...], after[...], before[...])
+    picked_tables = tuple(exact_dot(pick, table) for table in tables)
+    pick = pick.astype(bf16)
+    d_rows = d_branch[...]
+    d_joined = transposed_dot(d_rows, back[...])
+    grad_back[...] += first_dot(joined[...], d_rows)
+    d_attended = d_joined[:, :HEAD_COLS].astype(bf16)
+    pre = hidden[...]
+    slope = 0.5 * (1.0 + lax.erf(pre * 0.5**0.5)) + pre * jnp.exp(-0.5 * pre * pre) * (2.0 * 3.141592653589793) ** -0.5
+    d_hidden = (d_joined[:, HEAD_COLS:] * slope).astype(bf16)
+    allowed = line_allowed(places[...], span, tokens)
+    query, key, value = queries[...], keys[...], values[...]
+    d_query = d_key = d_value = None
+    for head in range(GROUP_HEADS):
+        probs = head_probs(query, key, allowed, head)
+        d_head = head_lanes(d_attended, head)
+        d_probs = transposed_dot(d_head, value)
+        d_scores = (probs * (d_probs - jnp.sum(probs * d_probs, axis=-1, keepdims=True))).astype(bf16)
+        terms = (
+            head_lanes(plain_dot(d_scores, key), head),
+            first_dot(d_scores, head_lanes(query, head)),
+            first_dot(probs.astype(bf16), d_head),
+        )
+        if d_query is None:
+            d_query, d_key, d_value = terms
+        else:
+            d_query, d_key, d_value = d_query + terms[0], d_key + terms[1], d_value + terms[2]
+    d_query = turn(d_query * HD ** (-0.5), picked_tables, -1.0).astype(bf16)
+    d_key = turn(d_key * HD ** (-0.5), tables, -1.0).astype(bf16)
+    d_value = d_value.astype(bf16)
+    unit, _ = centred_rows(residual[...].astype(jnp.float32))
+    low_one = (unit * gain_one + shift_one).astype(bf16)
+    two, three = 2 * HEAD_COLS, 3 * HEAD_COLS
+    grad_in[:, :HEAD_COLS] += first_dot(picked_one[...], d_query)
+    grad_in[:, HEAD_COLS:two] += first_dot(low_one, d_key)
+    grad_in[:, two:three] += first_dot(low_one, d_value)
+    grad_in[:, three:] += first_dot(picked_two[...], d_hidden)
+
+    def column_sum(rows):
+        return jnp.sum(rows.astype(jnp.float32), axis=0, keepdims=True)
+
+    grad_bias[0:1, :HEAD_COLS] += column_sum(d_query)
+    grad_bias[0:1, HEAD_COLS:two] += column_sum(d_key)
+    grad_bias[0:1, two:three] += column_sum(d_value)
+    grad_bias[0:1, three:] += column_sum(d_hidden)
+    d_normed = (
+        transposed_dot(first_dot(pick, d_query).astype(bf16), weights[:, :HEAD_COLS])
+        + transposed_dot(d_key, weights[:, HEAD_COLS:two])
+        + transposed_dot(d_value, weights[:, two:three])
+    )
+    d_unit = d_normed * gain_one
+    grad_scales[0:1, :] += column_sum(d_normed * unit)
+    grad_scales[1:2, :] += column_sum(d_normed)
+    d_normed = transposed_dot(first_dot(pick, d_hidden).astype(bf16), weights[:, three:])
+    grad_scales[2:3, :] += column_sum(d_normed * unit)
+    grad_scales[3:4, :] += column_sum(d_normed)
+    d_unit = d_unit + d_normed * gain_two
+    sum_one = jnp.sum(d_unit, axis=-1, keepdims=True)
+    sum_two = jnp.sum(d_unit * unit, axis=-1, keepdims=True)
+    lane = lax.broadcasted_iota(jnp.int32, (tokens, 128), 1)
+    both = jnp.where(lane == 0, sum_one, jnp.where(lane == 1, sum_two, 0.0))
+    stats[...] = both.T[:8, :]
+    feats = unit_parts.shape[2]
+    for part in range(unit_parts.shape[0]):
+        unit_parts[part] = d_unit[:, part * feats : (part + 1) * feats]
+
+
+def layer_backward(spans, residual, places, scales, tables, weights, back, kept, d_branch):
+    lines = spans.shape[0]
+    count, depth = residual.shape
+    tokens, slots = count // lines, places.shape[0] // lines
+    feats = depth // SG
+    f32 = jnp.float32
+    whole = lambda height, width: pl.BlockSpec((height, width), lambda line: (0, 0))
+    return pl.pallas_call(
+        backward_kernel,
+        grid=(lines,),
+        in_specs=[
+            pl.BlockSpec(memory_space=pltpu.SMEM),
+            line_block(tokens, depth),
+            line_block(slots, 1),
+            still(scales),
+            *[still(table) for table in tables],
+            still(weights),
+            still(back),
+            *[line_block(array.shape[0] // lines, array.shape[1]) for array in kept],
+            line_block(slots, depth),
+        ],
+        out_specs=[
+            pl.BlockSpec((SG, tokens, feats), lambda line: (0, line, 0)),
+            pl.BlockSpec((8, tokens), lambda line: (0, line)),
+            whole(depth, OWN_COLS),
+            whole(HEAD_COLS + UNITS, depth),
+            whole(8, depth),
+            whole(8, OWN_COLS),
+        ],
+        out_shape=[
+            jax.ShapeDtypeStruct((SG, count, feats), f32),
+            jax.ShapeDtypeStruct((8, count), f32),
+            jax.ShapeDtypeStruct((depth, OWN_COLS), f32),
+            jax.ShapeDtypeStruct((HEAD_COLS + UNITS, depth), f32),
+            jax.ShapeDtypeStruct((8, depth), f32),
+            jax.ShapeDtypeStruct((8, OWN_COLS), f32),
+        ],
+        compiler_params=pltpu.CompilerParams(vmem_limit_bytes=VMEM_LIMIT),
+    )(spans, residual, places, scales, *tables, weights, back, *kept, d_branch)
 
 
 def group_plan(
@@ -1312,7 +1632,21 @@
     small_low = small_params.astype(bf16).astype(jnp.float32).reshape(-1, 128)
     small_rows = small_low.shape[0]
     smalls = jnp.pad(small_low, ((0, 16 - small_rows), (0, 0)))
-    ints_all, smalls_all = share_facts(ints, smalls, 1)
+    in_low = proj_in.astype(bf16)
+    qkv_parts = in_low[:, : 3 * D].reshape(D // SG, 3, SG, HEAD_COLS)
+    in_parts = jnp.concatenate(
+        [
+            jnp.transpose(qkv_parts, (2, 0, 1, 3)).reshape(SG, D // SG, 3 * HEAD_COLS),
+            jnp.transpose(in_low[:, 3 * D :].reshape(D // SG, SG, UNITS), (1, 0, 2)),
+        ],
+        axis=2,
+    ).reshape(SG, 2, D // SG // 2, OWN_COLS)
+    back_tiles = proj_back.astype(bf16).reshape(5, 2, 64, D)
+    ints_all, smalls_all, residual_low, in_all, back_all = share_entry(
+        ints, smalls, in_parts, back_tiles, embed_table, tokens, 1
+    )
+    own_in = in_all.reshape(D, OWN_COLS)
+    own_back = back_all.reshape(5 * 128, D)
     wide_small = smalls_all[:, :small_rows].reshape(-1)
     (
         gain_one,
@@ -1338,95 +1672,23 @@
     used_all = slot_facts[0] < seq_dev
     targets_all = jnp.where(used_all, slot_facts[1] - shard_at * vocab_dev, -1)
     counted_all = used_all.astype(jnp.float32)
-    ids_group = lax.dynamic_index_in_dim(ids_all, rep_at, 0, False)
     pos_group = lax.dynamic_index_in_dim(slot_facts[0], rep_at, 0, False)
     targets_group = lax.dynamic_index_in_dim(targets_all, rep_at, 0, False)
     counted_group = lax.dynamic_index_in_dim(counted_all, rep_at, 0, False)
     spans = lax.dynamic_index_in_dim(by_group[0, :, :, 3, :micro], rep_at, 0, False).T.reshape(lines)
 
-    flat_ids = ids_all.reshape(-1)
-    sorted_ids, order = lax.sort((flat_ids, jnp.arange(flat_ids.shape[0], dtype=jnp.int32)), num_keys=1)
-    edges = jnp.arange(pl.cdiv(vocab, EMBED_BLOCK) * (EMBED_BLOCK // EMBED_PART) + 1) * EMBED_PART
-    starts = jnp.sum((flat_ids[None, :] < edges[:, None]).astype(jnp.int32), axis=1)
-
-    rows = embedding_rows(ids_group, embed_table)
-    in_low = proj_in.astype(bf16)
-    qkv_parts = in_low[:, : 3 * D].reshape(D // SG, 3, SG, HEAD_COLS)
-    in_parts = jnp.concatenate(
-        [
-            jnp.transpose(qkv_parts, (2, 0, 1, 3)).reshape(SG, D // SG, 3 * HEAD_COLS),
-            jnp.transpose(in_low[:, 3 * D :].reshape(D // SG, SG, UNITS), (1, 0, 2)),
-        ],
-        axis=2,
-    ).reshape(SG, 2, D // SG // 2, OWN_COLS)
-    back_tiles = proj_back.astype(bf16).reshape(5, 2, 64, D)
-    residual_low, in_all, back_all = share_embedding(rows, in_parts, back_tiles, 2)
-    own_in = in_all.reshape(D, OWN_COLS)
-    own_back = back_all.reshape(5 * 128, D)
-
-    residual = residual_low.astype(jnp.float32)
-    unit_rows, unit_scale = centred_rows(residual)
-    low_one = (unit_rows * gain_one + shift_one).astype(bf16)
-    low_two = (unit_rows * gain_two + shift_two).astype(bf16)
-    pick = (pos_group.reshape(blocks, slots, 1) == jnp.arange(seq_dev)[None, None, :]).astype(bf16)
-
-    def pick_rows(values):
-        blocked = values.reshape(blocks, seq_dev, values.shape[1])
-        return jnp.einsum("bst,btd->bsd", pick, blocked, preferred_element_type=jnp.float32).reshape(
-            slot_count, values.shape[1]
-        )
-
-    def put_rows(values):
-        blocked = values.reshape(blocks, slots, values.shape[1])
-        return jnp.einsum("bst,bsd->btd", pick, blocked, preferred_element_type=jnp.float32).reshape(
-            tokens, values.shape[1]
-        )
-
-    picked_one = pick_rows(low_one).astype(bf16)
-    picked_two = pick_rows(low_two).astype(bf16)
-    slot_places = (
-        (jnp.arange(blocks) % RG * seq_dev)[:, None] + jnp.minimum(pos_group.reshape(blocks, slots), seq_dev - 1)
-    ).reshape(-1)
-    key_places = jnp.arange(seq_len)
-    query_turn = turn_tables(slot_places.astype(jnp.float32))
-    key_turn = turn_tables(key_places.astype(jnp.float32))
-    key_turn = tuple(jnp.tile(table, (lines, 1)) for table in key_turn)
-    queries = turn(plain_dot(picked_one, own_in[:, :HEAD_COLS]) + head_cols[0], query_turn, 1.0).astype(bf16)
-    key_values = plain_dot(low_one, own_in[:, HEAD_COLS : 3 * HEAD_COLS])
-    keys = turn(key_values[:, :HEAD_COLS] + head_cols[1], key_turn, 1.0).astype(bf16)
-    values = (key_values[:, HEAD_COLS:] + head_cols[2]).astype(bf16)
-    line_slots = slot_count // lines
-    queries = queries.reshape(lines, line_slots, GROUP_HEADS, HD)
-    keys = keys.reshape(lines, seq_len, GROUP_HEADS, HD)
-    values = values.reshape(lines, seq_len, GROUP_HEADS, HD)
-    query_at = slot_places.reshape(lines, line_slots, 1)
-    key_at = key_places[None, None, :]
-    span_at = spans.reshape(lines, 1, 1)
-    in_query = (query_at >= span_at) & (query_at < span_at + PIC)
-    in_key = (key_at >= span_at) & (key_at < span_at + PIC)
-    allowed = ((key_at <= query_at) | (in_query & in_key))[:, None]
-    scores = jnp.einsum("nqhd,nkhd->nhqk", queries, keys, preferred_element_type=jnp.float32) * HD ** (-0.5)
-    scores = jnp.where(allowed, scores, -1e30)
-    highest = jnp.max(scores, axis=-1, keepdims=True)
-    exponent = jnp.exp(scores - highest)
-    probs = exponent / jnp.sum(exponent, axis=-1, keepdims=True)
-    low_probs = probs.astype(bf16)
-    attended = (
-        jnp.einsum("nhqk,nkhd->nqhd", low_probs, values, preferred_element_type=jnp.float32)
-        .reshape(slot_count, HEAD_COLS)
-        .astype(bf16)
-    )
-    hidden_pre = plain_dot(picked_two, own_in[:, 3 * HEAD_COLS :]) + own_hidden
-    activation = gelu_exact(hidden_pre).astype(bf16)
-    joined = jnp.concatenate([attended, activation], axis=1)
-    branch_parts = plain_dot(joined, own_back).reshape(SG, own_slots, D)
-    branch = shard_sum(branch_parts, 3)
-
-    own_pick = lax.dynamic_slice_in_dim(pick, shard_at * own_blocks, own_blocks, 0)
-    own_residual = lax.dynamic_slice_in_dim(residual_low, shard_at * own_blocks * seq_dev, own_blocks * seq_dev, 0)
-    own_residual = jnp.einsum(
-        "bst,btd->bsd", own_pick, own_residual.reshape(own_blocks, seq_dev, D), preferred_element_type=jnp.float32
-    ).reshape(own_slots, D)
+    block_starts = (jnp.arange(blocks) % RG * seq_dev)[:, None]
+    slot_places = pos_group.reshape(blocks, slots)
+    slot_places = jnp.where(slot_places < seq_dev, slot_places + block_starts, -1).reshape(slot_count, 1)
+    tables = turn_tables(jnp.arange(seq_len).astype(jnp.float32))
+    scales = jnp.stack([gain_one, shift_one, gain_two, shift_two] + [jnp.zeros_like(gain_one)] * 4)
+    own_bias = jnp.concatenate(head_cols + [own_hidden])[None]
+    *kept, picked_rows, branch_parts = layer_forward(
+        spans, residual_low, slot_places, scales, own_bias, tables, own_in, own_back
+    )
+    branch = shard_sum(branch_parts.reshape(SG, own_slots, D), 3)
+
+    own_residual = lax.dynamic_slice_in_dim(picked_rows, shard_at * own_slots, own_slots, 0).astype(jnp.float32)
     own_used = lax.dynamic_slice_in_dim(counted_group, shard_at * own_slots, own_slots, 0)
     after_add = own_residual + branch + bias_out
     final_rows, pull_last = jax.vjp(norm_rows, after_add, gain_last, shift_last)
@@ -1443,14 +1705,13 @@
     facts = jnp.concatenate(
         [logsum[None], counted_group[None], row_target[None], jnp.zeros((5, slot_count), jnp.float32)]
     )
-    picked_parts = picked_grads(rows_group, facts, targets_group[None], head_low)
+    picked_parts = picked_grads(rows_group, facts.T, targets_group[:, None], head_low)
     d_picked, rows_all, facts_all = sum_and_share(
         picked_parts.reshape(SG, own_slots, D), rows_group, facts, 6
     )
     loss_sum = jnp.sum((facts_all[:, 0] - facts_all[:, 2]) * facts_all[:, 1])
     count_sum = jnp.sum(facts_all[:, 1])
     targets_wide = jnp.broadcast_to(targets_all[:, None, :], (RG, 8, slot_count))
-    grad_head, head_squares = head_grads(rows_all, facts_all, targets_wide, head_low)
 
     d_after, d_gain_last, d_shift_last = pull_last(d_picked)
     d_branch_own = d_after.astype(bf16)
@@ -1459,78 +1720,53 @@
     d_branch, after_pieces = share_branch(d_branch_own, pieces, 7)
     d_after_feats = after_pieces.reshape(slot_count, D // SG)
 
-    d_joined = transposed_dot(d_branch, own_back)
-    grad_back = first_dot(joined, d_branch)
-    d_attended = d_joined[:, :HEAD_COLS].astype(bf16).reshape(lines, line_slots, GROUP_HEADS, HD)
-    _, pull_gelu = jax.vjp(gelu_exact, hidden_pre)
-    d_hidden = pull_gelu(d_joined[:, HEAD_COLS:])[0].astype(bf16)
-    d_probs = jnp.einsum("nqhd,nkhd->nhqk", d_attended, values, preferred_element_type=jnp.float32)
-    d_scores = (probs * (d_probs - jnp.sum(probs * d_probs, axis=-1, keepdims=True))).astype(bf16)
-    d_queries = jnp.einsum("nhqk,nkhd->nqhd", d_scores, keys, preferred_element_type=jnp.float32) * HD ** (-0.5)
-    d_keys = jnp.einsum("nhqk,nqhd->nkhd", d_scores, queries, preferred_element_type=jnp.float32) * HD ** (-0.5)
-    d_values = jnp.einsum("nhqk,nqhd->nkhd", low_probs, d_attended, preferred_element_type=jnp.float32)
-    d_query_rows = turn(d_queries.reshape(slot_count, HEAD_COLS), query_turn, -1.0).astype(bf16)
-    d_key_rows = turn(d_keys.reshape(tokens, HEAD_COLS), key_turn, -1.0).astype(bf16)
-    d_key_values = jnp.concatenate([d_key_rows, d_values.reshape(tokens, HEAD_COLS).astype(bf16)], axis=1)
-    grad_in = jnp.concatenate(
-        [first_dot(picked_one, d_query_rows), first_dot(low_one, d_key_values), first_dot(picked_two, d_hidden)],
-        axis=1,
-    )
-    d_projected = jnp.concatenate([put_rows(d_query_rows).astype(bf16), d_key_values], axis=1)
-    d_hidden_rows = put_rows(d_hidden).astype(bf16)
-    d_normed_one = transposed_dot(d_projected, own_in[:, : 3 * HEAD_COLS])
-    d_normed_two = transposed_dot(d_hidden_rows, own_in[:, 3 * HEAD_COLS :])
-    d_unit = d_normed_one * gain_one + d_normed_two * gain_two
-    norm_stats = jnp.stack([jnp.sum(d_unit, axis=1), jnp.sum(d_unit * unit_rows, axis=1)])
-    norm_stats = jnp.pad(norm_stats, ((0, 6), (0, 0)))
-    unit_parts = jnp.transpose(d_unit.reshape(tokens, SG, D // SG), (1, 0, 2))
+    unit_parts, norm_stats, grad_in, grad_back, grad_scales, grad_bias = layer_backward(
+        spans, residual_low, slot_places, scales, tables, own_in, own_back, kept, d_branch
+    )
 
     def whole(columns, length):
         start = shard_at * columns.shape[0]
         return lax.dynamic_update_slice(jnp.zeros((length,), jnp.float32), columns, (start,))
 
-    d_bias_parts = [
-        jnp.sum(d_query_rows.astype(jnp.float32), axis=0),
-        jnp.sum(d_key_rows.astype(jnp.float32), axis=0),
-        jnp.sum(d_key_values[:, HEAD_COLS:].astype(jnp.float32), axis=0),
-    ]
     grad_small = jnp.concatenate(
         [
-            jnp.sum(d_normed_one * unit_rows, axis=0),
-            jnp.sum(d_normed_one, axis=0),
-            jnp.sum(d_normed_two * unit_rows, axis=0),
-            jnp.sum(d_normed_two, axis=0),
+            grad_scales[:4].reshape(-1),
             d_gain_last,
             d_shift_last,
-            *[whole(part, D) for part in d_bias_parts],
-            whole(jnp.sum(d_hidden.astype(jnp.float32), axis=0), FF),
+            *[whole(grad_bias[0, part * HEAD_COLS : (part + 1) * HEAD_COLS], D) for part in range(3)],
+            whole(grad_bias[0, 3 * HEAD_COLS :], FF),
             d_bias_out,
         ]
     )
     grad_small = jnp.pad(grad_small.reshape(SG, small_rows, 128), ((0, 0), (0, 16 - small_rows), (0, 0)))
     in_quarters = jnp.transpose(grad_in.reshape(SG, RG, quarter, OWN_COLS), (1, 0, 2, 3))
     back_quarters = jnp.transpose(grad_back.reshape(5, RG, 32, D), (1, 0, 2, 3))
-    d_unit_feats, norm_stats_all, in_sum, back_sum, small_sum = layer_sums(
-        unit_parts, norm_stats, in_quarters, back_quarters, grad_small, 8
+    d_unit_feats, norm_stats_all, in_sum, back_sum, small_sum, grad_head, head_squares = layer_sums(
+        unit_parts, norm_stats, in_quarters, back_quarters, grad_small, rows_all, facts_all, targets_wide, head_low, 8
     )
 
     norm_sums = jnp.sum(norm_stats_all, axis=0)
+    residual = residual_low.astype(jnp.float32)
+    row_mean = jnp.mean(residual, axis=-1, keepdims=True)
+    centred = residual - row_mean
+    unit_scale = lax.rsqrt(jnp.mean(centred * centred, axis=-1, keepdims=True) + NORM_EPS)
     own_unit = lax.dynamic_slice_in_dim(residual_low, shard_at * (D // SG), D // SG, 1).astype(jnp.float32)
-    row_mean = jnp.mean(residual, axis=-1, keepdims=True)
     own_unit = (own_unit - row_mean) * unit_scale
     d_rows = (
         d_unit_feats - norm_sums[0][:, None] / D - own_unit * (norm_sums[1][:, None] / D)
     ) * unit_scale
+    pick = (pos_group.reshape(blocks, slots, 1) == jnp.arange(seq_dev)[None, None, :]).astype(jnp.float32)
     d_after_rows = jnp.einsum(
         "bst,bsd->btd",
-        pick.astype(jnp.float32),
+        pick,
         d_after_feats.reshape(blocks, slots, D // SG),
         precision=lax.Precision.HIGHEST,
     ).reshape(tokens, D // SG)
     d_rows = (d_after_rows + d_rows).astype(bf16)
-    d_rows_all, in_grads, back_grads = return_sums(d_rows, in_sum, back_sum, 9)
-    d_sorted = jnp.take(d_rows_all.reshape(RG * tokens, D // SG), order, axis=0)
-    grad_embed, embed_squares = embed_grads(starts, sorted_ids[:, None], d_sorted, vocab)
+    d_rows_all, in_own, back_own = return_sums(d_rows, in_sum, back_sum, 9)
+    in_grads = lax.all_gather(in_own, "rep")
+    back_grads = lax.all_gather(back_own, "rep")
+    grad_embed, embed_squares = embed_grads(ids_all.reshape(-1), d_rows_all.reshape(RG * tokens, D // SG), vocab)
 
     in_grads = jnp.transpose(in_grads, (0, 2, 1, 3)).reshape(D // SG, SG, OWN_COLS)
     qkv_grads = jnp.transpose(
@@ -1540,15 +1776,9 @@
     grad_back = jnp.transpose(back_grads, (1, 0, 2, 3)).reshape(proj_back.shape)
     grad_small = small_sum[:small_rows].reshape(-1)
 
-    local_square = (
-        jnp.sum(grad_in * grad_in)
-        + jnp.sum(grad_back * grad_back)
-        + jnp.sum(grad_small * grad_small)
-        + jnp.sum(head_squares)
-        + jnp.sum(embed_squares)
-    )
-    squares_all = shard_stats(jnp.broadcast_to(local_square, (8, 128)), 10)
-    norm_value = jnp.sqrt(jnp.sum(squares_all[:, 0, 0]))
+    repeated_square = jnp.sum(grad_small * grad_small) + jnp.sum(head_squares) + jnp.sum(embed_squares)
+    local_square = repeated_square / RG + jnp.sum(in_own * in_own) + jnp.sum(back_own * back_own)
+    norm_value = jnp.sqrt(total_everywhere(jnp.broadcast_to(local_square, (8, 128)), 10)[0, 0])
     factor = CLIP_LEVEL / jnp.maximum(norm_value, CLIP_LEVEL)
     next_in, moment_in, square_in = adamw(proj_in, grad_in * factor, first_in, second_in, RATE_IN)
     next_back, moment_back, square_back = adamw(

time: 1070 us -> 792 us (0.74)
  local copies, waits for them, and re-layouts: 149 us -> 47.5 us
  Pallas kernels: 622 us -> 541 us
  other arithmetic: 227 us -> 171 us
  matrix products: 56.6 us -> 1.1 us
  between operations: 7.49 us -> 20 us
    pallas_call x13 -> x12, Pallas kernels: 576 us -> 498 us  [the longest x9 406 us: comm_call(): pl.pallas_call(kernel, grid=grid, out_shape=out_shape, in_specs=[choose(s...]
    dot_general x22 -> x1, matrix products: 53.4 us -> 1.1 us  [group_plan(): jnp.einsum('bst,bsd->btd', pick, d_after_feats.reshape(blocks, slots, D /...]
    gather x1 -> x0, local copies, waits for them, and re-layouts: 29.5 us -> none  [group_plan(): d_sorted = jnp.take(d_rows_all.reshape(RG * tokens, D // SG), order, axis=0)]
    reduce_sum x11 -> x5, other arithmetic: 30.5 us -> 10.3 us  [the longest x1 2.98 us: group_plan(): jnp.mean(centred * centred, axis=-1, keepdims=True) + NORM_EPS]
    dot_general x2 -> x0, local copies, waits for them, and re-layouts: 18.5 us -> none  [transposed_dot(): lax.dot_general(left, right, (((1,), (1,)), ((), ())), preferred_element_...]
    unnamed x200 -> x62, local copies, waits for them, and re-layouts: 28 us -> 13.8 us
    concatenate x5 -> x1, local copies, waits for them, and re-layouts: 12.4 us -> 0.01 us  [group_plan(): jnp.concatenate([grad_scales[:4].reshape(-1), d_gain_last, d_shift_last,...]
    reshape x8 -> x2, local copies, waits for them, and re-layouts: 12.3 us -> 0.74 us  [the longest x1 0.59 us: group_plan(): lax.dynamic_index_in_dim(by_group[0, :, :, 3, :micro], rep_at, 0, False)]
  transfers between devices with their start and end apart: 0 -> 2, of which waited for: 0 -> 0; matrix products, arithmetic and copies ran while one was open for 0% -> 18% of each run, Pallas kernels for 0% -> 8%
where the time goes in v2:
time: 792 us; the launch traced here: 781 us
  Pallas kernels  541 us (68%)
  other arithmetic  171 us (22%)
  local copies, waits for them, and re-layouts  47.5 us (6%)
  between operations  20 us (3%)
    pallas_call x9, Pallas kernels, comm_call(): pl.pallas_call(kernel, grid=grid, out_shape=out_shape, in_specs=[choose(s...  406 us
    sub x5, other arithmetic, adamw(): weight - rate_value * (moment_hat / (jnp.sqrt(square_hat) + ADAM_EPS) + D...  133 us
    pallas_call x1, Pallas kernels, embed_grads(): pl.pallas_call(embed_grad_kernel, grid=(blocks,), in_specs=[pl.BlockSpec(...  42.3 us
    pallas_call x1, Pallas kernels, layer_backward(): pl.pallas_call(backward_kernel, grid=(lines,), in_specs=[pl.BlockSpec(mem...  32.1 us
    pallas_call x1, Pallas kernels, logit_stats(): pl.pallas_call(functools.partial(top_kernel, vocab), grid=(pl.cdiv(vocab,...  22.3 us
    pallas_call x1, Pallas kernels, picked_grads(): pl.pallas_call(functools.partial(rows_kernel, vocab), grid=(pl.cdiv(vocab...  21.4 us
    pallas_call x1, Pallas kernels, layer_forward(): pl.pallas_call(forward_kernel, grid=(lines,), in_specs=[pl.BlockSpec(memo...  17.6 us
  transfers between devices with their start and end apart: 2, of which 0 were waited for; matrix products, arithmetic and copies ran while one was open for 18% of the time, Pallas kernels for 8%

profile of v2, /device:TPU:0, one launch (start us, length us, event | category | flops | bytes accessed | tf_op | source)
XLA Modules:
  0.0 781.5 jit_solution(7755406962049673486)
XLA Ops:
  7.3 2.3 convert_element_type.74
  12.9 1.4 copy.152
  14.3 2.5 concatenate.32
  16.7 1.3 copy.151
  18.1 1.3 convert_element_type.75
  20.0 1.5 pad_maximum_fusion.in_parts
  22.2 100.4 %shard_map.314 = (s32[4,8,8,128]{3,2,1,0:T(8,128)}, f32[8,16,128]{2,1,0:T(8,128)}, bf16[2048,1024]{1,0:T(8,128)(2,1)}, bf16[8,2,64,896]{3,2,1,0:T(8,128)(2,1)}, bf16[5,2,64,1024]{3,2,1,0:T(8,128)(2,1)}) custom-call(s32[8,128]{1,0:T(8,128)} %add_add_fusion.2.ints, f32[16,128]{1,0:T(8,128)} %pad_convert_fusion.smalls, ...), custom_call_target="tpu_custom_call" | custom-call | tf_op jit(solution)/shard_map/pallas_call | solution.py:436
  128.3 2.8 convert_reduce_fusion
  132.4 1.9 fusion.9
  134.3 17.6 %shard_map.315 = (bf16[512,128]{1,0:T(8,128)(2,1)}, bf16[2048,128]{1,0:T(8,128)(2,1)}, bf16[2048,128]{1,0:T(8,128)(2,1)}, f32[512,512]{1,0:T(8,128)}, bf16[512,6...) custom-call(s32[4]{0:T(128)} %reshape.324.spans, ...), custom_call_target="tpu_custom_call" | custom-call | tf_op jit(solution)/shard_map/pallas_call | solution.py:1445
  151.9 1.6 copy-done.3
  153.5 29.9 %shard_map.316 = f32[64,1024]{1,0:T(8,128)S(1)} custom-call(f32[8,64,1024]{2,1,0:T(8,128)S(1)} %bitcast.150), custom_call_target="tpu_custom_call" | custom-call | tf_op jit(solution)/shard_map/pallas_call | solution.py:436
  183.4 1.0 fusion.41
  185.6 17.3 %shard_map.317.rows = bf16[512,1024]{1,0:T(8,128)(2,1)} custom-call(bf16[64,1024]{1,0:T(8,128)(2,1)} %multiply_convert_fusion.rows), custom_call_target="tpu_custom_call" | custom-call | tf_op jit(solution)/shard_map/pallas_call | solution.py:436
  202.9 22.3 %shard_map.318 = (f32[8,512]{1,0:T(8,128)}, bf16[6288,1024]{1,0:T(8,128)(2,1)}) custom-call(bf16[512,1024]{1,0:T(8,128)(2,1)} %shard_map.317.rows, s32[1,512]{1,0:T(1,128)} %constant_dynamic-slice_fusion.1.targets, f32[6288,1024]{1,0:T(8,128)} %bitcast.151), custom_call_target="tpu_custom_call" | custom-call | tf_op jit(solution)/shard_map/pallas_call | solution.py:1204
  225.2 11.8 %shard_map.319 = f32[8,8,512]{2,1,0:T(8,128)} custom-call(f32[8,512]{1,0:T(8,128)} %get-tuple-element.63.stats), custom_call_target="tpu_custom_call" | custom-call | tf_op jit(solution)/shard_map/pallas_call | solution.py:436
  237.0 1.1 slice_reduce_fusion.2
  240.0 21.4 %shard_map.320 = f32[512,1024]{1,0:T(8,128)} custom-call(bf16[512,1024]{1,0:T(8,128)(2,1)} %shard_map.317.rows, f32[512,8]{1,0:T(8,128)} %copy.109.facts, s32[512,1]{1,0:T(8,128)} %copy.110.targets, bf16[6288,1024]{1,0:T(8,128)(2,1)} %get-tuple-element.64.head), custom_call_target="tpu_custom_call" | custom-call | tf_op jit(solution)/shard_map/pallas_call | solution.py:1252
  261.4 1.6 copy-done.1
  263.0 40.3 %shard_map.321 = (f32[64,1024]{1,0:T(8,128)S(1)}, bf16[4,512,1024]{2,1,0:T(8,128)(2,1)S(1)}, f32[4,8,512]{2,1,0:T(8,128)S(1)}) custom-call(f32[8,64,1024]{2,1,0:T(8,128)S(1)} %bitcast.149, bf16[512,1024]{1,0:T(8,128)(2,1)S(1)} %copy-done, f32[8,512]{1,0:T(8,128)S(1)} %get-tuple-element.144.facts), custom_call_target="tpu_custom_call" | custom-call | tf_op jit(solution)/shard_map/pallas_call | solution.py:436
  303.3 2.0 copy-done.2
  307.4 23.5 %shard_map.322 = (bf16[512,1024]{1,0:T(8,128)(2,1)}, f32[8,64,128]{2,1,0:T(8,128)}) custom-call(bf16[64,1024]{1,0:T(8,128)(2,1)} %get-tuple-element.118.rows, f32[8,64,128]{2,1,0:T(8,128)} %bitcast.174), custom_call_target="tpu_custom_call" | custom-call | tf_op jit(solution)/shard_map/pallas_call | solution.py:436
  330.9 32.1 %shard_map.323 = (f32[8,2048,128]{2,1,0:T(8,128)}, f32[8,2048]{1,0:T(8,128)}, f32[1024,896]{1,0:T(8,128)}, f32[640,1024]{1,0:T(8,128)}, f32[8,1024]{1,0:T(8,128)}, /*index=5*/f32[8,896]{1,0:T(8,128)}) custom-call(s32[4]{0:T(128)} %reshape.324.spans, bf16[2048,1024]{1,0:T(8,128)(2,1)} %get-tuple-element.57.residual, s32[512,1]{1,0:T(8,128)} %add_select_fusion.places, ...), custom_call_target="tpu_custom_call" | custom-call | tf_op jit(solution)/shard_map/pallas_call | solution.py:1556
  367.5 4.3 copy.148
  371.9 1.8 copy.149
  374.9 134.3 %shard_map.324 = (f32[2048,128]{1,0:T(8,128)}, f32[8,8,2048]{2,1,0:T(8,128)}, f32[8,32,896]{2,1,0:T(8,128)}, f32[5,32,1024]{2,1,0:T(8,128)}, f32[16,128]{1,0:T(8...) custom-call(f32[8,2048,128]{2,1,0:T(8,128)} %get-tuple-element.75.parts, f32[8,2048]{1,0:T(8,128)} %get-tuple-element.76.stats, ...), custom_call_target="tpu_custom_call" | custom-call | tf_op jit(solution)/shard_map/pallas_call | solution.py:436
  509.3 1.2 reduce_sum.200
  510.6 3.0 fusion.4
  513.6 1.1 fusion.13
  514.7 3.6 fusion.8.rows
  518.4 29.6 %shard_map.325 = (bf16[4,2048,128]{2,1,0:T(8,128)(2,1)}, f32[8,32,896]{2,1,0:T(8,128)}, f32[5,32,1024]{2,1,0:T(8,128)}) custom-call(bf16[2048,128]{1,0:T(8,128)(2,1)} %fusion.8.rows, f32[8,32,896]{2,1,0:T(8,128)} %get-tuple-element.87.sum_in, f32[5,32,1024]{2,1,0:T(8,128)} %get-tuple-element.88.sum_back), custom_call_target="tpu_custom_call" | custom-call | tf_op jit(solution)/shard_map/pallas_call | solution.py:436
  549.6 2.0 multiply_reduce_fusion
  551.6 1.9 multiply_reduce_fusion.1
  553.5 1.6 multiply_reduce_fusion.6
  556.3 42.3 %shard_map.326 = (f32[128,50304]{1,0:T(8,128)}, f32[8,128]{1,0:T(8,128)}) custom-call(s32[8192]{0:T(1024)} %bitcast.177, bf16[8192,128]{1,0:T(8,128)(2,1)} %bitcast.173), custom_call_target="tpu_custom_call" | custom-call | tf_op jit(solution)/shard_map/pallas_call | solution.py:1295
  598.7 1.3 reduce_sum.203
  604.4 18.6 %shard_map.327 = f32[8,128]{1,0:T(8,128)} custom-call(f32[8,128]{1,0:T(8,128)} %broadcast_in_dim.115.value), custom_call_target="tpu_custom_call" | custom-call | tf_op jit(solution)/shard_map/pallas_call | solution.py:436
  623.0 1.2 slice.137
  625.0 1.9 pad_maximum_fusion.2
  627.5 60.9 %multiply_subtract_fusion = (f32[128,50304]{1,0:T(8,128)}, f32[128,50304]{1,0:T(8,128)}, f32[128,50304]{1,0:T(8,128)}) fusion(f32[128,50304]{1,0:T(8,128)} %table.1, f32[128,50304]{1,0:T(8,128)} %get-tuple-element.94, f32[]{:T(128)} %bitcast.53, f32[128,50304]{1,0:T(8,128)} %param.36, f32[128,50304]{1,0:T(8,128)} %param.37), kind=kLoop, calls=%fused_computation.6 | loop fusion | flops 103022592 | bytes 180289536 | tf_op jit(solution)/shard_map/sub | solution.py:104
  688.4 61.7 %multiply_subtract_fusion.1 = (f32[1024,6288]{0,1:T(8,128)}, f32[1024,6288]{0,1:T(8,128)}, f32[1024,6288]{0,1:T(8,128)}) fusion(f32[1024,6288]{0,1:T(8,128)} %param.26, f32[6288,1024]{1,0:T(8,128)} %get-tuple-element.93, f32[]{:T(128)} %bitcast.53, f32[1024,6288]{0,1:T(8,128)} %param.34, f32[1024,6288]{0,1:T(8,128)} %param.35), kind=kLoop, calls=%fused_computation.8 | loop fusion | flops 103022592 | bytes 180289536 | tf_op jit(solution)/shard_map/sub | solution.py:104
  750.2 2.1 broadcast_multiply_fusion
  752.7 1.4 copy-done.7
  754.9 4.7 multiply_subtract_fusion.3
  759.6 4.2 copy.115
  764.2 1.7 copy.129
  767.1 1.0 copy-done.8
  768.1 5.2 multiply_subtract_fusion.2
  (151 shorter events, 30.0 us)
Async XLA Ops:
  7.2 743.0 %all-gather.7.cloned.1.call-start = ((), (), s32[]{:S(2)}) async-start(), calls=%async_computation.1 | async-start | bytes 3276800 | tf_op jit(solution)/shard_map/all_gather | solution.py:1768
  7.2 3.9 copy-start.20
  7.2 4.7 copy-start.21
  12.7 5.3 copy-start.6
  14.3 5.1 copy-start.15
  18.1 3.4 copy-start.23
  18.1 3.5 copy-start.22
  151.9 1.6 copy-start.3
  240.0 21.4 %copy-start = (bf16[512,1024]{1,0:T(8,128)(2,1)S(1)}, bf16[512,1024]{1,0:T(8,128)(2,1)}, u32[]{:S(2)}) copy-start(bf16[512,1024]{1,0:T(8,128)(2,1)} %shard_map.317.rows) | copy-start | bytes 3145732
  261.4 1.6 copy-start.1
  303.3 2.0 copy-start.2
  305.3 0.6 copy-start.4
  367.5 4.3 copy-start.12
  509.3 4.3 copy-start.14
  509.3 5.4 copy-start.13
  514.7 41.0 %copy-start.16 = (f32[16,128]{1,0:T(8,128)S(1)}, f32[16,128]{1,0:T(8,128)}, u32[]{:S(2)}) copy-start(f32[16,128]{1,0:T(8,128)} %get-tuple-element.82) | copy-start | bytes 24580
  518.3 81.6 %copy-start.17 = (f32[8,1024]{1,0:T(8,128)S(1)}, f32[8,1024]{1,0:T(8,128)}, u32[]{:S(2)}) copy-start(f32[8,1024]{1,0:T(8,128)} %get-tuple-element.83) | copy-start | bytes 98308
  518.3 108.5 %copy-start.18 = (f32[1792]{0:T(1024)S(1)}, f32[1792]{0:T(1024)}, u32[]{:S(2)}) copy-start(f32[1792]{0:T(1024)} %param.32) | copy-start | bytes 21508
  518.4 108.5 %copy-start.19 = (f32[1792]{0:T(1024)S(1)}, f32[1792]{0:T(1024)}, u32[]{:S(2)}) copy-start(f32[1792]{0:T(1024)} %param.33) | copy-start | bytes 21508
  548.0 211.7 %all-gather.5.cloned.1.call-start = ((), (), s32[]{:S(2)}) async-start(), calls=%async_computation | async-start | bytes 4587520 | tf_op jit(solution)/shard_map/all_gather | solution.py:1767
  750.2 2.5 copy-start.11
  752.3 1.8 copy-start.7
  752.3 2.6 copy-start.10
  763.8 2.4 copy-start.9
  764.2 2.9 copy-start.5
  764.2 3.9 copy-start.8
Sparse Core Ops, SparseCore 0:
  548.1 33.1 all-gather.6
  582.9 31.5 all-gather.4

commit v3 on v2

--- a/solution.py
+++ b/solution.py
@@ -504,20 +504,21 @@
 
 
 def entry_kernel(
-    ints, smalls, in_parts, back_tiles, table,
-    ints_out, smalls_out, out, in_all, back_all,
-    ints_all, smalls_all, turned, wide, low, ids,
+    table_steps, ints, smalls, weights_in, weights_back, table, head,
+    ints_out, scales, bias, out, in_all, back_all, head_low,
+    ints_all, smalls_all, in_parts, back_tiles, turned, wide, low, ids,
     send_int, recv_int, send_small, recv_small, send_rep, recv_rep,
-    send_in, recv_in, send_back, recv_back, send_pair, recv_pair,
-    send_z, recv_z, send_y, recv_y, own,
+    send_in, recv_in, send_back, recv_back, send_far, recv_far, send_pair, recv_pair,
+    send_up, recv_up, send_down, recv_down, send_y, recv_y, own,
 ):
     at = pl.program_id(0)
-    rep, shard, core_twin, _, y_twin = whereabouts()
-    half = lax.rem(rep, 2)
+    last = pl.num_programs(0) - 1
+    rep, shard, core_twin, x_twin, y_twin = whereabouts()
+    level, side = shard // 2, lax.rem(shard, 2)
     shard_peers = [(rep, shard_peer(shard, step)) for step in range(1, SG)]
     rep_peers = [(lax.rem(rep + step, RG), shard) for step in range(1, RG)]
-    lines = low.shape[0]
-    tokens = low.shape[1]
+    lines, tokens, feats = low.shape
+    small_rows = 14
 
     def int_copies():
         return [
@@ -539,70 +540,120 @@
 
     def in_copies():
         return [
-            remote(in_parts.at[peer[1], half], in_all.at[shard, half], send_in.at[k], recv_in.at[k], peer)
+            remote(in_parts.at[peer[1], rep], in_all.at[shard, rep], send_in.at[k], recv_in.at[k], peer)
             for k, peer in enumerate(shard_peers)
         ]
 
     def own_in():
-        return pltpu.make_async_copy(in_parts.at[shard, half], in_all.at[shard, half], own.at[0])
+        return pltpu.make_async_copy(in_parts.at[shard, rep], in_all.at[shard, rep], own.at[0])
 
     def back_move(k):
         tile = 5 * shard + k
         user, slot = tile_user(tile), tile_slot(tile)
         there = remote(
-            back_tiles.at[k, half], back_all.at[slot, half], send_back.at[k], recv_back.at[slot], (rep, user)
+            back_tiles.at[k, rep], back_all.at[slot, rep], send_back.at[k], recv_back.at[slot], (rep, user)
         )
         return user, slot, there
+
+    def quarter_copies(quarter, sends, recvs, base, peer):
+        return [
+            remote(array.at[:, quarter], array.at[:, quarter], sends.at[base + k], recvs.at[base + k], (peer, shard))
+            for k, array in enumerate((in_all, back_all))
+        ]
+
+    def far_copies():
+        return quarter_copies(rep, send_far, recv_far, 0, x_twin)
+
+    def pair_copies():
+        return quarter_copies(rep, send_pair, recv_pair, 0, core_twin) + quarter_copies(
+            x_twin, send_pair, recv_pair, 2, core_twin
+        )
+
+    def slot(line, z_at, y_at):
+        index = 2 * z_at + y_at
+        return out.at[pl.ds(line * tokens, tokens), pl.ds(pl.multiple_of(index * feats, feats), feats)]
+
+    def up_copy(line, hop):
+        here = slot(line, level - hop, side)
+        source = low.at[line] if hop == 0 else here
+        return remote(source, here, send_up.at[line, hop], recv_up.at[line, hop], (rep, shard + 2))
+
+    def down_copy(line, hop):
+        here = slot(line, level + hop, side)
+        source = low.at[line] if hop == 0 else here
+        return remote(source, here, send_down.at[line, hop], recv_down.at[line, hop], (rep, shard - 2))
+
+    def side_copy(line, z_at, source=None):
+        here = slot(line, z_at, side)
+        return remote(
+            here if source is None else source, here, send_y.at[line, z_at], recv_y.at[line, z_at], (rep, y_twin)
+        )
+
+    def keep_copy(line):
+        return pltpu.make_async_copy(low.at[line], slot(line, level, side), own.at[2 + line])
+
+    def pass_on(line, hop):
+        @pl.when(level >= hop)
+        def _():
+            pltpu.make_async_copy(low.at[line], slot(line, level - hop, side), recv_up.at[line, hop - 1]).wait()
+            if hop < 3:
+                pl.when(level < 3)(lambda: up_copy(line, hop).start())
+            side_copy(line, level - hop).start()
+
+        @pl.when(level + hop <= 3)
+        def _():
+            pltpu.make_async_copy(low.at[line], slot(line, level + hop, side), recv_down.at[line, hop - 1]).wait()
+            if hop < 3:
+                pl.when(level > 0)(lambda: down_copy(line, hop).start())
+            side_copy(line, level + hop).start()
 
     @pl.when(at == 0)
     def _():
         greet(shard_peers + rep_peers)
-        for copy in int_copies() + small_copies() + in_copies():
+        for copy in int_copies() + small_copies():
+            copy.start()
+        for target in range(SG):
+            for part in range(3):
+                columns = weights_in[:, part * D + target * HEAD_COLS : part * D + (target + 1) * HEAD_COLS]
+                in_parts[target, :, :, part * HEAD_COLS : (part + 1) * HEAD_COLS] = columns.astype(
+                    in_parts.dtype
+                ).reshape(RG, in_parts.shape[2], HEAD_COLS)
+            columns = weights_in[:, 3 * D + target * UNITS : 3 * D + (target + 1) * UNITS]
+            in_parts[target, :, :, 3 * HEAD_COLS :] = columns.astype(in_parts.dtype).reshape(
+                RG, in_parts.shape[2], UNITS
+            )
+        back_tiles[...] = weights_back[...].astype(back_tiles.dtype).reshape(back_tiles.shape)
+        for copy in in_copies():
             copy.start()
         own_in().start()
         for k in range(5):
-            user, slot, there = back_move(k)
-            here = pltpu.make_async_copy(back_tiles.at[k, half], back_all.at[slot, half], recv_back.at[slot])
+            user, slot_at, there = back_move(k)
+            here = pltpu.make_async_copy(back_tiles.at[k, rep], back_all.at[slot_at, rep], recv_back.at[slot_at])
             pl.when(user == shard)(here.start)
             pl.when(user != shard)(there.start)
         ints_all[rep, shard] = ints[...]
         smalls_all[shard] = smalls[...]
 
-    block = table[...].astype(jnp.bfloat16).astype(jnp.float32)
-    width = block.shape[1]
-    turned[pl.ds(pl.multiple_of(at * width, width), width), :] = block.T
-
-    @pl.when(at == 4)
+    @pl.when(at < table_steps)
+    def _():
+        block = table[...].astype(jnp.bfloat16).astype(jnp.float32)
+        width = block.shape[1]
+        turned[pl.ds(pl.multiple_of(at * width, width), width), :] = block.T
+
+    @pl.when(at == 5)
     def _():
         for copy in int_copies():
             copy.wait()
         for copy in rep_copies():
             copy.start()
 
-    @pl.when(at == pl.num_programs(0) - 1)
+    @pl.when(at == table_steps)
     def _():
         for copy in rep_copies():
             copy.wait()
         to_scalars = pltpu.make_async_copy(ints_all.at[:, pl.ds(2 * rep, 2)], ids, own.at[1])
         to_scalars.start()
         to_scalars.wait()
-
-        def slot(index, line):
-            return out.at[
-                pl.ds(line * tokens, tokens),
-                pl.ds(pl.multiple_of(index * low.shape[2], low.shape[2]), low.shape[2]),
-            ]
-
-        def line_copies(line):
-            z_copies = [
-                remote(low.at[line], slot(shard, line), send_z.at[line, k - 1], recv_z.at[line, k - 1], (rep, z_peer(shard, k)))
-                for k in range(1, 4)
-            ]
-            first_y = remote(low.at[line], slot(shard, line), send_y.at[line, 0], recv_y.at[line, 0], (rep, y_twin))
-            keep = pltpu.make_async_copy(low.at[line], slot(shard, line), own.at[2 + line])
-            return z_copies, first_y, keep
-
-        started = []
         for line in range(lines):
             micro, member = line // 2, line % 2
             for block_at in range(RG):
@@ -616,65 +667,97 @@
                         ]
 
             low[line] = wide[...].astype(jnp.bfloat16)
-            z_copies, first_y, keep = line_copies(line)
-            for copy in z_copies + [first_y, keep]:
-                copy.start()
-            started.append((z_copies, first_y, keep))
-        passed = []
-        for line in range(lines):
-            for k in range(1, 4):
-                started[line][0][k - 1].wait_recv()
-                came_from = z_peer(shard, 4 - k)
-                copy = remote(
-                    slot(came_from, line), slot(came_from, line), send_y.at[line, k], recv_y.at[line, k], (rep, y_twin)
-                )
-                copy.start()
-                passed.append(copy)
+            pl.when(level < 3)(lambda: up_copy(line, 0).start())
+            pl.when(level > 0)(lambda: down_copy(line, 0).start())
+            side_copy(line, level, low.at[line]).start()
+            keep_copy(line).start()
         own_in().wait()
         for copy in in_copies():
             copy.wait()
         for k in range(5):
-            pltpu.make_async_copy(back_tiles.at[0, half], back_all.at[k, half], recv_back.at[k]).wait()
-        pair_in = remote(in_all.at[:, half], in_all.at[:, half], send_pair.at[0], recv_pair.at[0], (core_twin, shard))
-        pair_back = remote(back_all.at[:, half], back_all.at[:, half], send_pair.at[1], recv_pair.at[1], (core_twin, shard))
-        pair_in.start()
-        pair_back.start()
+            pltpu.make_async_copy(back_tiles.at[0, rep], back_all.at[k, rep], recv_back.at[k]).wait()
+        for copy in far_copies():
+            copy.start()
+
+    @pl.when(at >= table_steps)
+    def _():
+        head_low[...] = head[...].astype(jnp.bfloat16)
+
+    order = sorted(((line, hop) for line in range(lines) for hop in range(1, 4)), key=lambda item: (sum(item), item[1]))
+    for step, (line, hop) in enumerate(order):
+        pl.when(at == table_steps + 1 + step)(functools.partial(pass_on, line, hop))
+
+    @pl.when(at == last - 2)
+    def _():
+        for copy in far_copies():
+            copy.wait()
+        for copy in pair_copies():
+            copy.start()
+
+    @pl.when(at == last)
+    def _():
         for copy in small_copies():
             copy.wait()
         ints_out[...] = ints_all[...]
-        smalls_out[...] = smalls_all[...]
+
+        def small_row(row):
+            return smalls_all[row // small_rows, pl.ds(lax.rem(row, small_rows), 1), :]
+
+        scales[...] = jnp.zeros_like(scales)
+        for vector, start in enumerate([8 * k for k in range(6)] + [8 * 13]):
+            for part in range(8):
+                row = start + part
+                scales[vector : vector + 1, part * 128 : (part + 1) * 128] = smalls_all[
+                    row // small_rows, row % small_rows : row % small_rows + 1, :
+                ]
+        for part in range(3):
+            bias[:, part * 128 : (part + 1) * 128] = small_row(48 + 8 * part + shard)
+        for part in range(4):
+            bias[:, (3 + part) * 128 : (4 + part) * 128] = small_row(72 + 4 * shard + part)
         for k in range(5):
             user, _, there = back_move(k)
             pl.when(user != shard)(there.wait_send)
-        for z_copies, first_y, keep in started:
-            keep.wait()
-            first_y.wait()
-            for copy in z_copies:
-                copy.wait_send()
-        for copy in passed:
+        for line in range(lines):
+            keep_copy(line).wait()
+            for hop in range(3):
+                pl.when((level >= hop) & (level < 3))(lambda: up_copy(line, hop).wait_send())
+                pl.when((level + hop <= 3) & (level > 0))(lambda: down_copy(line, hop).wait_send())
+            for z_at in range(4):
+                side_copy(line, z_at).wait()
+        for copy in pair_copies():
             copy.wait()
-        pair_in.wait()
-        pair_back.wait()
-
-
-def share_entry(ints, smalls, in_parts, back_tiles, table, tokens, number):
+
+
+def share_entry(ints, smalls, weights_in, weights_back, table, head, tokens, number):
+    quarter = weights_in.shape[0] // RG
+    in_shape = (SG, RG, quarter, OWN_COLS)
+    back_shape = (5, RG, 32, weights_back.shape[1])
     dma = pltpu.SemaphoreType.DMA
     feats, vocab = table.shape
     blocks = pl.cdiv(vocab, TABLE_BLOCK)
+    head_blocks = max(pl.cdiv(head.shape[0], CAST_BLOCK), 13)
     lines = 4
     per_line = tokens // lines
+    head_spec = pl.BlockSpec(
+        (CAST_BLOCK, head.shape[1]),
+        lambda at: (jnp.clip(at - blocks, 0, pl.cdiv(head.shape[0], CAST_BLOCK) - 1), 0),
+    )
     return comm_call(
-        entry_kernel,
+        functools.partial(entry_kernel, blocks),
         [
             jax.ShapeDtypeStruct((RG, SG) + ints.shape, ints.dtype),
-            jax.ShapeDtypeStruct((SG,) + smalls.shape, smalls.dtype),
+            jax.ShapeDtypeStruct((8, SG * feats), jnp.float32),
+            jax.ShapeDtypeStruct((1, OWN_COLS), jnp.float32),
             jax.ShapeDtypeStruct((tokens, SG * feats), jnp.bfloat16),
-            jax.ShapeDtypeStruct(in_parts.shape, in_parts.dtype),
-            jax.ShapeDtypeStruct(back_tiles.shape, back_tiles.dtype),
+            jax.ShapeDtypeStruct(in_shape, jnp.bfloat16),
+            jax.ShapeDtypeStruct(back_shape, jnp.bfloat16),
+            jax.ShapeDtypeStruct(head.shape, jnp.bfloat16),
         ],
         [
             pltpu.VMEM((RG, SG) + ints.shape, ints.dtype),
             pltpu.VMEM((SG,) + smalls.shape, smalls.dtype),
+            pltpu.VMEM(in_shape, jnp.bfloat16),
+            pltpu.VMEM(back_shape, jnp.bfloat16),
             pltpu.VMEM((blocks * TABLE_BLOCK, feats), jnp.float32),
             pltpu.VMEM((per_line, feats), jnp.float32),
             pltpu.VMEM((lines, per_line, feats), jnp.bfloat16),
@@ -685,15 +768,16 @@
         + [dma((SG - 1,))] * 2
         + [dma((5,))] * 2
         + [dma((2,))] * 2
-        + [dma((lines, 3))] * 2
+        + [dma((4,))] * 2
+        + [dma((lines, 3))] * 4
         + [dma((lines, 4))] * 2
         + [dma((2 + lines,))],
         number,
-        (ints, smalls, in_parts, back_tiles, table),
-        ["v", "v", "a", "a", pl.BlockSpec((feats, TABLE_BLOCK), lambda at: (0, at))],
-        "vvaaa",
+        (ints, smalls, weights_in, weights_back, table, head),
+        ["v", "v", "v", "v", pl.BlockSpec((feats, TABLE_BLOCK), lambda at: (0, jnp.minimum(at, blocks - 1))), head_spec],
+        ["v", "v", "v", "a", "a", "a", head_spec],
         VMEM_LIMIT,
-        (blocks,),
+        (blocks + head_blocks,),
     )
 
 
@@ -890,12 +974,18 @@
     )
 
 
+def coded(rows, steps):
+    inverse = jnp.where(steps > 0.0, 1.0 / steps, 0.0)
+    return jnp.clip(jnp.round(rows * inverse), -32767.0, 32767.0).astype(jnp.int32).astype(jnp.int16)
+
+
 def layer_kernel(
-    vocab, parts, stats, grad_in, grad_back, smalls, rows, facts, targets, head,
-    out, stats_out, sum_in, sum_back, smalls_out, head_out, squares,
-    stats_all, from_y, own_sum, from_z, pair_in, pair_back, half_in, half_back, far_in, far_back, small_rep, small_sum, small_shard,
+    vocab, parts, stats, base, unit, grad_in, grad_back, smalls, rows, facts, targets, head,
+    rows_all, in_all, back_all, smalls_out, head_out, squares,
+    low, sum_in, sum_back, turned, stats_all, steps_all, from_y, own_sum, from_z, pair_in, pair_back, half_in, half_back, far_in, far_back, small_rep, small_sum, small_shard,
     send_y, recv_y, send_z, recv_z, send_stat, recv_stat, send_pair, recv_pair, send_far, recv_far,
     send_rep, recv_rep, send_small, recv_small,
+    send_row, recv_row, send_in, recv_in, send_back, recv_back, own,
 ):
     at = pl.program_id(0)
     last = pl.num_programs(0) - 1
@@ -945,22 +1035,48 @@
             for k, peer in enumerate(shard_peers)
         ]
 
+    def in_copies():
+        return [
+            remote(sum_in.at[peer[1]], in_all.at[shard], send_in.at[k], recv_in.at[k], peer)
+            for k, peer in enumerate(shard_peers)
+        ]
+
+    def own_in():
+        return pltpu.make_async_copy(sum_in.at[shard], in_all.at[shard], own.at[0])
+
+    def back_move(slot):
+        tile = shard if slot == 0 else SG + 4 * shard + slot - 1
+        owner, place = tile // 5, lax.rem(tile, 5)
+        there = remote(sum_back.at[slot], back_all.at[place], send_back.at[slot], recv_back.at[place], (rep, owner))
+        return owner, place, there
+
+    def decoded(codes, steps):
+        return codes.astype(jnp.int32).astype(jnp.float32) * steps
+
+    def pair_sum(step):
+        y_copy(step).wait_recv()
+        own = decoded(parts[z_peer(shard, step)], steps_all[:, 0:1])
+        return own + decoded(from_y[step], steps_all[:, 4:5])
+
     def pass_on(step):
-        y_copy(step).wait_recv()
-        own_sum[step] = parts[z_peer(shard, step)] + from_y[step]
+        own_sum[step] = coded(pair_sum(step), steps_all[:, 0:1] + steps_all[:, 4:5])
         z_copy(step).start()
 
     @pl.when(at == 0)
     def _():
         greet(shard_peers + rep_peers)
+        for copy in stat_copies():
+            copy.start()
         for step in (2, 1, 3, 0):
             y_copy(step).start()
-        for copy in pair_copies(core_far, 1) + pair_copies(core_twin, 0) + rep_copies() + stat_copies():
+        for copy in pair_copies(core_far, 1) + pair_copies(core_twin, 0) + rep_copies():
             copy.start()
         stats_all[shard] = stats[...]
         squares[...] = jnp.zeros_like(squares)
-
-    @pl.when(at == 2)
+        for group in range(RG):
+            turned[group] = rows[group].T
+
+    @pl.when(at == 1)
     def _():
         for copy in pair_copies(core_far, 1):
             copy.wait()
@@ -974,46 +1090,94 @@
         for copy in small_copies():
             copy.start()
 
-    pl.when(at == 5)(lambda: pass_on(2))
-    pl.when(at == 9)(lambda: pass_on(1))
-
-    _, low = vocab_rows(vocab, head[...])
-    total = None
-    for group in range(RG):
-        grads = logit_grads(
-            vocab, low, rows[group], facts[group, 0:1, :], targets[group, 0:1, :], facts[group, 1:2, :]
-        )
-        term = plain_dot(grads, rows[group])
-        total = term if total is None else total + term
-    head_out[...] = total
-    squares[0:1, :] += jnp.sum(total * total, axis=0, keepdims=True)
-
-    @pl.when(at == last)
+    @pl.when(at == 3)
     def _():
-        pass_on(3)
+        for copy in stat_copies():
+            copy.wait()
+        near = [stats_all[z_peer(shard, k), 2:3, :] for k in range(4)]
+        near += [stats_all[z_peer(y_twin, k), 2:3, :] for k in range(4)]
+        sums = stats_all[0]
+        for k in range(1, SG):
+            sums = sums + stats_all[k]
+        near += [sums[0:2, :], stats[3:4, :], jnp.zeros((5, sums.shape[1]), jnp.float32)]
+        steps_all[:, 0:16] = jnp.concatenate(near, axis=0).T
+        pass_on(2)
+
+    pl.when(at == 6)(lambda: pass_on(1))
+    pl.when(at == 8)(lambda: pass_on(3))
+
+    @pl.when(at == 10)
+    def _():
         for copy in pair_copies(core_twin, 0):
             copy.wait()
         for copy in far_copies():
             copy.wait()
         sum_in[...] = grad_in[rep] + pair_in[0] + far_in[...]
         sum_back[...] = grad_back[rep] + pair_back[0] + far_back[...]
-        for copy in stat_copies() + small_copies():
+        for copy in in_copies():
+            copy.start()
+        own_in().start()
+        for slot in range(5):
+            owner, place, there = back_move(slot)
+            here = pltpu.make_async_copy(sum_back.at[slot], back_all.at[place], recv_back.at[place])
+            pl.when(owner == shard)(here.start)
+            pl.when(owner != shard)(there.start)
+
+    def head_block(size):
+        total = None
+        for group in range(RG):
+            base = at * VOCAB_BLOCK
+            grads = logit_grads(head[:size], turned[group], facts[group, 0:1, :], targets[group, 0:1, :] - base)
+            term = plain_dot(grads, rows[group])
+            total = term if total is None else total + term
+        head_out[:size] = total
+        squares[0:1, :] += jnp.sum(total * total, axis=0, keepdims=True)
+
+    vocab_blocks(vocab, VOCAB_BLOCK, head_block)
+
+    @pl.when(at == last)
+    def _():
+        total = pair_sum(0)
+        for step in (1, 2, 3):
+            z_copy(step).wait()
+            behind = 4 - step
+            steps = steps_all[:, behind : behind + 1] + steps_all[:, 4 + behind : 5 + behind]
+            total = total + decoded(from_z[step - 1], steps)
+        mean, slope, scale = (steps_all[:, k : k + 1] for k in (8, 9, 10))
+        d_rows = (total - mean / D - unit[...] * (slope / D)) * scale
+        low[...] = (base[...] + d_rows).astype(low.dtype)
+        to_x = remote(low, rows_all.at[rep], send_row.at[0], recv_row.at[0], (x_twin, shard))
+        to_core = remote(low, rows_all.at[rep], send_row.at[1], recv_row.at[1], (core_twin, shard))
+        keep = pltpu.make_async_copy(low, rows_all.at[rep], own.at[1])
+        to_x.start()
+        to_core.start()
+        keep.start()
+        for copy in small_copies():
             copy.wait()
-        stats_out[...] = stats_all[...]
         whole = small_sum[shard]
         for k in range(SG - 1):
             whole = whole + small_shard[k]
         smalls_out[...] = whole
-        y_copy(0).wait_recv()
-        own = parts[shard] + from_y[0]
-        for step in (1, 2, 3):
-            z_copy(step).wait()
-        out[...] = own + from_z[0] + from_z[1] + from_z[2]
         for step in range(4):
             y_copy(step).wait_send()
-
-
-def layer_sums(parts, stats, grad_in, grad_back, smalls, rows, facts, targets, head, number):
+        to_x.wait_recv()
+        passed = remote(rows_all.at[x_twin], rows_all.at[x_twin], send_row.at[2], recv_row.at[2], (core_twin, shard))
+        passed.start()
+        own_in().wait()
+        for copy in in_copies():
+            copy.wait()
+        for place in range(5):
+            pltpu.make_async_copy(sum_back.at[0], back_all.at[place], recv_back.at[place]).wait()
+        for slot in range(5):
+            owner, _, there = back_move(slot)
+            pl.when(owner != shard)(there.wait_send)
+        keep.wait()
+        to_x.wait_send()
+        to_core.wait()
+        passed.wait()
+
+
+def layer_sums(parts, stats, base, unit, grad_in, grad_back, smalls, rows, facts, targets, head, number):
     dma = pltpu.SemaphoreType.DMA
     chunk = parts.shape[1:]
     quarter_in, quarter_back, piece = grad_in.shape[1:], grad_back.shape[1:], smalls.shape[1:]
@@ -1023,77 +1187,28 @@
     block = pl.BlockSpec((VOCAB_BLOCK, depth), lambda at: (at, 0))
     return comm_call(
         functools.partial(layer_kernel, vocab),
-        [shape(chunk), shape((SG,) + stats.shape), shape(quarter_in), shape(quarter_back), shape(piece), shape(head.shape), shape((8, depth))],
-        [vmem((SG,) + stats.shape)]
-        + sum_buffers(chunk)
+        [
+            jax.ShapeDtypeStruct((RG,) + chunk, jnp.bfloat16),
+            shape(quarter_in),
+            shape(quarter_back),
+            shape(piece),
+            shape(head.shape),
+            shape((8, depth)),
+        ],
+        [pltpu.VMEM(chunk, jnp.bfloat16), vmem(quarter_in), vmem(quarter_back)]
+        + [pltpu.VMEM((RG, depth, rows.shape[1]), rows.dtype), vmem((SG,) + stats.shape), vmem((chunk[0], 128))]
+        + [pltpu.VMEM((count,) + chunk, parts.dtype) for count in (4, 4, 3)]
         + [vmem((2,) + quarter_in), vmem((2,) + quarter_back), vmem(quarter_in), vmem(quarter_back), vmem(quarter_in), vmem(quarter_back)]
         + [vmem((3,) + smalls.shape), vmem(smalls.shape), vmem((SG - 1,) + piece)]
         + sum_sems()
-        + [dma((SG - 1,))] * 2 + [dma((4,))] * 2 + [dma((2,))] * 2 + [dma((3,))] * 2 + [dma((SG - 1,))] * 2,
+        + [dma((SG - 1,))] * 2 + [dma((4,))] * 2 + [dma((2,))] * 2 + [dma((3,))] * 2 + [dma((SG - 1,))] * 2
+        + [dma((3,))] * 2 + [dma((SG - 1,))] * 2 + [dma((5,))] * 2 + [dma((2,))],
         number,
-        (parts, stats, grad_in, grad_back, smalls, rows, facts, targets, head),
-        ["v"] * 8 + [block],
-        ["v"] * 5 + [block, "v"],
+        (parts, stats, base, unit, grad_in, grad_back, smalls, rows, facts, targets, head),
+        ["v"] * 10 + [block],
+        ["a"] * 3 + ["v", block, "v"],
         62 << 20,
         (pl.cdiv(vocab, VOCAB_BLOCK),),
-    )
-
-
-def return_kernel(
-    rows, sum_in, sum_back, rows_all, in_all, back_all, send_row, recv_row, own, send_in, recv_in, send_back, recv_back
-):
-    rep, shard, core_twin, x_twin, _ = whereabouts()
-    shard_peers = [(rep, shard_peer(shard, step)) for step in range(1, SG)]
-    greet(shard_peers + [(core_twin, shard), (x_twin, shard)])
-    keep = pltpu.make_async_copy(rows, rows_all.at[rep], own.at[0])
-    keep.start()
-    to_x = remote(rows, rows_all.at[rep], send_row.at[0], recv_row.at[0], (x_twin, shard))
-    to_core = remote(rows, rows_all.at[rep], send_row.at[1], recv_row.at[1], (core_twin, shard))
-    to_x.start()
-    to_core.start()
-    in_copies = [
-        remote(sum_in.at[peer[1]], in_all.at[shard], send_in.at[k], recv_in.at[k], peer)
-        for k, peer in enumerate(shard_peers)
-    ]
-    for copy in in_copies:
-        copy.start()
-    keep_in = pltpu.make_async_copy(sum_in.at[shard], in_all.at[shard], own.at[1])
-    keep_in.start()
-    moves = []
-    for slot in range(5):
-        tile = shard if slot == 0 else SG + 4 * shard + slot - 1
-        owner = tile // 5
-        at = lax.rem(tile, 5)
-        there = remote(sum_back.at[slot], back_all.at[at], send_back.at[slot], recv_back.at[at], (rep, owner))
-        here = pltpu.make_async_copy(sum_back.at[slot], back_all.at[at], recv_back.at[at])
-        pl.when(owner == shard)(here.start)
-        pl.when(owner != shard)(there.start)
-        moves.append((owner, there))
-    to_x.wait_recv()
-    passed = remote(rows_all.at[x_twin], rows_all.at[x_twin], send_row.at[2], recv_row.at[2], (core_twin, shard))
-    passed.start()
-    keep_in.wait()
-    for copy in in_copies:
-        copy.wait()
-    for at in range(5):
-        pltpu.make_async_copy(sum_back.at[0], back_all.at[at], recv_back.at[at]).wait()
-    for owner, there in moves:
-        pl.when(owner != shard)(there.wait_send)
-    keep.wait()
-    to_x.wait_send()
-    to_core.wait()
-    passed.wait()
-
-
-def return_sums(rows, sum_in, sum_back, number):
-    dma = pltpu.SemaphoreType.DMA
-    shape = lambda dims, like: jax.ShapeDtypeStruct(dims, like.dtype)
-    return comm_call(
-        return_kernel,
-        [shape((RG,) + rows.shape, rows), shape(sum_in.shape, sum_in), shape(sum_back.shape, sum_back)],
-        [dma((3,))] * 2 + [dma((2,))] + [dma((SG - 1,))] * 2 + [dma((5,))] * 2,
-        number,
-        (rows, sum_in, sum_back),
     )
 
 
@@ -1145,7 +1260,9 @@
 UNITS = FF // SG
 OWN_COLS = 3 * HEAD_COLS + UNITS
 VOCAB_BLOCK = 512
+ROW_BLOCK = 1024
 TABLE_BLOCK = 4096
+CAST_BLOCK = 512
 VMEM_LIMIT = 60 << 20
 
 
@@ -1161,33 +1278,34 @@
     return jnp.dot(left, right, preferred_element_type=jnp.float32)
 
 
-def vocab_rows(vocab, block):
+def vocab_blocks(vocab, height, body):
     at = pl.program_id(0)
-    places = at * VOCAB_BLOCK + lax.broadcasted_iota(jnp.int32, block.shape, 0)
-    return places, jnp.where(places < vocab, block, jnp.zeros_like(block))
-
-
-def top_kernel(vocab, rows, targets, head, stats, head_out, top, total, target):
+    full, tail = divmod(vocab, height)
+    pl.when(at < full)(lambda: body(height))
+    if tail > 0:
+        pl.when(at == full)(lambda: body(tail))
+
+
+def top_kernel(vocab, rows, targets, head, stats, turned, top, total, target):
     at = pl.program_id(0)
 
     @pl.when(at == 0)
     def _():
+        turned[...] = rows[...].T
         top[...] = jnp.full_like(top, -1e30)
         total[...] = jnp.zeros_like(total)
         target[...] = jnp.zeros_like(target)
 
-    low = head[...].astype(jnp.bfloat16)
-    head_out[...] = low
-    logits = transposed_dot(low, rows[...])
-    places = at * VOCAB_BLOCK + lax.broadcasted_iota(jnp.int32, logits.shape, 0)
-    valid = places < vocab
-    masked = jnp.where(valid, logits, -1e30)
-    highest = jnp.maximum(top[...], jnp.max(masked, axis=0, keepdims=True))
-    weights = jnp.where(valid, jnp.exp(masked - highest), 0.0)
-    total[...] = total[...] * jnp.exp(top[...] - highest) + jnp.sum(weights, axis=0, keepdims=True)
-    top[...] = highest
-    hits = (places == targets[...]) & valid
-    target[...] += jnp.sum(jnp.where(hits, logits, 0.0), axis=0, keepdims=True)
+    def block(size):
+        logits = plain_dot(head[:size], turned[...])
+        hits = lax.broadcasted_iota(jnp.int32, logits.shape, 0) == targets[...] - at * ROW_BLOCK
+        target[...] += jnp.sum(jnp.where(hits, logits, 0.0), axis=0, keepdims=True)
+        highest = jnp.maximum(top[...], jnp.max(logits, axis=0, keepdims=True))
+        weights = jnp.sum(jnp.exp(logits - highest), axis=0, keepdims=True)
+        total[...] = total[...] * jnp.exp(top[...] - highest) + weights
+        top[...] = highest
+
+    vocab_blocks(vocab, ROW_BLOCK, block)
 
     @pl.when(at == pl.num_programs(0) - 1)
     def _():
@@ -1203,47 +1321,39 @@
     line = pltpu.VMEM((1, count), jnp.float32)
     return pl.pallas_call(
         functools.partial(top_kernel, vocab),
-        grid=(pl.cdiv(vocab, VOCAB_BLOCK),),
+        grid=(pl.cdiv(vocab, ROW_BLOCK),),
         in_specs=[
             pl.BlockSpec((count, depth), lambda at: (0, 0)),
             pl.BlockSpec((1, count), lambda at: (0, 0)),
-            pl.BlockSpec((VOCAB_BLOCK, depth), lambda at: (at, 0)),
+            pl.BlockSpec((ROW_BLOCK, depth), lambda at: (at, 0)),
         ],
-        out_specs=[
-            pl.BlockSpec((8, count), lambda at: (0, 0)),
-            pl.BlockSpec((VOCAB_BLOCK, depth), lambda at: (at, 0)),
-        ],
-        out_shape=[
-            jax.ShapeDtypeStruct((8, count), jnp.float32),
-            jax.ShapeDtypeStruct(head.shape, jnp.bfloat16),
-        ],
-        scratch_shapes=[line, line, line],
+        out_specs=pl.BlockSpec((8, count), lambda at: (0, 0)),
+        out_shape=jax.ShapeDtypeStruct((8, count), jnp.float32),
+        scratch_shapes=[pltpu.VMEM((depth, count), rows.dtype), line, line, line],
         compiler_params=pltpu.CompilerParams(vmem_limit_bytes=VMEM_LIMIT),
     )(rows, targets, head)
 
 
-def logit_grads(vocab, low, rows, logsum, targets, counted):
-    logits = transposed_dot(low, rows)
-    places = pl.program_id(0) * VOCAB_BLOCK + lax.broadcasted_iota(jnp.int32, logits.shape, 0)
-    hits = (places == targets).astype(jnp.float32)
-    grads = (jnp.exp(logits - logsum) - hits) * counted
-    return jnp.where(places < vocab, grads, 0.0).astype(jnp.bfloat16)
-
-
-def rows_kernel(vocab, rows, facts, targets, head, out):
+def logit_grads(low, turned, logsum, targets):
+    logits = plain_dot(low, turned)
+    hits = lax.broadcasted_iota(jnp.int32, logits.shape, 0) == targets
+    weights = jnp.exp(logits - logsum)
+    return jnp.where(hits, weights - 1.0, weights).astype(jnp.bfloat16)
+
+
+def rows_kernel(vocab, rows, facts, targets, head, out, turned):
     at = pl.program_id(0)
 
     @pl.when(at == 0)
     def _():
+        turned[...] = rows[...].T
         out[...] = jnp.zeros_like(out)
 
-    _, low = vocab_rows(vocab, head[...])
-    logits = transposed_dot(rows[...], low)
-    places = at * VOCAB_BLOCK + lax.broadcasted_iota(jnp.int32, logits.shape, 1)
-    hits = (places == targets[...]).astype(jnp.float32)
-    grads = (jnp.exp(logits - facts[:, 0:1]) - hits) * facts[:, 1:2]
-    grads = jnp.where(places < vocab, grads, 0.0).astype(jnp.bfloat16)
-    out[...] += plain_dot(grads, low)
+    def block(size):
+        low = head[:size]
+        out[...] += first_dot(logit_grads(low, turned[...], facts[0:1, :], targets[...] - at * ROW_BLOCK), low)
+
+    vocab_blocks(vocab, ROW_BLOCK, block)
 
 
 def picked_grads(rows, facts, targets, head):
@@ -1251,15 +1361,16 @@
     count = rows.shape[0]
     return pl.pallas_call(
         functools.partial(rows_kernel, vocab),
-        grid=(pl.cdiv(vocab, VOCAB_BLOCK),),
+        grid=(pl.cdiv(vocab, ROW_BLOCK),),
         in_specs=[
             pl.BlockSpec((count, depth), lambda at: (0, 0)),
-            pl.BlockSpec((count, 8), lambda at: (0, 0)),
-            pl.BlockSpec((count, 1), lambda at: (0, 0)),
-            pl.BlockSpec((VOCAB_BLOCK, depth), lambda at: (at, 0)),
+            pl.BlockSpec((8, count), lambda at: (0, 0)),
+            pl.BlockSpec((1, count), lambda at: (0, 0)),
+            pl.BlockSpec((ROW_BLOCK, depth), lambda at: (at, 0)),
         ],
         out_specs=pl.BlockSpec((count, depth), lambda at: (0, 0)),
         out_shape=jax.ShapeDtypeStruct((count, depth), jnp.float32),
+        scratch_shapes=[pltpu.VMEM((depth, count), rows.dtype)],
         compiler_params=pltpu.CompilerParams(vmem_limit_bytes=VMEM_LIMIT),
     )(rows, facts, targets, head)
 
@@ -1336,13 +1447,15 @@
     return centred * scale, scale
 
 
-def exact_dot(left, right):
-    return jnp.dot(left, right, precision=lax.Precision.HIGHEST, preferred_element_type=jnp.float32)
+def exact_dot(left, right, dims):
+    return lax.dot_general(
+        left, right, (dims, ((), ())), precision=lax.Precision.HIGHEST, preferred_element_type=jnp.float32
+    )
 
 
 def pick_matrix(places, tokens):
-    lane = lax.broadcasted_iota(jnp.int32, (places.shape[0], tokens), 1)
-    return (places == lane).astype(jnp.float32)
+    token = lax.broadcasted_iota(jnp.int32, (tokens, places.shape[1]), 0)
+    return (places == token).astype(jnp.float32)
 
 
 def turn(rows, tables, sign):
@@ -1362,14 +1475,14 @@
 
 
 def head_probs(queries, keys, allowed, head):
-    scores = transposed_dot(head_lanes(queries, head), keys) * HD ** (-0.5)
+    scores = transposed_dot(keys, head_lanes(queries, head)) * HD ** (-0.5)
     scores = jnp.where(allowed, scores, -1e30)
-    exponent = jnp.exp(scores - jnp.max(scores, axis=-1, keepdims=True))
-    return exponent / jnp.sum(exponent, axis=-1, keepdims=True)
+    exponent = jnp.exp(scores - jnp.max(scores, axis=0, keepdims=True))
+    return exponent / jnp.sum(exponent, axis=0, keepdims=True)
 
 
 def line_allowed(places, span, tokens):
-    keys = lax.broadcasted_iota(jnp.int32, (places.shape[0], tokens), 1)
+    keys = lax.broadcasted_iota(jnp.int32, (tokens, places.shape[1]), 0)
     in_query = (places >= span) & (places < span + PIC)
     in_key = (keys >= span) & (keys < span + PIC)
     return (keys <= places) | (in_query & in_key)
@@ -1386,8 +1499,9 @@
     gain_two, shift_two = scales[2:3, :], scales[3:4, :]
     unit, _ = centred_rows(residual[...].astype(jnp.float32))
     low_one = (unit * gain_one + shift_one).astype(bf16)
-    pick = pick_matrix(places[...], tokens)
-    rows = plain_dot(pick.astype(bf16), residual[...])
+    slots = places[0:1, :]
+    pick = pick_matrix(slots, tokens)
+    rows = first_dot(pick.astype(bf16), residual[...])
     picked_rows[...] = rows.astype(bf16)
     unit, _ = centred_rows(rows)
     low_picked = (unit * gain_one + shift_one).astype(bf16)
@@ -1395,7 +1509,7 @@
     low_two = (unit * gain_two + shift_two).astype(bf16)
     picked_two[...] = low_two
     tables = (own[...], after[...], before[...])
-    picked_tables = tuple(exact_dot(pick, table) for table in tables)
+    picked_tables = tuple(exact_dot(pick, table, ((0,), (0,))) for table in tables)
     two, three = 2 * HEAD_COLS, 3 * HEAD_COLS
     query = plain_dot(low_picked, weights[:, :HEAD_COLS]) + bias[:, :HEAD_COLS]
     query = turn(query, picked_tables, 1.0).astype(bf16)
@@ -1405,11 +1519,11 @@
     keys[...] = key
     value = (plain_dot(low_one, weights[:, two:three]) + bias[:, two:three]).astype(bf16)
     values[...] = value
-    allowed = line_allowed(places[...], span, tokens)
+    allowed = line_allowed(slots, span, tokens)
     attended = None
     for head in range(GROUP_HEADS):
         probs = head_probs(query, key, allowed, head).astype(bf16)
-        term = head_lanes(plain_dot(probs, value), head)
+        term = head_lanes(first_dot(probs, value), head)
         attended = term if attended is None else attended + term
     joined[:, :HEAD_COLS] = attended.astype(bf16)
     pre = plain_dot(low_two, weights[:, three:]) + bias[:, three:]
@@ -1428,7 +1542,7 @@
 
 def layer_forward(spans, residual, places, scales, bias, tables, weights, back):
     lines = spans.shape[0]
-    tokens, slots = residual.shape[0] // lines, places.shape[0] // lines
+    tokens, slots = residual.shape[0] // lines, places.shape[1]
     depth = residual.shape[1]
     bf16, f32 = jnp.bfloat16, jnp.float32
     outs = [
@@ -1448,7 +1562,7 @@
         in_specs=[
             pl.BlockSpec(memory_space=pltpu.SMEM),
             line_block(tokens, depth),
-            line_block(slots, 1),
+            line_block(8, slots),
             still(scales),
             still(bias),
             *[still(table) for table in tables],
@@ -1463,8 +1577,8 @@
 
 def backward_kernel(
     spans, residual, places, scales, own, after, before, weights, back,
-    queries, keys, values, hidden, joined, picked_one, picked_two, d_branch,
-    unit_parts, stats, grad_in, grad_back, grad_scales, grad_bias,
+    queries, keys, values, hidden, joined, picked_one, picked_two, d_branch, d_after,
+    unit_parts, stats, base, own_unit, grad_in, grad_back, grad_scales, grad_bias, unit_rows,
 ):
     bf16 = jnp.bfloat16
     line = pl.program_id(0)
@@ -1478,9 +1592,11 @@
         for total in (grad_in, grad_back, grad_scales, grad_bias):
             total[...] = jnp.zeros_like(total)
 
-    pick = pick_matrix(places[...], tokens)
+    slots = places[0:1, :]
+    pick = pick_matrix(slots, tokens)
+    base[...] = exact_dot(pick, d_after[...], ((1,), (0,)))
     tables = (own[...], after[...], before[...])
-    picked_tables = tuple(exact_dot(pick, table) for table in tables)
+    picked_tables = tuple(exact_dot(pick, table, ((0,), (0,))) for table in tables)
     pick = pick.astype(bf16)
     d_rows = d_branch[...]
     d_joined = transposed_dot(d_rows, back[...])
@@ -1489,18 +1605,18 @@
     pre = hidden[...]
     slope = 0.5 * (1.0 + lax.erf(pre * 0.5**0.5)) + pre * jnp.exp(-0.5 * pre * pre) * (2.0 * 3.141592653589793) ** -0.5
     d_hidden = (d_joined[:, HEAD_COLS:] * slope).astype(bf16)
-    allowed = line_allowed(places[...], span, tokens)
+    allowed = line_allowed(slots, span, tokens)
     query, key, value = queries[...], keys[...], values[...]
     d_query = d_key = d_value = None
     for head in range(GROUP_HEADS):
         probs = head_probs(query, key, allowed, head)
         d_head = head_lanes(d_attended, head)
-        d_probs = transposed_dot(d_head, value)
-        d_scores = (probs * (d_probs - jnp.sum(probs * d_probs, axis=-1, keepdims=True))).astype(bf16)
+        d_probs = transposed_dot(value, d_head)
+        d_scores = (probs * (d_probs - jnp.sum(probs * d_probs, axis=0, keepdims=True))).astype(bf16)
         terms = (
-            head_lanes(plain_dot(d_scores, key), head),
-            first_dot(d_scores, head_lanes(query, head)),
-            first_dot(probs.astype(bf16), d_head),
+            head_lanes(first_dot(d_scores, key), head),
+            plain_dot(d_scores, head_lanes(query, head)),
+            plain_dot(probs.astype(bf16), d_head),
         )
         if d_query is None:
             d_query, d_key, d_value = terms
@@ -1509,7 +1625,10 @@
     d_query = turn(d_query * HD ** (-0.5), picked_tables, -1.0).astype(bf16)
     d_key = turn(d_key * HD ** (-0.5), tables, -1.0).astype(bf16)
     d_value = d_value.astype(bf16)
-    unit, _ = centred_rows(residual[...].astype(jnp.float32))
+    unit, unit_scale = centred_rows(residual[...].astype(jnp.float32))
+    unit_rows[...] = unit
+    feats = own_unit.shape[1]
+    own_unit[...] = unit_rows[:, pl.ds(pl.multiple_of(lax.axis_index("shard") * feats, feats), feats)]
     low_one = (unit * gain_one + shift_one).astype(bf16)
     two, three = 2 * HEAD_COLS, 3 * HEAD_COLS
     grad_in[:, :HEAD_COLS] += first_dot(picked_one[...], d_query)
@@ -1525,31 +1644,32 @@
     grad_bias[0:1, two:three] += column_sum(d_value)
     grad_bias[0:1, three:] += column_sum(d_hidden)
     d_normed = (
-        transposed_dot(first_dot(pick, d_query).astype(bf16), weights[:, :HEAD_COLS])
+        transposed_dot(plain_dot(pick, d_query).astype(bf16), weights[:, :HEAD_COLS])
         + transposed_dot(d_key, weights[:, HEAD_COLS:two])
         + transposed_dot(d_value, weights[:, two:three])
     )
     d_unit = d_normed * gain_one
     grad_scales[0:1, :] += column_sum(d_normed * unit)
     grad_scales[1:2, :] += column_sum(d_normed)
-    d_normed = transposed_dot(first_dot(pick, d_hidden).astype(bf16), weights[:, three:])
+    d_normed = transposed_dot(plain_dot(pick, d_hidden).astype(bf16), weights[:, three:])
     grad_scales[2:3, :] += column_sum(d_normed * unit)
     grad_scales[3:4, :] += column_sum(d_normed)
     d_unit = d_unit + d_normed * gain_two
     sum_one = jnp.sum(d_unit, axis=-1, keepdims=True)
     sum_two = jnp.sum(d_unit * unit, axis=-1, keepdims=True)
+    steps = jnp.max(jnp.abs(d_unit), axis=-1, keepdims=True) * (1.0 / 32767.0)
     lane = lax.broadcasted_iota(jnp.int32, (tokens, 128), 1)
-    both = jnp.where(lane == 0, sum_one, jnp.where(lane == 1, sum_two, 0.0))
-    stats[...] = both.T[:8, :]
-    feats = unit_parts.shape[2]
+    columns = jnp.where(lane == 0, sum_one, jnp.where(lane == 1, sum_two, jnp.where(lane == 2, steps, unit_scale)))
+    stats[...] = columns.T[:8, :]
+    codes = coded(d_unit, steps)
     for part in range(unit_parts.shape[0]):
-        unit_parts[part] = d_unit[:, part * feats : (part + 1) * feats]
-
-
-def layer_backward(spans, residual, places, scales, tables, weights, back, kept, d_branch):
+        unit_parts[part] = codes[:, part * feats : (part + 1) * feats]
+
+
+def layer_backward(spans, residual, places, scales, tables, weights, back, kept, d_branch, d_after):
     lines = spans.shape[0]
     count, depth = residual.shape
-    tokens, slots = count // lines, places.shape[0] // lines
+    tokens, slots = count // lines, places.shape[1]
     feats = depth // SG
     f32 = jnp.float32
     whole = lambda height, width: pl.BlockSpec((height, width), lambda line: (0, 0))
@@ -1559,32 +1679,38 @@
         in_specs=[
             pl.BlockSpec(memory_space=pltpu.SMEM),
             line_block(tokens, depth),
-            line_block(slots, 1),
+            line_block(8, slots),
             still(scales),
             *[still(table) for table in tables],
             still(weights),
             still(back),
             *[line_block(array.shape[0] // lines, array.shape[1]) for array in kept],
             line_block(slots, depth),
+            line_block(slots, feats),
         ],
         out_specs=[
             pl.BlockSpec((SG, tokens, feats), lambda line: (0, line, 0)),
             pl.BlockSpec((8, tokens), lambda line: (0, line)),
+            line_block(tokens, feats),
+            line_block(tokens, feats),
             whole(depth, OWN_COLS),
             whole(HEAD_COLS + UNITS, depth),
             whole(8, depth),
             whole(8, OWN_COLS),
         ],
         out_shape=[
-            jax.ShapeDtypeStruct((SG, count, feats), f32),
+            jax.ShapeDtypeStruct((SG, count, feats), jnp.int16),
             jax.ShapeDtypeStruct((8, count), f32),
+            jax.ShapeDtypeStruct((count, feats), f32),
+            jax.ShapeDtypeStruct((count, feats), f32),
             jax.ShapeDtypeStruct((depth, OWN_COLS), f32),
             jax.ShapeDtypeStruct((HEAD_COLS + UNITS, depth), f32),
             jax.ShapeDtypeStruct((8, depth), f32),
             jax.ShapeDtypeStruct((8, OWN_COLS), f32),
         ],
+        scratch_shapes=[pltpu.VMEM((tokens, depth), f32)],
         compiler_params=pltpu.CompilerParams(vmem_limit_bytes=VMEM_LIMIT),
-    )(spans, residual, places, scales, *tables, weights, back, *kept, d_branch)
+    )(spans, residual, places, scales, *tables, weights, back, *kept, d_branch, d_after)
 
 
 def group_plan(
@@ -1632,37 +1758,12 @@
     small_low = small_params.astype(bf16).astype(jnp.float32).reshape(-1, 128)
     small_rows = small_low.shape[0]
     smalls = jnp.pad(small_low, ((0, 16 - small_rows), (0, 0)))
-    in_low = proj_in.astype(bf16)
-    qkv_parts = in_low[:, : 3 * D].reshape(D // SG, 3, SG, HEAD_COLS)
-    in_parts = jnp.concatenate(
-        [
-            jnp.transpose(qkv_parts, (2, 0, 1, 3)).reshape(SG, D // SG, 3 * HEAD_COLS),
-            jnp.transpose(in_low[:, 3 * D :].reshape(D // SG, SG, UNITS), (1, 0, 2)),
-        ],
-        axis=2,
-    ).reshape(SG, 2, D // SG // 2, OWN_COLS)
-    back_tiles = proj_back.astype(bf16).reshape(5, 2, 64, D)
-    ints_all, smalls_all, residual_low, in_all, back_all = share_entry(
-        ints, smalls, in_parts, back_tiles, embed_table, tokens, 1
+    ints_all, scales, own_bias, residual_low, in_all, back_all, head_low = share_entry(
+        ints, smalls, proj_in, proj_back, embed_table, head_table.T, tokens, 1
     )
     own_in = in_all.reshape(D, OWN_COLS)
     own_back = back_all.reshape(5 * 128, D)
-    wide_small = smalls_all[:, :small_rows].reshape(-1)
-    (
-        gain_one,
-        shift_one,
-        gain_two,
-        shift_two,
-        gain_last,
-        shift_last,
-        bias_qkv,
-        bias_hidden,
-        bias_out,
-    ) = split_small(wide_small)
-    head_cols = [
-        lax.dynamic_slice(bias_qkv, (part * D + shard_at * HEAD_COLS,), (HEAD_COLS,)) for part in range(3)
-    ]
-    own_hidden = lax.dynamic_slice(bias_hidden, (shard_at * UNITS,), (UNITS,))
+    gain_last, shift_last, bias_out = scales[4], scales[5], scales[6]
 
     by_group = ints_all.reshape(RG, RG, SG // RG, 8, seq_dev)
     ids_all = jnp.transpose(by_group[:, :, :, :micro], (1, 3, 2, 0, 4)).reshape(RG, tokens)
@@ -1677,12 +1778,11 @@
     counted_group = lax.dynamic_index_in_dim(counted_all, rep_at, 0, False)
     spans = lax.dynamic_index_in_dim(by_group[0, :, :, 3, :micro], rep_at, 0, False).T.reshape(lines)
 
-    block_starts = (jnp.arange(blocks) % RG * seq_dev)[:, None]
-    slot_places = pos_group.reshape(blocks, slots)
-    slot_places = jnp.where(slot_places < seq_dev, slot_places + block_starts, -1).reshape(slot_count, 1)
+    slot_places = pos_group.reshape(lines, RG, slots)
+    block_starts = (jnp.arange(RG) * seq_dev)[None, :, None]
+    slot_places = jnp.where(slot_places < seq_dev, slot_places + block_starts, -1).reshape(lines, 1, RG * slots)
+    slot_places = jnp.broadcast_to(slot_places, (lines, 8, RG * slots)).reshape(lines * 8, RG * slots)
     tables = turn_tables(jnp.arange(seq_len).astype(jnp.float32))
-    scales = jnp.stack([gain_one, shift_one, gain_two, shift_two] + [jnp.zeros_like(gain_one)] * 4)
-    own_bias = jnp.concatenate(head_cols + [own_hidden])[None]
     *kept, picked_rows, branch_parts = layer_forward(
         spans, residual_low, slot_places, scales, own_bias, tables, own_in, own_back
     )
@@ -1695,22 +1795,23 @@
     picked = (final_rows * own_used[:, None]).astype(bf16)
     rows_group = shard_gather(picked, 4)
 
-    head_turned = head_table.T
-    stats, head_low = logit_stats(rows_group, targets_group[None], head_turned)
+    stats = logit_stats(rows_group, targets_group[None], head_low)
     stats_all = shard_stats(stats, 5)
     tops = stats_all[:, 0]
     top = jnp.max(tops, axis=0)
     logsum = top + jnp.log(jnp.sum(stats_all[:, 1] * jnp.exp(tops - top), axis=0))
     row_target = jnp.sum(stats_all[:, 2], axis=0)
+    row_loss = jnp.where(counted_group > 0.0, logsum - row_target, 0.0)
+    logsum = jnp.where(counted_group > 0.0, logsum, 1e30)
     facts = jnp.concatenate(
-        [logsum[None], counted_group[None], row_target[None], jnp.zeros((5, slot_count), jnp.float32)]
-    )
-    picked_parts = picked_grads(rows_group, facts.T, targets_group[:, None], head_low)
+        [logsum[None], row_loss[None], counted_group[None], jnp.zeros((5, slot_count), jnp.float32)]
+    )
+    picked_parts = picked_grads(rows_group, facts, targets_group[None], head_low)
     d_picked, rows_all, facts_all = sum_and_share(
         picked_parts.reshape(SG, own_slots, D), rows_group, facts, 6
     )
-    loss_sum = jnp.sum((facts_all[:, 0] - facts_all[:, 2]) * facts_all[:, 1])
-    count_sum = jnp.sum(facts_all[:, 1])
+    loss_sum = jnp.sum(facts_all[:, 1])
+    count_sum = jnp.sum(facts_all[:, 2])
     targets_wide = jnp.broadcast_to(targets_all[:, None, :], (RG, 8, slot_count))
 
     d_after, d_gain_last, d_shift_last = pull_last(d_picked)
@@ -1720,8 +1821,8 @@
     d_branch, after_pieces = share_branch(d_branch_own, pieces, 7)
     d_after_feats = after_pieces.reshape(slot_count, D // SG)
 
-    unit_parts, norm_stats, grad_in, grad_back, grad_scales, grad_bias = layer_backward(
-        spans, residual_low, slot_places, scales, tables, own_in, own_back, kept, d_branch
+    unit_parts, norm_stats, base, own_unit, grad_in, grad_back, grad_scales, grad_bias = layer_backward(
+        spans, residual_low, slot_places, scales, tables, own_in, own_back, kept, d_branch, d_after_feats
     )
 
     def whole(columns, length):
@@ -1741,29 +1842,20 @@
     grad_small = jnp.pad(grad_small.reshape(SG, small_rows, 128), ((0, 0), (0, 16 - small_rows), (0, 0)))
     in_quarters = jnp.transpose(grad_in.reshape(SG, RG, quarter, OWN_COLS), (1, 0, 2, 3))
     back_quarters = jnp.transpose(grad_back.reshape(5, RG, 32, D), (1, 0, 2, 3))
-    d_unit_feats, norm_stats_all, in_sum, back_sum, small_sum, grad_head, head_squares = layer_sums(
-        unit_parts, norm_stats, in_quarters, back_quarters, grad_small, rows_all, facts_all, targets_wide, head_low, 8
-    )
-
-    norm_sums = jnp.sum(norm_stats_all, axis=0)
-    residual = residual_low.astype(jnp.float32)
-    row_mean = jnp.mean(residual, axis=-1, keepdims=True)
-    centred = residual - row_mean
-    unit_scale = lax.rsqrt(jnp.mean(centred * centred, axis=-1, keepdims=True) + NORM_EPS)
-    own_unit = lax.dynamic_slice_in_dim(residual_low, shard_at * (D // SG), D // SG, 1).astype(jnp.float32)
-    own_unit = (own_unit - row_mean) * unit_scale
-    d_rows = (
-        d_unit_feats - norm_sums[0][:, None] / D - own_unit * (norm_sums[1][:, None] / D)
-    ) * unit_scale
-    pick = (pos_group.reshape(blocks, slots, 1) == jnp.arange(seq_dev)[None, None, :]).astype(jnp.float32)
-    d_after_rows = jnp.einsum(
-        "bst,bsd->btd",
-        pick,
-        d_after_feats.reshape(blocks, slots, D // SG),
-        precision=lax.Precision.HIGHEST,
-    ).reshape(tokens, D // SG)
-    d_rows = (d_after_rows + d_rows).astype(bf16)
-    d_rows_all, in_own, back_own = return_sums(d_rows, in_sum, back_sum, 9)
+    d_rows_all, in_own, back_own, small_sum, grad_head, head_squares = layer_sums(
+        unit_parts,
+        norm_stats,
+        base,
+        own_unit,
+        in_quarters,
+        back_quarters,
+        grad_small,
+        rows_all,
+        facts_all,
+        targets_wide,
+        head_low,
+        8,
+    )
     in_grads = lax.all_gather(in_own, "rep")
     back_grads = lax.all_gather(back_own, "rep")
     grad_embed, embed_squares = embed_grads(ids_all.reshape(-1), d_rows_all.reshape(RG * tokens, D // SG), vocab)

time: 792 us -> 670 us (0.85)
  Pallas kernels: 541 us -> 444 us
  other arithmetic: 171 us -> 159 us
  local copies, waits for them, and re-layouts: 47.5 us -> 37.8 us
    pallas_call x9 -> x8, Pallas kernels: 406 us -> 319 us  [comm_call(): pl.pallas_call(kernel, grid=grid, out_shape=out_shape, in_specs=[choose(s...]
    pallas_call x1, Pallas kernels: 22.3 us -> 13.1 us  [logit_stats(): pl.pallas_call(functools.partial(top_kernel, vocab), grid=(pl.cdiv(vocab,...]
  transfers between devices with their start and end apart: 2 -> 2, of which waited for: 0 -> 0; matrix products, arithmetic and copies ran while one was open for 18% -> 22% of each run, Pallas kernels for 8% -> 8%
where the time goes in v3:
time: 670 us; the launch traced here: 662 us
  Pallas kernels  444 us (66%)
  other arithmetic  159 us (24%)
  local copies, waits for them, and re-layouts  37.8 us (6%)
  between operations  20.1 us (3%)
    pallas_call x8, Pallas kernels, comm_call(): pl.pallas_call(kernel, grid=grid, out_shape=out_shape, in_specs=[choose(s...  319 us
    sub x5, other arithmetic, adamw(): weight - rate_value * (moment_hat / (jnp.sqrt(square_hat) + ADAM_EPS) + D...  133 us
    pallas_call x1, Pallas kernels, embed_grads(): pl.pallas_call(embed_grad_kernel, grid=(blocks,), in_specs=[pl.BlockSpec(...  42.3 us
    pallas_call x1, Pallas kernels, layer_backward(): pl.pallas_call(backward_kernel, grid=(lines,), in_specs=[pl.BlockSpec(mem...  33.8 us
    pallas_call x1, Pallas kernels, picked_grads(): pl.pallas_call(functools.partial(rows_kernel, vocab), grid=(pl.cdiv(vocab...  20.3 us
    pallas_call x1, Pallas kernels, layer_forward(): pl.pallas_call(forward_kernel, grid=(lines,), in_specs=[pl.BlockSpec(memo...  15.9 us
    unnamed x48, local copies, waits for them, and re-layouts  13.6 us
  transfers between devices with their start and end apart: 2, of which 0 were waited for; matrix products, arithmetic and copies ran while one was open for 22% of the time, Pallas kernels for 8%

profile of v3, /device:TPU:0, one launch (start us, length us, event | category | flops | bytes accessed | tf_op | source)
XLA Modules:
  0.0 661.7 jit_solution(12435975107630559786)
XLA Ops:
  7.8 1.3 reduce.11
  9.2 1.3 reduce.12
  12.7 1.3 add_add_fusion.2.ints
  14.1 75.0 %shard_map.314 = (s32[4,8,8,128]{3,2,1,0:T(8,128)}, f32[8,1024]{1,0:T(8,128)}, f32[1,896]{1,0:T(1,128)}, bf16[2048,1024]{1,0:T(8,128)(2,1)}, bf16[8,4,32,896]{3,...) custom-call(s32[8,128]{1,0:T(8,128)} %add_add_fusion.2.ints, ...), custom_call_target="tpu_custom_call" | custom-call | tf_op jit(solution)/shard_map/pallas_call | solution.py:436
  89.1 0.9 slice.92
  90.0 0.8 slice.91
  92.6 0.9 fusion.33
  93.5 1.9 fusion.6
  95.4 15.9 %shard_map.315 = (bf16[512,128]{1,0:T(8,128)(2,1)}, bf16[2048,128]{1,0:T(8,128)(2,1)}, bf16[2048,128]{1,0:T(8,128)(2,1)}, f32[512,512]{1,0:T(8,128)}, bf16[512,6...) custom-call(s32[4]{0:T(128)} %reshape.263.spans, ...), custom_call_target="tpu_custom_call" | custom-call | tf_op jit(solution)/shard_map/pallas_call | solution.py:1559
  111.4 1.6 copy-done.3
  112.9 34.0 %shard_map.316 = f32[64,1024]{1,0:T(8,128)S(1)} custom-call(f32[8,64,1024]{2,1,0:T(8,128)S(1)} %bitcast.123), custom_call_target="tpu_custom_call" | custom-call | tf_op jit(solution)/shard_map/pallas_call | solution.py:436
  147.0 1.0 fusion.32
  148.5 0.8 multiply_convert_fusion.rows
  149.2 19.3 %shard_map.317.rows = bf16[512,1024]{1,0:T(8,128)(2,1)} custom-call(bf16[64,1024]{1,0:T(8,128)(2,1)} %multiply_convert_fusion.rows), custom_call_target="tpu_custom_call" | custom-call | tf_op jit(solution)/shard_map/pallas_call | solution.py:436
  169.2 13.1 %shard_map.318.stats = f32[8,512]{1,0:T(8,128)} custom-call(bf16[512,1024]{1,0:T(8,128)(2,1)} %shard_map.317.rows, s32[1,512]{1,0:T(1,128)} %constant_dynamic-slice_fusion.targets, bf16[6288,1024]{1,0:T(8,128)(2,1)} %get-tuple-element.62.head), custom_call_target="tpu_custom_call" | custom-call | tf_op jit(solution)/shard_map/pallas_call | solution.py:1322
  182.3 10.6 %shard_map.319 = f32[8,8,512]{2,1,0:T(8,128)} custom-call(f32[8,512]{1,0:T(8,128)} %shard_map.318.stats), custom_call_target="tpu_custom_call" | custom-call | tf_op jit(solution)/shard_map/pallas_call | solution.py:436
  192.9 1.1 slice_reduce_fusion
  194.9 20.3 %shard_map.320 = f32[512,1024]{1,0:T(8,128)} custom-call(bf16[512,1024]{1,0:T(8,128)(2,1)} %shard_map.317.rows, f32[8,512]{1,0:T(8,128)} %maximum_maximum_fusion.facts, s32[1,512]{1,0:T(1,128)} %constant_dynamic-slice_fusion.targets, bf16[6288,1024]{1,0:T(8,128)(2,1)} %get-tuple-element.62.head), custom_call_target="tpu_custom_call" | custom-call | tf_op jit(solution)/shard_map/pallas_call | solution.py:1362
  215.2 1.6 copy-done.1
  216.8 37.4 %shard_map.321 = (f32[64,1024]{1,0:T(8,128)S(1)}, bf16[4,512,1024]{2,1,0:T(8,128)(2,1)S(1)}, f32[4,8,512]{2,1,0:T(8,128)S(1)}) custom-call(f32[8,64,1024]{2,1,0:T(8,128)S(1)} %bitcast.122, bf16[512,1024]{1,0:T(8,128)(2,1)S(1)} %copy-done, f32[8,512]{1,0:T(8,128)S(1)} %copy-done.4), custom_call_target="tpu_custom_call" | custom-call | tf_op jit(solution)/shard_map/pallas_call | solution.py:436
  254.2 2.0 copy-done.2
  258.3 23.5 %shard_map.322 = (bf16[512,1024]{1,0:T(8,128)(2,1)}, f32[8,64,128]{2,1,0:T(8,128)}) custom-call(bf16[64,1024]{1,0:T(8,128)(2,1)} %get-tuple-element.114.rows, f32[8,64,128]{2,1,0:T(8,128)} %bitcast.142), custom_call_target="tpu_custom_call" | custom-call | tf_op jit(solution)/shard_map/pallas_call | solution.py:436
  281.8 33.8 %shard_map.323 = (s16[8,2048,128]{2,1,0:T(8,128)(2,1)}, f32[8,2048]{1,0:T(8,128)}, f32[2048,128]{1,0:T(8,128)}, f32[2048,128]{1,0:T(8,128)}, f32[1024,896]{1,0:T...) custom-call(s32[4]{0:T(128)} %reshape.263.spans, ...), custom_call_target="tpu_custom_call" | custom-call | tf_op jit(solution)/shard_map/pallas_call | solution.py:1676
  318.6 0.8 bitcast_dynamic-update-slice_fusion.1
  319.7 4.3 copy.113
  324.1 1.8 copy.114
  327.1 105.2 %shard_map.324 = (bf16[4,2048,128]{2,1,0:T(8,128)(2,1)}, f32[8,32,896]{2,1,0:T(8,128)}, f32[5,32,1024]{2,1,0:T(8,128)}, f32[16,128]{1,0:T(8,128)}, f32[6288,1024]{1,0:T(8,128)}, /*index=5*/f32[8,1024]{1,0:T(8,128)}) custom-call(s16[8,2048,128]{2,1,0:T(8,128)(2,1)} %get-tuple-element.74.parts, f32[8,2048]{1,0:T(8,128)} %get-tuple-element.75.stats, ...), custom_call_target="tpu_custom_call" | custom-call | tf_op jit(solution)/shard_map/pallas_call | solution.py:436
  433.1 0.9 slice.95
  434.0 2.0 multiply_reduce_fusion
  436.0 1.9 multiply_reduce_fusion.1
  437.9 1.5 slice_reduce_fusion.2
  440.1 1.3 multiply_reduce_fusion.5
  441.4 42.3 %shard_map.325 = (f32[128,50304]{1,0:T(8,128)}, f32[8,128]{1,0:T(8,128)}) custom-call(s32[8192]{0:T(1024)} %bitcast.145, bf16[8192,128]{1,0:T(8,128)(2,1)} %bitcast.141), custom_call_target="tpu_custom_call" | custom-call | tf_op jit(solution)/shard_map/pallas_call | solution.py:1406
  483.7 1.3 reduce_sum.176
  489.5 13.7 %shard_map.326 = f32[8,128]{1,0:T(8,128)} custom-call(f32[8,128]{1,0:T(8,128)} %broadcast_in_dim.111.value), custom_call_target="tpu_custom_call" | custom-call | tf_op jit(solution)/shard_map/pallas_call | solution.py:436
  503.1 1.2 slice.88
  505.0 1.9 pad_maximum_fusion
  507.6 60.9 %multiply_subtract_fusion = (f32[128,50304]{1,0:T(8,128)}, f32[128,50304]{1,0:T(8,128)}, f32[128,50304]{1,0:T(8,128)}) fusion(f32[128,50304]{1,0:T(8,128)} %table.1, f32[128,50304]{1,0:T(8,128)} %get-tuple-element.90, f32[]{:T(128)} %bitcast.44, f32[128,50304]{1,0:T(8,128)} %param.36, f32[128,50304]{1,0:T(8,128)} %param.37), kind=kLoop, calls=%fused_computation.6 | loop fusion | flops 103022592 | bytes 180289536 | tf_op jit(solution)/shard_map/sub | solution.py:104
  568.5 61.7 %multiply_subtract_fusion.1 = (f32[1024,6288]{0,1:T(8,128)}, f32[1024,6288]{0,1:T(8,128)}, f32[1024,6288]{0,1:T(8,128)}) fusion(f32[1024,6288]{0,1:T(8,128)} %param.26, f32[6288,1024]{1,0:T(8,128)} %get-tuple-element.89, f32[]{:T(128)} %bitcast.44, f32[1024,6288]{0,1:T(8,128)} %param.34, f32[1024,6288]{0,1:T(8,128)} %param.35), kind=kLoop, calls=%fused_computation.8 | loop fusion | flops 103022592 | bytes 180289536 | tf_op jit(solution)/shard_map/sub | solution.py:104
  630.2 2.1 broadcast_multiply_fusion
  632.7 1.4 copy-done.7
  634.2 0.8 copy-done.10
  634.9 4.7 multiply_subtract_fusion.3
  639.7 4.2 copy.84
  644.3 1.7 copy.96
  646.3 0.8 copy-done.6
  647.1 1.0 copy-done.8
  648.2 5.2 multiply_subtract_fusion.2
  (109 shorter events, 17.4 us)
Async XLA Ops:
  7.2 623.0 %all-gather.7.cloned.1.call-start = ((), (), s32[]{:S(2)}) async-start(), calls=%async_computation.1 | async-start | bytes 3276800 | tf_op jit(solution)/shard_map/all_gather | solution.py:1860
  111.3 1.6 copy-start.3
  194.9 20.4 %copy-start = (bf16[512,1024]{1,0:T(8,128)(2,1)S(1)}, bf16[512,1024]{1,0:T(8,128)(2,1)}, u32[]{:S(2)}) copy-start(bf16[512,1024]{1,0:T(8,128)(2,1)} %shard_map.317.rows) | copy-start | bytes 3145732
  194.9 20.4 %copy-start.4 = (f32[8,512]{1,0:T(8,128)S(1)}, f32[8,512]{1,0:T(8,128)}, u32[]{:S(2)}) copy-start(f32[8,512]{1,0:T(8,128)} %maximum_maximum_fusion.facts) | copy-start | bytes 49156
  215.2 1.6 copy-start.1
  254.2 2.0 copy-start.2
  256.2 0.6 copy-start.5
  319.7 4.3 copy-start.12
  432.3 52.7 %copy-start.15 = (f32[8,1024]{1,0:T(8,128)S(1)}, f32[8,1024]{1,0:T(8,128)}, u32[]{:S(2)}) copy-start(f32[8,1024]{1,0:T(8,128)} %get-tuple-element.84) | copy-start | bytes 98308
  432.3 74.6 %copy-start.13 = (f32[1792]{0:T(1024)S(1)}, f32[1792]{0:T(1024)}, u32[]{:S(2)}) copy-start(f32[1792]{0:T(1024)} %param.25) | copy-start | bytes 21508
  432.3 74.6 %copy-start.14 = (f32[16,128]{1,0:T(8,128)S(1)}, f32[16,128]{1,0:T(8,128)}, u32[]{:S(2)}) copy-start(f32[16,128]{1,0:T(8,128)} %get-tuple-element.83) | copy-start | bytes 24580
  432.3 74.6 %copy-start.16 = (f32[1792]{0:T(1024)S(1)}, f32[1792]{0:T(1024)}, u32[]{:S(2)}) copy-start(f32[1792]{0:T(1024)} %param.32) | copy-start | bytes 21508
  432.3 74.6 %copy-start.17 = (f32[1792]{0:T(1024)S(1)}, f32[1792]{0:T(1024)}, u32[]{:S(2)}) copy-start(f32[1792]{0:T(1024)} %param.33) | copy-start | bytes 21508
  432.4 207.3 %all-gather.5.cloned.1.call-start = ((), (), s32[]{:S(2)}) async-start(), calls=%async_computation | async-start | bytes 4587520 | tf_op jit(solution)/shard_map/all_gather | solution.py:1859
  630.2 2.5 copy-start.11
  632.3 1.8 copy-start.7
  632.3 2.6 copy-start.10
  643.9 2.4 copy-start.9
  644.3 2.9 copy-start.6
  644.3 3.9 copy-start.8
Sparse Core Ops, SparseCore 0:
  432.5 28.3 all-gather.6
  462.4 31.4 all-gather.4

commit v4 on v3

--- a/solution.py
+++ b/solution.py
@@ -504,8 +504,8 @@
 
 
 def entry_kernel(
-    table_steps, ints, smalls, weights_in, weights_back, table, head,
-    ints_out, scales, bias, out, in_all, back_all, head_low,
+    table_steps, head_rows, ints, smalls, weights_in, weights_back, table, head,
+    ints_out, places, marks, scales, bias, out, in_all, back_all, head_low,
     ints_all, smalls_all, in_parts, back_tiles, turned, wide, low, ids,
     send_int, recv_int, send_small, recv_small, send_rep, recv_rep,
     send_in, recv_in, send_back, recv_back, send_far, recv_far, send_pair, recv_pair,
@@ -700,6 +700,28 @@
             copy.wait()
         ints_out[...] = ints_all[...]
 
+        seq_dev, slots = ints.shape[1], ints.shape[1] // 4
+        for group in range(RG):
+            for line in range(lines):
+                micro, member = line // 2, line % 2
+                for block_at in range(RG):
+                    facts = ints_all[block_at, 2 * group + member, 2:3, :]
+                    where = facts[:, slots * micro : slots * (micro + 1)]
+                    goal = facts[:, slots * (2 + micro) : slots * (3 + micro)]
+                    some = where < seq_dev
+                    start = (line * RG + block_at) * slots
+                    marks[group, 0:1, start : start + slots] = jnp.where(some, goal - shard * head_rows, -1)
+                    marks[group, 1:2, start : start + slots] = some.astype(jnp.int32)
+        for line in range(lines):
+            micro, member = line // 2, line % 2
+            for block_at in range(RG):
+                where = ints_all[block_at, 2 * rep + member, 2:3, slots * micro : slots * (micro + 1)]
+                places[8 * line : 8 * line + 1, block_at * slots : (block_at + 1) * slots] = jnp.where(
+                    where < seq_dev, where + block_at * seq_dev, -1
+                )
+            span = ints_all[0, 2 * rep + member, 3:4, micro : micro + 1]
+            places[8 * line + 1 : 8 * line + 2, :] = jnp.broadcast_to(span, (1, places.shape[1]))
+
         def small_row(row):
             return smalls_all[row // small_rows, pl.ds(lax.rem(row, small_rows), 1), :]
 
@@ -743,9 +765,11 @@
         lambda at: (jnp.clip(at - blocks, 0, pl.cdiv(head.shape[0], CAST_BLOCK) - 1), 0),
     )
     return comm_call(
-        functools.partial(entry_kernel, blocks),
+        functools.partial(entry_kernel, blocks, head.shape[0]),
         [
             jax.ShapeDtypeStruct((RG, SG) + ints.shape, ints.dtype),
+            jax.ShapeDtypeStruct((8 * lines, ints.shape[1]), ints.dtype),
+            jax.ShapeDtypeStruct((RG, 8, ints.shape[1] * lines), ints.dtype),
             jax.ShapeDtypeStruct((8, SG * feats), jnp.float32),
             jax.ShapeDtypeStruct((1, OWN_COLS), jnp.float32),
             jax.ShapeDtypeStruct((tokens, SG * feats), jnp.bfloat16),
@@ -775,202 +799,232 @@
         number,
         (ints, smalls, weights_in, weights_back, table, head),
         ["v", "v", "v", "v", pl.BlockSpec((feats, TABLE_BLOCK), lambda at: (0, jnp.minimum(at, blocks - 1))), head_spec],
-        ["v", "v", "v", "a", "a", "a", head_spec],
+        ["v"] * 5 + ["a", "a", "a", head_spec],
         VMEM_LIMIT,
         (blocks + head_blocks,),
     )
 
 
-def gather_kernel(rows, out, *sems):
+def loss_kernel(
+    vocab, parts, picked_rows, scales, used, marks, head,
+    rows_all, facts_out, branch, features_out, vectors,
+    rows, turned, low, after, branch_y, branch_sum, branch_z, picked_y, picked_sum, picked_z, picked,
+    stats, stats_all, facts, facts_all, features, pieces, low_branch, top, total, target,
+    branch_send_y, branch_recv_y, branch_send_z, branch_recv_z,
+    picked_send_y, picked_recv_y, picked_send_z, picked_recv_z,
+    row_z_send, row_z_recv, row_y_send, row_y_recv, row_own,
+    back_z_send, back_z_recv, back_y_send, back_y_recv, back_own,
+    send_stat, recv_stat, send_row, recv_row, send_fact, recv_fact, send_feat, recv_feat, own,
+):
+    at = pl.program_id(0)
+    blocks = pl.num_programs(0) // 2
     place = whereabouts()
-    greet(gather_partners(place))
-    started = start_gather(rows, out, row_slot, place, sems)
-    finish_gather(started, out, row_slot, place, sems)
-
-
-def shard_gather(rows, number):
+    rep, shard, core_twin, x_twin, y_twin = place
+    shard_peers = [(rep, shard_peer(shard, step)) for step in range(1, SG)]
+    rep_peers = [(lax.rem(rep + step, RG), shard) for step in range(1, RG)]
+    slots = after.shape[0]
+    own_rows = pl.ds(pl.multiple_of(shard * slots, slots), slots)
+
+    def shard_total(values, from_y, own_sum, from_z, send_y, recv_y, send_z, recv_z):
+        y_copies = {}
+        for step in (2, 1, 3, 0):
+            y_copies[step] = remote(
+                values.at[z_peer(y_twin, step)], from_y.at[step], send_y.at[step], recv_y.at[step], (rep, y_twin)
+            )
+            y_copies[step].start()
+        z_copies = []
+        for step in (2, 1, 3):
+            y_copies[step].wait_recv()
+            own_sum[step] = values[z_peer(shard, step)] + from_y[step]
+            z_copies.append(
+                remote(
+                    own_sum.at[step], from_z.at[step - 1], send_z.at[step - 1], recv_z.at[step - 1],
+                    (rep, z_peer(shard, step)),
+                )
+            )
+            z_copies[-1].start()
+        y_copies[0].wait_recv()
+        result = values[shard] + from_y[0]
+        for copy in z_copies:
+            copy.wait()
+        for step in range(4):
+            y_copies[step].wait_send()
+        return result + from_z[0] + from_z[1] + from_z[2]
+
+    row_sems = (row_z_send, row_z_recv, row_y_send, row_y_recv, row_own)
+    back_sems = (back_z_send, back_z_recv, back_y_send, back_y_recv, back_own)
+
+    def stat_copies():
+        return [
+            remote(stats, stats_all.at[shard], send_stat.at[k], recv_stat.at[k], peer)
+            for k, peer in enumerate(shard_peers)
+        ]
+
+    def row_copy(k, peer):
+        return remote(rows, rows_all.at[rep], send_row.at[k], recv_row.at[k], (peer, shard))
+
+    def passed_copy():
+        return remote(rows_all.at[x_twin], rows_all.at[x_twin], send_row.at[2], recv_row.at[2], (core_twin, shard))
+
+    def keep_rows():
+        return pltpu.make_async_copy(rows, rows_all.at[rep], own)
+
+    def fact_copies():
+        return [
+            remote(facts, facts_all.at[rep], send_fact.at[k], recv_fact.at[k], peer) for k, peer in enumerate(rep_peers)
+        ]
+
+    @pl.when(at == 0)
+    def _():
+        greet(shard_peers + rep_peers)
+        sum_buffers = (branch_y, branch_sum, branch_z)
+        whole = shard_total(parts, *sum_buffers, branch_send_y, branch_recv_y, branch_send_z, branch_recv_z)
+        after[...] = picked_rows[own_rows, :].astype(jnp.float32) + whole + scales[6:7, :]
+        unit, _ = centred_rows(after[...])
+        final = unit * scales[4:5, :] + scales[5:6, :]
+        low[...] = (final * used[own_rows, 0:1]).astype(low.dtype)
+        started = start_gather(low, rows, row_slot, place, row_sems)
+        finish_gather(started, rows, row_slot, place, row_sems)
+        row_copy(0, x_twin).start()
+        row_copy(1, core_twin).start()
+        keep_rows().start()
+        turned[...] = rows[...].T
+        top[...] = jnp.full_like(top, -1e30)
+        total[...] = jnp.zeros_like(total)
+        target[...] = jnp.zeros_like(target)
+        picked[...] = jnp.zeros_like(picked)
+
+    full, tail = divmod(vocab, ROW_BLOCK)
+
+    def each_block(start, body):
+        pl.when((at >= start) & (at < start + full))(lambda: body(ROW_BLOCK))
+        if tail > 0:
+            pl.when(at == start + full)(lambda: body(tail))
+
+    def top_block(size):
+        logits = plain_dot(head[:size], turned[...])
+        hits = lax.broadcasted_iota(jnp.int32, logits.shape, 0) == marks[rep, 0:1, :] - at * ROW_BLOCK
+        target[...] += jnp.sum(jnp.where(hits, logits, 0.0), axis=0, keepdims=True)
+        highest = jnp.maximum(top[...], jnp.max(logits, axis=0, keepdims=True))
+        weights = jnp.sum(jnp.exp(logits - highest), axis=0, keepdims=True)
+        total[...] = total[...] * jnp.exp(top[...] - highest) + weights
+        top[...] = highest
+
+    each_block(0, top_block)
+
+    @pl.when(at == blocks - 1)
+    def _():
+        stats[...] = jnp.zeros_like(stats)
+        stats[0:1, :] = top[...]
+        stats[1:2, :] = total[...]
+        stats[2:3, :] = target[...]
+        for copy in stat_copies():
+            copy.start()
+        stats_all[shard] = stats[...]
+        for copy in stat_copies():
+            copy.wait()
+        highest = stats_all[0, 0:1, :]
+        for k in range(1, SG):
+            highest = jnp.maximum(highest, stats_all[k, 0:1, :])
+        weights = row_target = jnp.zeros_like(highest)
+        for k in range(SG):
+            weights = weights + stats_all[k, 1:2, :] * jnp.exp(stats_all[k, 0:1, :] - highest)
+            row_target = row_target + stats_all[k, 2:3, :]
+        logsum = highest + jnp.log(weights)
+        some = marks[rep, 1:2, :] > 0
+        facts[...] = jnp.zeros_like(facts)
+        facts[0:1, :] = jnp.where(some, logsum, 1e30)
+        facts[1:2, :] = jnp.where(some, logsum - row_target, 0.0)
+        facts[2:3, :] = some.astype(jnp.float32)
+        for copy in fact_copies():
+            copy.start()
+        facts_all[rep] = facts[...]
+        row_copy(0, x_twin).wait_recv()
+        passed_copy().start()
+
+    def grad_block(size):
+        block = head[:size]
+        grads = logit_grads(block, turned[...], facts[0:1, :], marks[rep, 0:1, :] - (at - blocks) * ROW_BLOCK)
+        picked[...] += first_dot(grads, block).reshape(picked.shape)
+
+    each_block(blocks, grad_block)
+
+    @pl.when(at == pl.num_programs(0) - 1)
+    def _():
+        sum_buffers = (picked_y, picked_sum, picked_z)
+        d_final = shard_total(picked, *sum_buffers, picked_send_y, picked_recv_y, picked_send_z, picked_recv_z)
+        unit, unit_scale = centred_rows(after[...])
+        d_unit = d_final * scales[4:5, :]
+        mean = jnp.mean(d_unit, axis=-1, keepdims=True)
+        slope = jnp.mean(d_unit * unit, axis=-1, keepdims=True)
+        d_after = (d_unit - mean - unit * slope) * unit_scale
+        low_branch[...] = d_after.astype(low_branch.dtype)
+        started = start_gather(low_branch, branch, row_slot, place, back_sems)
+        width = pieces.shape[2]
+        for k in range(SG):
+            pieces[k] = d_after[:, k * width : (k + 1) * width]
+        copies = [
+            remote(pieces.at[peer[1]], features.at[shard], send_feat.at[k], recv_feat.at[k], peer)
+            for k, peer in enumerate(shard_peers)
+        ]
+        for copy in copies:
+            copy.start()
+        features[shard] = pieces[shard]
+        vectors[...] = jnp.zeros_like(vectors)
+        vectors[0:1, :] = jnp.sum(d_final * unit, axis=0, keepdims=True)
+        vectors[1:2, :] = jnp.sum(d_final, axis=0, keepdims=True)
+        vectors[2:3, :] = jnp.sum(low_branch[...].astype(jnp.float32), axis=0, keepdims=True)
+        finish_gather(started, branch, row_slot, place, back_sems)
+        for copy in copies + fact_copies():
+            copy.wait()
+        facts_out[...] = facts_all[...]
+        features_out[...] = features[...]
+        row_copy(0, x_twin).wait_send()
+        row_copy(1, core_twin).wait()
+        passed_copy().wait()
+        keep_rows().wait()
+
+
+def loss_and_branch(parts, picked_rows, scales, used, marks, head, number):
+    dma = pltpu.SemaphoreType.DMA
+    f32, bf16 = jnp.float32, jnp.bfloat16
+    _, slots, depth = parts.shape
+    vocab = head.shape[0]
+    count = SG * slots
+    blocks = pl.cdiv(vocab, ROW_BLOCK)
+    vmem = lambda *shape: pltpu.VMEM(shape, f32)
     return comm_call(
-        gather_kernel,
-        [jax.ShapeDtypeStruct((SG * rows.shape[0], rows.shape[1]), rows.dtype)],
-        GATHER_SEMS,
+        functools.partial(loss_kernel, vocab),
+        [
+            jax.ShapeDtypeStruct((RG, count, depth), bf16),
+            jax.ShapeDtypeStruct((RG, 8, count), f32),
+            jax.ShapeDtypeStruct((count, depth), bf16),
+            jax.ShapeDtypeStruct((SG, slots, depth // SG), f32),
+            jax.ShapeDtypeStruct((8, depth), f32),
+        ],
+        [
+            pltpu.VMEM((count, depth), bf16),
+            pltpu.VMEM((depth, count), bf16),
+            pltpu.VMEM((slots, depth), bf16),
+            vmem(slots, depth),
+        ]
+        + [vmem(rounds, slots, depth) for rounds in (4, 4, 3, 4, 4, 3, SG)]
+        + [vmem(8, count), vmem(SG, 8, count), vmem(8, count), vmem(RG, 8, count)]
+        + [vmem(SG, slots, depth // SG)] * 2
+        + [pltpu.VMEM((slots, depth), bf16)]
+        + [vmem(1, count)] * 3
+        + [dma((4,)), dma((4,)), dma((3,)), dma((3,))] * 2
+        + GATHER_SEMS * 2
+        + [dma((SG - 1,))] * 2
+        + [dma((3,))] * 4
+        + [dma((SG - 1,))] * 2
+        + [dma],
         number,
-        (rows,),
-        "v",
-        "v",
-    )[0]
-
-
-def stats_kernel(stats, out, send, recv):
-    rep, shard, _, _, _ = whereabouts()
-    peers = [(rep, shard_peer(shard, step)) for step in range(1, SG)]
-    greet(peers)
-    copies = [remote(stats, out.at[shard], send.at[at], recv.at[at], peer) for at, peer in enumerate(peers)]
-    for copy in copies:
-        copy.start()
-    out[shard] = stats[...]
-    for copy in copies:
-        copy.wait()
-
-
-def shard_stats(stats, number):
-    dma = pltpu.SemaphoreType.DMA
-    return comm_call(
-        stats_kernel,
-        [jax.ShapeDtypeStruct((SG,) + stats.shape, stats.dtype)],
-        [dma((SG - 1,)), dma((SG - 1,))],
-        number,
-        (stats,),
-        "v",
-        "v",
-    )[0]
-
-
-def sum_sems():
-    dma = pltpu.SemaphoreType.DMA
-    return [dma((4,)), dma((4,)), dma((3,)), dma((3,))]
-
-
-def sum_buffers(chunk):
-    return [pltpu.VMEM((4,) + chunk, jnp.float32), pltpu.VMEM((4,) + chunk, jnp.float32), pltpu.VMEM((3,) + chunk, jnp.float32)]
-
-
-def start_sum(parts, place, buffers, sems):
-    rep, shard, _, _, y_twin = place
-    from_y, own_sum, from_z = buffers
-    send_y, recv_y, send_z, recv_z = sems
-    y_copies = {}
-    for step in (2, 1, 3, 0):
-        y_copies[step] = remote(
-            parts.at[z_peer(y_twin, step)], from_y.at[step], send_y.at[step], recv_y.at[step], (rep, y_twin)
-        )
-        y_copies[step].start()
-    return y_copies
-
-
-def finish_sum(y_copies, parts, out, place, buffers, sems, post=None):
-    rep, shard, _, _, y_twin = place
-    from_y, own_sum, from_z = buffers
-    send_y, recv_y, send_z, recv_z = sems
-    z_copies = []
-    for step in (2, 1, 3):
-        y_copies[step].wait_recv()
-        own_sum[step] = parts[z_peer(shard, step)] + from_y[step]
-        z_copies.append(
-            remote(own_sum.at[step], from_z.at[step - 1], send_z.at[step - 1], recv_z.at[step - 1], (rep, z_peer(shard, step)))
-        )
-        z_copies[-1].start()
-    y_copies[0].wait_recv()
-    total = parts[shard] + from_y[0]
-    for copy in z_copies:
-        copy.wait_recv()
-    out[...] = total + from_z[0] + from_z[1] + from_z[2]
-    for step in range(4):
-        y_copies[step].wait_send()
-    for copy in z_copies:
-        copy.wait_send()
-
-
-def sum_kernel(parts, out, from_y, own_sum, from_z, *sems):
-    place = whereabouts()
-    greet(gather_partners(place))
-    buffers = (from_y, own_sum, from_z)
-    y_copies = start_sum(parts, place, buffers, sems)
-    finish_sum(y_copies, parts, out, place, buffers, sems)
-
-
-def shard_sum(parts, number):
-    chunk = parts.shape[1:]
-    return comm_call(
-        sum_kernel,
-        [jax.ShapeDtypeStruct(chunk, jnp.float32)],
-        sum_buffers(chunk) + sum_sems(),
-        number,
-        (parts,),
-        "v",
-        "v",
-        40 << 20,
-    )[0]
-
-
-def picked_kernel(parts, rows, facts, out, rows_all, facts_all, from_y, own_sum, from_z, *sems):
-    place = whereabouts()
-    rep, shard, core_twin, x_twin, _ = place
-    sum_sem = sems[:4]
-    send_row, recv_row, send_fact, recv_fact, own = sems[4:]
-    rep_peers = [(lax.rem(rep + step, RG), shard) for step in range(1, RG)]
-    greet(gather_partners(place) + rep_peers)
-    buffers = (from_y, own_sum, from_z)
-    y_copies = start_sum(parts, place, buffers, sum_sem)
-    keep = pltpu.make_async_copy(rows, rows_all.at[rep], own)
-    keep.start()
-    to_x = remote(rows, rows_all.at[rep], send_row.at[0], recv_row.at[0], (x_twin, shard))
-    to_core = remote(rows, rows_all.at[rep], send_row.at[1], recv_row.at[1], (core_twin, shard))
-    to_x.start()
-    to_core.start()
-    fact_copies = [
-        remote(facts, facts_all.at[rep], send_fact.at[at], recv_fact.at[at], peer) for at, peer in enumerate(rep_peers)
-    ]
-    for copy in fact_copies:
-        copy.start()
-    facts_all[rep] = facts[...]
-    finish_sum(y_copies, parts, out, place, buffers, sum_sem)
-    to_x.wait_recv()
-    passed = remote(rows_all.at[x_twin], rows_all.at[x_twin], send_row.at[2], recv_row.at[2], (core_twin, shard))
-    passed.start()
-    keep.wait()
-    to_x.wait_send()
-    to_core.wait()
-    for copy in fact_copies:
-        copy.wait()
-    passed.wait()
-
-
-def sum_and_share(parts, rows, facts, number):
-    dma = pltpu.SemaphoreType.DMA
-    chunk = parts.shape[1:]
-    return comm_call(
-        picked_kernel,
-        [
-            jax.ShapeDtypeStruct(chunk, jnp.float32),
-            jax.ShapeDtypeStruct((RG,) + rows.shape, rows.dtype),
-            jax.ShapeDtypeStruct((RG,) + facts.shape, facts.dtype),
-        ],
-        sum_buffers(chunk) + sum_sems() + [dma((3,))] * 4 + [dma],
-        number,
-        (parts, rows, facts),
-        "vvv",
-        "vvv",
-        40 << 20,
-    )
-
-
-def branch_kernel(rows, pieces, out, features, *sems):
-    place = whereabouts()
-    rep, shard, _, _, _ = place
-    send, recv = sems[5:]
-    peers = [(rep, shard_peer(shard, step)) for step in range(1, SG)]
-    greet(peers)
-    started = start_gather(rows, out, row_slot, place, sems[:5])
-    copies = []
-    for at, peer in enumerate(peers):
-        copies.append(remote(pieces.at[peer[1]], features.at[shard], send.at[at], recv.at[at], peer))
-        copies[-1].start()
-    features[shard] = pieces[shard]
-    finish_gather(started, out, row_slot, place, sems[:5])
-    for copy in copies:
-        copy.wait()
-
-
-def share_branch(rows, pieces, number):
-    dma = pltpu.SemaphoreType.DMA
-    return comm_call(
-        branch_kernel,
-        [jax.ShapeDtypeStruct((SG * rows.shape[0], rows.shape[1]), rows.dtype), jax.ShapeDtypeStruct(pieces.shape, pieces.dtype)],
-        GATHER_SEMS + [dma((SG - 1,))] * 2,
-        number,
-        (rows, pieces),
-        "vv",
-        "vv",
+        (parts, picked_rows, scales, used, marks, head),
+        ["v"] * 5 + [pl.BlockSpec((ROW_BLOCK, depth), lambda at: (lax.rem(at, blocks), 0))],
+        ["a", "v", "a", "v", "v"],
+        VMEM_LIMIT,
+        (2 * blocks,),
     )
 
 
@@ -980,9 +1034,9 @@
 
 
 def layer_kernel(
-    vocab, parts, stats, base, unit, grad_in, grad_back, smalls, rows, facts, targets, head,
+    vocab, parts, stats, base, unit, grad_in, grad_back, grad_scales, grad_bias, vectors, rows, facts, targets, head,
     rows_all, in_all, back_all, smalls_out, head_out, squares,
-    low, sum_in, sum_back, turned, stats_all, steps_all, from_y, own_sum, from_z, pair_in, pair_back, half_in, half_back, far_in, far_back, small_rep, small_sum, small_shard,
+    smalls, low, sum_in, sum_back, turned, stats_all, steps_all, from_y, own_sum, from_z, pair_in, pair_back, half_in, half_back, far_in, far_back, small_rep, small_sum, small_shard,
     send_y, recv_y, send_z, recv_z, send_stat, recv_stat, send_pair, recv_pair, send_far, recv_far,
     send_rep, recv_rep, send_small, recv_small,
     send_row, recv_row, send_in, recv_in, send_back, recv_back, own,
@@ -991,6 +1045,7 @@
     last = pl.num_programs(0) - 1
     rep, shard, core_twin, x_twin, y_twin = whereabouts()
     core_far = lax.rem(core_twin + 2, RG)
+    small_rows = 14
     shard_peers = [(rep, shard_peer(shard, step)) for step in range(1, SG)]
     rep_peers = [(lax.rem(rep + step, RG), shard) for step in range(1, RG)]
 
@@ -1003,7 +1058,7 @@
         pairs = ((grad_in, pair_in), (grad_back, pair_back))
         return [
             remote(
-                source.at[which], target.at[slot], send_pair.at[2 * slot + k], recv_pair.at[2 * slot + k],
+                source.at[:, which], target.at[slot], send_pair.at[2 * slot + k], recv_pair.at[2 * slot + k],
                 (core_twin, shard),
             )
             for k, (source, target) in enumerate(pairs)
@@ -1069,7 +1124,24 @@
             copy.start()
         for step in (2, 1, 3, 0):
             y_copy(step).start()
-        for copy in pair_copies(core_far, 1) + pair_copies(core_twin, 0) + rep_copies():
+        for copy in pair_copies(core_far, 1) + pair_copies(core_twin, 0):
+            copy.start()
+        smalls[...] = jnp.zeros_like(smalls)
+
+        def put(row, values):
+            smalls[row // small_rows, pl.ds(lax.rem(row, small_rows), 1), :] = values
+
+        for k in range(8):
+            lanes = slice(k * 128, (k + 1) * 128)
+            for vector in range(4):
+                put(8 * vector + k, grad_scales[vector : vector + 1, lanes])
+            put(8 * 4 + k, vectors[0:1, lanes])
+            put(8 * 5 + k, vectors[1:2, lanes])
+            put(8 * 13 + k, vectors[2:3, lanes])
+        for k in range(7):
+            row = 48 + 8 * k + shard if k < 3 else 72 + 4 * shard + k - 3
+            put(row, grad_bias[0:1, k * 128 : (k + 1) * 128])
+        for copy in rep_copies():
             copy.start()
         stats_all[shard] = stats[...]
         squares[...] = jnp.zeros_like(squares)
@@ -1080,8 +1152,8 @@
     def _():
         for copy in pair_copies(core_far, 1):
             copy.wait()
-        half_in[...] = grad_in[x_twin] + pair_in[1]
-        half_back[...] = grad_back[x_twin] + pair_back[1]
+        half_in[...] = grad_in[:, x_twin] + pair_in[1]
+        half_back[...] = grad_back[:, x_twin] + pair_back[1]
         for copy in far_copies():
             copy.start()
         for copy in rep_copies():
@@ -1112,8 +1184,8 @@
             copy.wait()
         for copy in far_copies():
             copy.wait()
-        sum_in[...] = grad_in[rep] + pair_in[0] + far_in[...]
-        sum_back[...] = grad_back[rep] + pair_back[0] + far_back[...]
+        sum_in[...] = grad_in[:, rep] + pair_in[0] + far_in[...]
+        sum_back[...] = grad_back[:, rep] + pair_back[0] + far_back[...]
         for copy in in_copies():
             copy.start()
         own_in().start()
@@ -1177,10 +1249,13 @@
         passed.wait()
 
 
-def layer_sums(parts, stats, base, unit, grad_in, grad_back, smalls, rows, facts, targets, head, number):
+def layer_sums(
+    parts, stats, base, unit, grad_in, grad_back, grad_scales, grad_bias, vectors, rows, facts, targets, head, number
+):
     dma = pltpu.SemaphoreType.DMA
     chunk = parts.shape[1:]
-    quarter_in, quarter_back, piece = grad_in.shape[1:], grad_back.shape[1:], smalls.shape[1:]
+    quarter_in, quarter_back = (array.shape[:1] + array.shape[2:] for array in (grad_in, grad_back))
+    piece = (16, 128)
     vocab, depth = head.shape
     vmem = lambda shape: pltpu.VMEM(shape, jnp.float32)
     shape = lambda dims: jax.ShapeDtypeStruct(dims, jnp.float32)
@@ -1195,28 +1270,45 @@
             shape(head.shape),
             shape((8, depth)),
         ],
-        [pltpu.VMEM(chunk, jnp.bfloat16), vmem(quarter_in), vmem(quarter_back)]
+        [vmem((SG,) + piece), pltpu.VMEM(chunk, jnp.bfloat16), vmem(quarter_in), vmem(quarter_back)]
         + [pltpu.VMEM((RG, depth, rows.shape[1]), rows.dtype), vmem((SG,) + stats.shape), vmem((chunk[0], 128))]
         + [pltpu.VMEM((count,) + chunk, parts.dtype) for count in (4, 4, 3)]
         + [vmem((2,) + quarter_in), vmem((2,) + quarter_back), vmem(quarter_in), vmem(quarter_back), vmem(quarter_in), vmem(quarter_back)]
-        + [vmem((3,) + smalls.shape), vmem(smalls.shape), vmem((SG - 1,) + piece)]
-        + sum_sems()
+        + [vmem((3, SG) + piece), vmem((SG,) + piece), vmem((SG - 1,) + piece)]
+        + [dma((4,)), dma((4,)), dma((3,)), dma((3,))]
         + [dma((SG - 1,))] * 2 + [dma((4,))] * 2 + [dma((2,))] * 2 + [dma((3,))] * 2 + [dma((SG - 1,))] * 2
         + [dma((3,))] * 2 + [dma((SG - 1,))] * 2 + [dma((5,))] * 2 + [dma((2,))],
         number,
-        (parts, stats, base, unit, grad_in, grad_back, smalls, rows, facts, targets, head),
-        ["v"] * 10 + [block],
+        (parts, stats, base, unit, grad_in, grad_back, grad_scales, grad_bias, vectors, rows, facts, targets, head),
+        ["v"] * 12 + [block],
         ["a"] * 3 + ["v", block, "v"],
         62 << 20,
         (pl.cdiv(vocab, VOCAB_BLOCK),),
     )
 
 
-def total_kernel(value, out, from_rep, half, from_shard, send_rep, recv_rep, send_shard, recv_shard):
+def norm_kernel(
+    head_squares, embed_squares, smalls, grad_in, grad_back, out,
+    value, from_rep, half, from_shard, send_rep, recv_rep, send_shard, recv_shard,
+):
     rep, shard, _, _, _ = whereabouts()
     shard_peers = [(rep, shard_peer(shard, step)) for step in range(1, SG)]
     rep_peers = [(lax.rem(rep + step, RG), shard) for step in range(1, RG)]
     greet(shard_peers + rep_peers)
+
+    def squares(rows):
+        return jnp.sum(rows * rows, axis=0, keepdims=True)
+
+    def lanes(row):
+        return sum(row[:, k * 128 : (k + 1) * 128] for k in range(row.shape[1] // 128))
+
+    repeated = jnp.sum(embed_squares[...], axis=0, keepdims=True) + squares(smalls[...])
+    repeated = repeated + lanes(jnp.sum(head_squares[...], axis=0, keepdims=True))
+    total = repeated * (1.0 / RG)
+    for rows in (grad_in, grad_back):
+        for k in range(rows.shape[0]):
+            total = total + lanes(squares(rows[k]))
+    value[...] = jnp.broadcast_to(jnp.sum(total, axis=1, keepdims=True), value.shape)
     copies = [
         remote(value, from_rep.at[rep], send_rep.at[k], recv_rep.at[k], peer) for k, peer in enumerate(rep_peers)
     ]
@@ -1238,20 +1330,24 @@
     total = from_shard[0]
     for k in range(1, SG):
         total = total + from_shard[k]
-    out[...] = total
-
-
-def total_everywhere(value, number):
+    norm = jnp.sqrt(total)
+    row = lax.broadcasted_iota(jnp.int32, norm.shape, 0)
+    out[...] = jnp.where(row == 0, norm, CLIP_LEVEL / jnp.maximum(norm, CLIP_LEVEL))
+
+
+def global_norm(head_squares, embed_squares, smalls, grad_in, grad_back, number):
     dma = pltpu.SemaphoreType.DMA
+    tile = (8, 128)
+    vmem = lambda *shape: pltpu.VMEM(shape, jnp.float32)
     return comm_call(
-        total_kernel,
-        [jax.ShapeDtypeStruct(value.shape, value.dtype)],
-        [pltpu.VMEM((RG,) + value.shape, value.dtype), pltpu.VMEM(value.shape, value.dtype), pltpu.VMEM((SG,) + value.shape, value.dtype)]
-        + [dma((RG - 1,))] * 2 + [dma((SG - 1,))] * 2,
+        norm_kernel,
+        [jax.ShapeDtypeStruct(tile, jnp.float32)],
+        [vmem(*tile), vmem(RG, *tile), vmem(*tile), vmem(SG, *tile)] + [dma((RG - 1,))] * 2 + [dma((SG - 1,))] * 2,
         number,
-        (value,),
+        (head_squares, embed_squares, smalls, grad_in, grad_back),
+        "vvvvv",
         "v",
-        "v",
+        12 << 20,
     )[0]
 
 
@@ -1264,6 +1360,7 @@
 TABLE_BLOCK = 4096
 CAST_BLOCK = 512
 VMEM_LIMIT = 60 << 20
+EMBED_LIMIT = 30 << 20
 
 
 def transposed_dot(left, right):
@@ -1286,54 +1383,6 @@
         pl.when(at == full)(lambda: body(tail))
 
 
-def top_kernel(vocab, rows, targets, head, stats, turned, top, total, target):
-    at = pl.program_id(0)
-
-    @pl.when(at == 0)
-    def _():
-        turned[...] = rows[...].T
-        top[...] = jnp.full_like(top, -1e30)
-        total[...] = jnp.zeros_like(total)
-        target[...] = jnp.zeros_like(target)
-
-    def block(size):
-        logits = plain_dot(head[:size], turned[...])
-        hits = lax.broadcasted_iota(jnp.int32, logits.shape, 0) == targets[...] - at * ROW_BLOCK
-        target[...] += jnp.sum(jnp.where(hits, logits, 0.0), axis=0, keepdims=True)
-        highest = jnp.maximum(top[...], jnp.max(logits, axis=0, keepdims=True))
-        weights = jnp.sum(jnp.exp(logits - highest), axis=0, keepdims=True)
-        total[...] = total[...] * jnp.exp(top[...] - highest) + weights
-        top[...] = highest
-
-    vocab_blocks(vocab, ROW_BLOCK, block)
-
-    @pl.when(at == pl.num_programs(0) - 1)
-    def _():
-        stats[...] = jnp.zeros_like(stats)
-        stats[0:1, :] = top[...]
-        stats[1:2, :] = total[...]
-        stats[2:3, :] = target[...]
-
-
-def logit_stats(rows, targets, head):
-    vocab, depth = head.shape
-    count = rows.shape[0]
-    line = pltpu.VMEM((1, count), jnp.float32)
-    return pl.pallas_call(
-        functools.partial(top_kernel, vocab),
-        grid=(pl.cdiv(vocab, ROW_BLOCK),),
-        in_specs=[
-            pl.BlockSpec((count, depth), lambda at: (0, 0)),
-            pl.BlockSpec((1, count), lambda at: (0, 0)),
-            pl.BlockSpec((ROW_BLOCK, depth), lambda at: (at, 0)),
-        ],
-        out_specs=pl.BlockSpec((8, count), lambda at: (0, 0)),
-        out_shape=jax.ShapeDtypeStruct((8, count), jnp.float32),
-        scratch_shapes=[pltpu.VMEM((depth, count), rows.dtype), line, line, line],
-        compiler_params=pltpu.CompilerParams(vmem_limit_bytes=VMEM_LIMIT),
-    )(rows, targets, head)
-
-
 def logit_grads(low, turned, logsum, targets):
     logits = plain_dot(low, turned)
     hits = lax.broadcasted_iota(jnp.int32, logits.shape, 0) == targets
@@ -1341,89 +1390,114 @@
     return jnp.where(hits, weights - 1.0, weights).astype(jnp.bfloat16)
 
 
-def rows_kernel(vocab, rows, facts, targets, head, out, turned):
-    at = pl.program_id(0)
-
-    @pl.when(at == 0)
-    def _():
-        turned[...] = rows[...].T
-        out[...] = jnp.zeros_like(out)
-
-    def block(size):
-        low = head[:size]
-        out[...] += first_dot(logit_grads(low, turned[...], facts[0:1, :], targets[...] - at * ROW_BLOCK), low)
-
-    vocab_blocks(vocab, ROW_BLOCK, block)
-
-
-def picked_grads(rows, facts, targets, head):
-    vocab, depth = head.shape
-    count = rows.shape[0]
-    return pl.pallas_call(
-        functools.partial(rows_kernel, vocab),
-        grid=(pl.cdiv(vocab, ROW_BLOCK),),
-        in_specs=[
-            pl.BlockSpec((count, depth), lambda at: (0, 0)),
-            pl.BlockSpec((8, count), lambda at: (0, 0)),
-            pl.BlockSpec((1, count), lambda at: (0, 0)),
-            pl.BlockSpec((ROW_BLOCK, depth), lambda at: (at, 0)),
-        ],
-        out_specs=pl.BlockSpec((count, depth), lambda at: (0, 0)),
-        out_shape=jax.ShapeDtypeStruct((count, depth), jnp.float32),
-        scratch_shapes=[pltpu.VMEM((depth, count), rows.dtype)],
-        compiler_params=pltpu.CompilerParams(vmem_limit_bytes=VMEM_LIMIT),
-    )(rows, facts, targets, head)
-
-
-def embed_grad_kernel(ids, rows, out, squares, table, wide):
-    at = pl.program_id(0)
-    width = out.shape[1]
-
-    @pl.when(at == 0)
-    def _():
-        squares[...] = jnp.zeros_like(squares)
-        wide[...] = rows[...].astype(jnp.float32)
-
-        @pl.loop(0, table.shape[0] // 512)
-        def _(part):
-            table[pl.ds(pl.multiple_of(part * 512, 512), 512), :] = jnp.zeros((512, table.shape[1]), jnp.float32)
-
-        @pl.loop(0, rows.shape[0] // 8)
-        def _(group):
-            for lane in range(8):
-                token = group * 8 + lane
-                here = pl.ds(ids[token], 1)
-                table[here, :] = table[here, :] + wide[pl.ds(token, 1), :]
-
-    block = table[pl.ds(pl.multiple_of(at * width, width), width), :]
-    out[...] = block.T
-    squares[...] += jnp.sum((block * block).reshape(width // 8, 8, block.shape[1]), axis=0)
+def embed_grad_kernel(ids, rows, table, squares, wide):
+    wide[...] = rows[...].astype(jnp.float32)
+    squares[...] = jnp.zeros_like(squares)
+    parts = table.shape[0] // 512
+
+    def part_rows(part):
+        return pl.ds(pl.multiple_of(part * 512, 512), 512)
+
+    @pl.loop(0, parts)
+    def _(part):
+        table[part_rows(part), :] = jnp.zeros((512, table.shape[1]), jnp.float32)
+
+    @pl.loop(0, rows.shape[0] // 8)
+    def _(group):
+        for lane in range(8):
+            token = group * 8 + lane
+            here = pl.ds(ids[token], 1)
+            table[here, :] = table[here, :] + wide[pl.ds(token, 1), :]
+
+    @pl.loop(0, parts)
+    def _(part):
+        block = table[part_rows(part), :]
+        squares[...] += jnp.sum((block * block).reshape(64, 8, block.shape[1]), axis=0)
 
 
 def embed_grads(ids, rows, vocab):
     count, feats = rows.shape
-    blocks = pl.cdiv(vocab, TABLE_BLOCK)
+    height = pl.cdiv(vocab, TABLE_BLOCK) * TABLE_BLOCK
     return pl.pallas_call(
         embed_grad_kernel,
-        grid=(blocks,),
+        in_specs=[pl.BlockSpec(memory_space=pltpu.SMEM), pl.BlockSpec(memory_space=pltpu.VMEM)],
+        out_specs=[pl.BlockSpec(memory_space=pltpu.VMEM)] * 2,
+        out_shape=[pltpu.VMEM((height, feats), jnp.float32), jax.ShapeDtypeStruct((8, feats), jnp.float32)],
+        scratch_shapes=[pltpu.VMEM((count, feats), jnp.float32)],
+        compiler_params=pltpu.CompilerParams(vmem_limit_bytes=EMBED_LIMIT),
+    )(ids, rows)
+
+
+def embed_update_kernel(norm, grads, weight, moment, square, next_weight, next_moment, next_square):
+    width = weight.shape[1]
+    here = pl.ds(pl.multiple_of(pl.program_id(0) * width, width), width)
+    gradient = grads[here, :].T * norm[1:2, 0:1]
+    next_weight[...], next_moment[...], next_square[...] = adamw(
+        weight[...], gradient, moment[...], square[...], RATE_EMBED
+    )
+
+
+def update_embed(norm, grads, state):
+    feats, vocab = state[0].shape
+    block = pl.BlockSpec((feats, TABLE_BLOCK), lambda at: (0, at))
+    return pl.pallas_call(
+        embed_update_kernel,
+        grid=(pl.cdiv(vocab, TABLE_BLOCK),),
+        in_specs=[pl.BlockSpec(norm.shape, lambda at: (0, 0)), pl.BlockSpec(memory_space=pltpu.VMEM)] + [block] * 3,
+        out_specs=[block] * 3,
+        out_shape=[jax.ShapeDtypeStruct(state[0].shape, jnp.float32)] * 3,
+        compiler_params=pltpu.CompilerParams(vmem_limit_bytes=EMBED_LIMIT),
+    )(norm, pltpu.with_memory_space_constraint(grads, pltpu.VMEM), *state)
+
+
+def update_kernel(
+    norm, grads_in, grads_back, *refs
+):
+    factor = norm[1:2, 0:1]
+    ins, backs = refs[0:3], refs[3:6]
+    out_ins, out_backs = refs[6:9], refs[9:12]
+
+    def update(here, gradient, sources, targets, rate):
+        results = adamw(sources[0][here], gradient * factor, sources[1][here], sources[2][here], rate)
+        for target, result in zip(targets, results):
+            target[here] = result
+
+    for source in range(SG):
+        for part in range(3):
+            first = part * D + source * HEAD_COLS
+            gradient = grads_in[0, source, :, part * HEAD_COLS : (part + 1) * HEAD_COLS]
+            update((slice(None), slice(first, first + HEAD_COLS)), gradient, ins, out_ins, RATE_IN)
+        first = 3 * D + source * UNITS
+        gradient = grads_in[0, source, :, 3 * HEAD_COLS :]
+        update((slice(None), slice(first, first + UNITS)), gradient, ins, out_ins, RATE_IN)
+    for tile in range(5):
+        update((tile, 0), grads_back[0, tile], backs, out_backs, RATE_BACK)
+
+
+def update_layer(norm, grads_in, grads_back, state_in, state_back):
+    quarters, sources, rows, columns = grads_in.shape
+    _, tiles, back_rows, depth = grads_back.shape
+    wide = state_in[0].shape
+    tall = state_back[0].shape
+    back_shape = (tiles, quarters, back_rows, depth)
+    in_block = pl.BlockSpec((rows, wide[1]), lambda at: (at, 0))
+    back_block = pl.BlockSpec((tiles, 1, back_rows, depth), lambda at: (0, at, 0, 0))
+    f32 = jnp.float32
+    results = pl.pallas_call(
+        update_kernel,
+        grid=(quarters,),
         in_specs=[
-            pl.BlockSpec(memory_space=pltpu.SMEM),
-            pl.BlockSpec(memory_space=pltpu.VMEM),
-        ],
-        out_specs=[
-            pl.BlockSpec((feats, TABLE_BLOCK), lambda at: (0, at)),
-            pl.BlockSpec((8, feats), lambda at: (0, 0)),
-        ],
-        out_shape=[
-            jax.ShapeDtypeStruct((feats, vocab), jnp.float32),
-            jax.ShapeDtypeStruct((8, feats), jnp.float32),
-        ],
-        scratch_shapes=[
-            pltpu.VMEM((blocks * TABLE_BLOCK, feats), jnp.float32),
-            pltpu.VMEM((count, feats), jnp.float32),
-        ],
+            pl.BlockSpec(norm.shape, lambda at: (0, 0)),
+            pl.BlockSpec((1, sources, rows, columns), lambda at: (at, 0, 0, 0)),
+            pl.BlockSpec((1, tiles, back_rows, depth), lambda at: (at, 0, 0, 0)),
+        ]
+        + [in_block] * 3
+        + [back_block] * 3,
+        out_specs=[in_block] * 3 + [back_block] * 3,
+        out_shape=[jax.ShapeDtypeStruct(wide, f32)] * 3 + [jax.ShapeDtypeStruct(back_shape, f32)] * 3,
         compiler_params=pltpu.CompilerParams(vmem_limit_bytes=VMEM_LIMIT),
-    )(ids, rows)
+    )(norm, grads_in, grads_back, *state_in, *[array.reshape(back_shape) for array in state_back])
+    return (*results[:3], *[array.reshape(tall) for array in results[3:]])
 
 
 def turn_tables(places):
@@ -1489,12 +1563,12 @@
 
 
 def forward_kernel(
-    spans, residual, places, scales, bias, own, after, before, weights, back,
-    queries, keys, values, hidden, joined, picked_one, picked_two, picked_rows, branch,
+    residual, places, scales, bias, own, after, before, weights, back,
+    queries, keys, values, hidden, joined, picked_one, picked_two, picked_rows, used, branch,
 ):
     bf16 = jnp.bfloat16
     tokens = residual.shape[0]
-    span = spans[pl.program_id(0)]
+    span = places[1:2, :]
     gain_one, shift_one = scales[0:1, :], scales[1:2, :]
     gain_two, shift_two = scales[2:3, :], scales[3:4, :]
     unit, _ = centred_rows(residual[...].astype(jnp.float32))
@@ -1503,6 +1577,7 @@
     pick = pick_matrix(slots, tokens)
     rows = first_dot(pick.astype(bf16), residual[...])
     picked_rows[...] = rows.astype(bf16)
+    used[...] = first_dot(pick.astype(bf16), jnp.ones((tokens, used.shape[1]), bf16))
     unit, _ = centred_rows(rows)
     low_picked = (unit * gain_one + shift_one).astype(bf16)
     picked_one[...] = low_picked
@@ -1540,8 +1615,8 @@
     return pl.BlockSpec(array.shape, lambda line: (0,) * array.ndim)
 
 
-def layer_forward(spans, residual, places, scales, bias, tables, weights, back):
-    lines = spans.shape[0]
+def layer_forward(residual, places, scales, bias, tables, weights, back):
+    lines = places.shape[0] // 8
     tokens, slots = residual.shape[0] // lines, places.shape[1]
     depth = residual.shape[1]
     bf16, f32 = jnp.bfloat16, jnp.float32
@@ -1554,13 +1629,13 @@
         (slots, depth, bf16),
         (slots, depth, bf16),
         (slots, depth, bf16),
+        (slots, 128, f32),
         (slots, depth, f32),
     ]
     return pl.pallas_call(
         forward_kernel,
         grid=(lines,),
         in_specs=[
-            pl.BlockSpec(memory_space=pltpu.SMEM),
             line_block(tokens, depth),
             line_block(8, slots),
             still(scales),
@@ -1572,18 +1647,18 @@
         out_specs=[line_block(height, width) for height, width, _ in outs],
         out_shape=[jax.ShapeDtypeStruct((lines * height, width), kind) for height, width, kind in outs],
         compiler_params=pltpu.CompilerParams(vmem_limit_bytes=VMEM_LIMIT),
-    )(spans, residual, places, scales, bias, *tables, weights, back)
+    )(residual, places, scales, bias, *tables, weights, back)
 
 
 def backward_kernel(
-    spans, residual, places, scales, own, after, before, weights, back,
+    residual, places, scales, own, after, before, weights, back,
     queries, keys, values, hidden, joined, picked_one, picked_two, d_branch, d_after,
     unit_parts, stats, base, own_unit, grad_in, grad_back, grad_scales, grad_bias, unit_rows,
 ):
     bf16 = jnp.bfloat16
     line = pl.program_id(0)
     tokens = residual.shape[0]
-    span = spans[line]
+    span = places[1:2, :]
     gain_one, shift_one = scales[0:1, :], scales[1:2, :]
     gain_two = scales[2:3, :]
 
@@ -1630,24 +1705,20 @@
     feats = own_unit.shape[1]
     own_unit[...] = unit_rows[:, pl.ds(pl.multiple_of(lax.axis_index("shard") * feats, feats), feats)]
     low_one = (unit * gain_one + shift_one).astype(bf16)
-    two, three = 2 * HEAD_COLS, 3 * HEAD_COLS
+    three = 3 * HEAD_COLS
     grad_in[:, :HEAD_COLS] += first_dot(picked_one[...], d_query)
-    grad_in[:, HEAD_COLS:two] += first_dot(low_one, d_key)
-    grad_in[:, two:three] += first_dot(low_one, d_value)
+    d_both = jnp.concatenate([d_key, d_value], axis=1)
+    grad_in[:, HEAD_COLS:three] += first_dot(low_one, d_both)
     grad_in[:, three:] += first_dot(picked_two[...], d_hidden)
 
     def column_sum(rows):
         return jnp.sum(rows.astype(jnp.float32), axis=0, keepdims=True)
 
     grad_bias[0:1, :HEAD_COLS] += column_sum(d_query)
-    grad_bias[0:1, HEAD_COLS:two] += column_sum(d_key)
-    grad_bias[0:1, two:three] += column_sum(d_value)
+    grad_bias[0:1, HEAD_COLS:three] += column_sum(d_both)
     grad_bias[0:1, three:] += column_sum(d_hidden)
-    d_normed = (
-        transposed_dot(plain_dot(pick, d_query).astype(bf16), weights[:, :HEAD_COLS])
-        + transposed_dot(d_key, weights[:, HEAD_COLS:two])
-        + transposed_dot(d_value, weights[:, two:three])
-    )
+    d_projected = jnp.concatenate([plain_dot(pick, d_query).astype(bf16), d_both], axis=1)
+    d_normed = transposed_dot(d_projected, weights[:, :three])
     d_unit = d_normed * gain_one
     grad_scales[0:1, :] += column_sum(d_normed * unit)
     grad_scales[1:2, :] += column_sum(d_normed)
@@ -1666,8 +1737,8 @@
         unit_parts[part] = codes[:, part * feats : (part + 1) * feats]
 
 
-def layer_backward(spans, residual, places, scales, tables, weights, back, kept, d_branch, d_after):
-    lines = spans.shape[0]
+def layer_backward(residual, places, scales, tables, weights, back, kept, d_branch, d_after):
+    lines = places.shape[0] // 8
     count, depth = residual.shape
     tokens, slots = count // lines, places.shape[1]
     feats = depth // SG
@@ -1677,7 +1748,6 @@
         backward_kernel,
         grid=(lines,),
         in_specs=[
-            pl.BlockSpec(memory_space=pltpu.SMEM),
             line_block(tokens, depth),
             line_block(8, slots),
             still(scales),
@@ -1710,7 +1780,7 @@
         ],
         scratch_shapes=[pltpu.VMEM((tokens, depth), f32)],
         compiler_params=pltpu.CompilerParams(vmem_limit_bytes=VMEM_LIMIT),
-    )(spans, residual, places, scales, *tables, weights, back, *kept, d_branch, d_after)
+    )(residual, places, scales, *tables, weights, back, *kept, d_branch, d_after)
 
 
 def group_plan(
@@ -1758,90 +1828,35 @@
     small_low = small_params.astype(bf16).astype(jnp.float32).reshape(-1, 128)
     small_rows = small_low.shape[0]
     smalls = jnp.pad(small_low, ((0, 16 - small_rows), (0, 0)))
-    ints_all, scales, own_bias, residual_low, in_all, back_all, head_low = share_entry(
+    ints_all, places, marks, scales, own_bias, residual_low, in_all, back_all, head_low = share_entry(
         ints, smalls, proj_in, proj_back, embed_table, head_table.T, tokens, 1
     )
     own_in = in_all.reshape(D, OWN_COLS)
     own_back = back_all.reshape(5 * 128, D)
-    gain_last, shift_last, bias_out = scales[4], scales[5], scales[6]
-
-    by_group = ints_all.reshape(RG, RG, SG // RG, 8, seq_dev)
-    ids_all = jnp.transpose(by_group[:, :, :, :micro], (1, 3, 2, 0, 4)).reshape(RG, tokens)
-    slot_facts = jnp.transpose(
-        by_group[:, :, :, 2].reshape(RG, RG, SG // RG, 2, micro, slots), (3, 1, 4, 2, 0, 5)
-    ).reshape(2, RG, slot_count)
-    used_all = slot_facts[0] < seq_dev
-    targets_all = jnp.where(used_all, slot_facts[1] - shard_at * vocab_dev, -1)
-    counted_all = used_all.astype(jnp.float32)
-    pos_group = lax.dynamic_index_in_dim(slot_facts[0], rep_at, 0, False)
-    targets_group = lax.dynamic_index_in_dim(targets_all, rep_at, 0, False)
-    counted_group = lax.dynamic_index_in_dim(counted_all, rep_at, 0, False)
-    spans = lax.dynamic_index_in_dim(by_group[0, :, :, 3, :micro], rep_at, 0, False).T.reshape(lines)
-
-    slot_places = pos_group.reshape(lines, RG, slots)
-    block_starts = (jnp.arange(RG) * seq_dev)[None, :, None]
-    slot_places = jnp.where(slot_places < seq_dev, slot_places + block_starts, -1).reshape(lines, 1, RG * slots)
-    slot_places = jnp.broadcast_to(slot_places, (lines, 8, RG * slots)).reshape(lines * 8, RG * slots)
+
     tables = turn_tables(jnp.arange(seq_len).astype(jnp.float32))
-    *kept, picked_rows, branch_parts = layer_forward(
-        spans, residual_low, slot_places, scales, own_bias, tables, own_in, own_back
-    )
-    branch = shard_sum(branch_parts.reshape(SG, own_slots, D), 3)
-
-    own_residual = lax.dynamic_slice_in_dim(picked_rows, shard_at * own_slots, own_slots, 0).astype(jnp.float32)
-    own_used = lax.dynamic_slice_in_dim(counted_group, shard_at * own_slots, own_slots, 0)
-    after_add = own_residual + branch + bias_out
-    final_rows, pull_last = jax.vjp(norm_rows, after_add, gain_last, shift_last)
-    picked = (final_rows * own_used[:, None]).astype(bf16)
-    rows_group = shard_gather(picked, 4)
-
-    stats = logit_stats(rows_group, targets_group[None], head_low)
-    stats_all = shard_stats(stats, 5)
-    tops = stats_all[:, 0]
-    top = jnp.max(tops, axis=0)
-    logsum = top + jnp.log(jnp.sum(stats_all[:, 1] * jnp.exp(tops - top), axis=0))
-    row_target = jnp.sum(stats_all[:, 2], axis=0)
-    row_loss = jnp.where(counted_group > 0.0, logsum - row_target, 0.0)
-    logsum = jnp.where(counted_group > 0.0, logsum, 1e30)
-    facts = jnp.concatenate(
-        [logsum[None], row_loss[None], counted_group[None], jnp.zeros((5, slot_count), jnp.float32)]
-    )
-    picked_parts = picked_grads(rows_group, facts, targets_group[None], head_low)
-    d_picked, rows_all, facts_all = sum_and_share(
-        picked_parts.reshape(SG, own_slots, D), rows_group, facts, 6
+    *kept, picked_rows, used, branch_parts = layer_forward(
+        residual_low, places, scales, own_bias, tables, own_in, own_back
+    )
+    rows_all, facts_all, d_branch, after_pieces, vectors = loss_and_branch(
+        branch_parts.reshape(SG, own_slots, D),
+        picked_rows,
+        scales,
+        used,
+        marks,
+        head_low,
+        3,
     )
     loss_sum = jnp.sum(facts_all[:, 1])
     count_sum = jnp.sum(facts_all[:, 2])
-    targets_wide = jnp.broadcast_to(targets_all[:, None, :], (RG, 8, slot_count))
-
-    d_after, d_gain_last, d_shift_last = pull_last(d_picked)
-    d_branch_own = d_after.astype(bf16)
-    d_bias_out = jnp.sum(d_branch_own.astype(jnp.float32), axis=0)
-    pieces = jnp.transpose(d_after.reshape(own_slots, SG, D // SG), (1, 0, 2))
-    d_branch, after_pieces = share_branch(d_branch_own, pieces, 7)
     d_after_feats = after_pieces.reshape(slot_count, D // SG)
 
     unit_parts, norm_stats, base, own_unit, grad_in, grad_back, grad_scales, grad_bias = layer_backward(
-        spans, residual_low, slot_places, scales, tables, own_in, own_back, kept, d_branch, d_after_feats
-    )
-
-    def whole(columns, length):
-        start = shard_at * columns.shape[0]
-        return lax.dynamic_update_slice(jnp.zeros((length,), jnp.float32), columns, (start,))
-
-    grad_small = jnp.concatenate(
-        [
-            grad_scales[:4].reshape(-1),
-            d_gain_last,
-            d_shift_last,
-            *[whole(grad_bias[0, part * HEAD_COLS : (part + 1) * HEAD_COLS], D) for part in range(3)],
-            whole(grad_bias[0, 3 * HEAD_COLS :], FF),
-            d_bias_out,
-        ]
-    )
-    grad_small = jnp.pad(grad_small.reshape(SG, small_rows, 128), ((0, 0), (0, 16 - small_rows), (0, 0)))
-    in_quarters = jnp.transpose(grad_in.reshape(SG, RG, quarter, OWN_COLS), (1, 0, 2, 3))
-    back_quarters = jnp.transpose(grad_back.reshape(5, RG, 32, D), (1, 0, 2, 3))
+        residual_low, places, scales, tables, own_in, own_back, kept, d_branch, d_after_feats
+    )
+
+    in_quarters = grad_in.reshape(SG, RG, quarter, OWN_COLS)
+    back_quarters = grad_back.reshape(5, RG, 32, D)
     d_rows_all, in_own, back_own, small_sum, grad_head, head_squares = layer_sums(
         unit_parts,
         norm_stats,
@@ -1849,41 +1864,35 @@
         own_unit,
         in_quarters,
         back_quarters,
-        grad_small,
+        grad_scales,
+        grad_bias,
+        vectors,
         rows_all,
         facts_all,
-        targets_wide,
+        marks,
         head_low,
         8,
     )
     in_grads = lax.all_gather(in_own, "rep")
     back_grads = lax.all_gather(back_own, "rep")
-    grad_embed, embed_squares = embed_grads(ids_all.reshape(-1), d_rows_all.reshape(RG * tokens, D // SG), vocab)
-
-    in_grads = jnp.transpose(in_grads, (0, 2, 1, 3)).reshape(D // SG, SG, OWN_COLS)
-    qkv_grads = jnp.transpose(
-        in_grads[:, :, : 3 * HEAD_COLS].reshape(D // SG, SG, 3, HEAD_COLS), (0, 2, 1, 3)
-    ).reshape(D // SG, 3 * D)
-    grad_in = jnp.concatenate([qkv_grads, in_grads[:, :, 3 * HEAD_COLS :].reshape(D // SG, FF)], axis=1)
-    grad_back = jnp.transpose(back_grads, (1, 0, 2, 3)).reshape(proj_back.shape)
+    by_group = ints_all.reshape(RG, RG, SG // RG, 8, seq_dev)[:, :, :, :micro]
+    ids_all = jnp.transpose(by_group, (1, 3, 2, 0, 4)).reshape(-1)
+    grad_embed, embed_squares = embed_grads(ids_all, d_rows_all.reshape(RG * tokens, D // SG), vocab)
+
+    norm_rows_out = global_norm(head_squares, embed_squares, small_sum, in_own, back_own, 10)
+    norm_value, factor = norm_rows_out[0, 0], norm_rows_out[1, 0]
+    next_in, moment_in, square_in, next_back, moment_back, square_back = update_layer(
+        norm_rows_out, in_grads, back_grads, (proj_in, first_in, second_in), (proj_back, first_back, second_back)
+    )
     grad_small = small_sum[:small_rows].reshape(-1)
-
-    repeated_square = jnp.sum(grad_small * grad_small) + jnp.sum(head_squares) + jnp.sum(embed_squares)
-    local_square = repeated_square / RG + jnp.sum(in_own * in_own) + jnp.sum(back_own * back_own)
-    norm_value = jnp.sqrt(total_everywhere(jnp.broadcast_to(local_square, (8, 128)), 10)[0, 0])
-    factor = CLIP_LEVEL / jnp.maximum(norm_value, CLIP_LEVEL)
-    next_in, moment_in, square_in = adamw(proj_in, grad_in * factor, first_in, second_in, RATE_IN)
-    next_back, moment_back, square_back = adamw(
-        proj_back, grad_back * factor, first_back, second_back, RATE_BACK
-    )
     next_small, moment_small, square_small = adamw(
         small_params, grad_small * factor, first_small, second_small, RATE_SMALL
     )
     next_head, moment_head, square_head = adamw(
         head_table, grad_head.T * factor, first_head, second_head, RATE_HEAD
     )
-    next_embed, moment_embed, square_embed = adamw(
-        embed_table, grad_embed * factor, first_embed, second_embed, RATE_EMBED
+    next_embed, moment_embed, square_embed = update_embed(
+        norm_rows_out, grad_embed, (embed_table, first_embed, second_embed)
     )
     return (
         jnp.stack([loss_sum, count_sum]),

time: 670 us -> 599 us (0.89)
  other arithmetic: 159 us -> 74.7 us
  Pallas kernels: 444 us -> 495 us
  local copies, waits for them, and re-layouts: 37.8 us -> 7.25 us
    sub x5 -> x2, other arithmetic: 133 us -> 63.3 us  [adamw(): weight - rate_value * (moment_hat / (jnp.sqrt(square_hat) + ADAM_EPS) + D...]
    pallas_call x5, Pallas kernels: 126 us -> 156 us  [the longest x1 54.7 us: update_embed(): pl.pallas_call(embed_update_kernel, grid=(pl.cdiv(vocab, TABLE_BLOCK),),...]
    pallas_call x8 -> x4, Pallas kernels: 319 us -> 339 us  [comm_call(): pl.pallas_call(kernel, grid=grid, out_shape=out_shape, in_specs=[choose(s...]
    reduce_sum x12 -> x0, other arithmetic: 10.7 us -> none  [the longest x1 2.02 us: group_plan(): jnp.sum(in_own * in_own)]
    reshape x6 -> x0, local copies, waits for them, and re-layouts: 8.05 us -> none  [the longest x1 4.33 us: group_plan(): grad_in.reshape(SG, RG, quarter, OWN_COLS)]
    unnamed x48 -> x22, local copies, waits for them, and re-layouts: 13.6 us -> 5.57 us
  transfers between devices with their start and end apart: 2 -> 2, of which waited for: 0 -> 0; matrix products, arithmetic and copies ran while one was open for 22% -> 12% of each run, Pallas kernels for 8% -> 18%
where the time goes in v4:
time: 599 us; the launch traced here: 593 us
  Pallas kernels  495 us (83%)
  other arithmetic  74.7 us (12%)
  between operations  14.6 us (2%)
  local copies, waits for them, and re-layouts  7.25 us (1%)
    pallas_call x4, Pallas kernels, comm_call(): pl.pallas_call(kernel, grid=grid, out_shape=out_shape, in_specs=[choose(s...  339 us
    sub x2, other arithmetic, adamw(): weight - rate_value * (moment_hat / (jnp.sqrt(square_hat) + ADAM_EPS) + D...  63.3 us
    pallas_call x1, Pallas kernels, update_embed(): pl.pallas_call(embed_update_kernel, grid=(pl.cdiv(vocab, TABLE_BLOCK),),...  54.7 us
    pallas_call x1, Pallas kernels, embed_grads(): pl.pallas_call(embed_grad_kernel, in_specs=[pl.BlockSpec(memory_space=plt...  38 us
    pallas_call x1, Pallas kernels, layer_backward(): pl.pallas_call(backward_kernel, grid=(lines,), in_specs=[line_block(token...  32 us
    pallas_call x1, Pallas kernels, layer_forward(): pl.pallas_call(forward_kernel, grid=(lines,), in_specs=[line_block(tokens...  16 us
    pallas_call x1, Pallas kernels, update_layer(): pl.pallas_call(update_kernel, grid=(quarters,), in_specs=[pl.BlockSpec(no...  15.7 us
  transfers between devices with their start and end apart: 2, of which 0 were waited for; matrix products, arithmetic and copies ran while one was open for 12% of the time, Pallas kernels for 18%

profile of v4, /device:TPU:0, one launch (start us, length us, event | category | flops | bytes accessed | tf_op | source)
XLA Modules:
  0.0 592.7 jit_solution(11396742754850076430)
XLA Ops:
  7.2 0.0 all-gather.7.cloned.1.call-start
  7.3 0.5 broadcast.138
  7.8 1.3 reduce.8
  9.1 0.1 reshape_squeeze.10
  9.2 1.3 reduce.9
  10.6 0.1 reshape_squeeze.9
  10.7 0.1 pad.14.clone
  10.7 0.7 convert_bitcast_fusion
  11.4 0.6 pad_convert_fusion.smalls
  12.0 0.7 add_bitcast_fusion
  12.8 1.3 add_add_fusion.ints
  14.1 1.9 fusion.2
  16.0 75.2 %shard_map.314 = (s32[4,8,8,128]{3,2,1,0:T(8,128)}, s32[32,128]{1,0:T(8,128)}, s32[4,8,512]{2,1,0:T(8,128)}, f32[8,1024]{1,0:T(8,128)}, f32[1,896]{1,0:T(1,128)}...) custom-call(s32[8,128]{1,0:T(8,128)} %add_add_fusion.ints, ...), custom_call_target="tpu_custom_call" | custom-call | tf_op jit(solution)/shard_map/pallas_call | solution.py:436
  91.1 16.0 %shard_map.315 = (bf16[512,128]{1,0:T(8,128)(2,1)}, bf16[2048,128]{1,0:T(8,128)(2,1)}, bf16[2048,128]{1,0:T(8,128)(2,1)}, f32[512,512]{1,0:T(8,128)}, bf16[512,6...) custom-call(bf16[2048,1024]{1,0:T(8,128)(2,1)} %get-tuple-element.66, ...), custom_call_target="tpu_custom_call" | custom-call | tf_op jit(solution)/shard_map/pallas_call | solution.py:1635
  107.2 145.8 %shard_map.316 = (bf16[4,512,1024]{2,1,0:T(8,128)(2,1)}, f32[4,8,512]{2,1,0:T(8,128)}, bf16[512,1024]{1,0:T(8,128)(2,1)}, f32[8,64,128]{2,1,0:T(8,128)}, f32[8,1024]{1,0:T(8,128)}) custom-call(f32[8,64,1024]{2,1,0:T(8,128)} %bitcast.59, bf16[512,1024]{1,0:T(8,128)(2,1)} %get-tuple-element.73.picked_rows, f32[8,1024]{1,0:T(8,128)} %get-tuple-element.68.scales, ...), custom_call_target="tpu_custom_call" | custom-call | tf_op jit(solution)/shard_map/pallas_call | solution.py:436
  253.0 32.0 %shard_map.317 = (s16[8,2048,128]{2,1,0:T(8,128)(2,1)}, f32[8,2048]{1,0:T(8,128)}, f32[2048,128]{1,0:T(8,128)}, f32[2048,128]{1,0:T(8,128)}, f32[1024,896]{1,0:T...) custom-call(bf16[2048,1024]{1,0:T(8,128)(2,1)} %get-tuple-element.66.residual, ...), custom_call_target="tpu_custom_call" | custom-call | tf_op jit(solution)/shard_map/pallas_call | solution.py:1747
  285.0 102.9 %shard_map.318 = (bf16[4,2048,128]{2,1,0:T(8,128)(2,1)}, f32[8,32,896]{2,1,0:T(8,128)}, f32[5,32,1024]{2,1,0:T(8,128)}, f32[16,128]{1,0:T(8,128)}, f32[6288,1024]{1,0:T(8,128)}, /*index=5*/f32[8,1024]{1,0:T(8,128)}) custom-call(s16[8,2048,128]{2,1,0:T(8,128)(2,1)} %get-tuple-element.87.parts, f32[8,2048]{1,0:T(8,128)} %get-tuple-element.88.stats, ...), custom_call_target="tpu_custom_call" | custom-call | tf_op jit(solution)/shard_map/pallas_call | solution.py:436
  387.9 0.0 all-gather.7.cloned.1.call-update
  387.9 0.0 all-gather.5.cloned.1.call-start
  388.0 0.7 all-gather.5.cloned.1.call-update
  388.7 1.5 slice_reduce_fusion.1
  390.2 0.9 slice.24
  391.1 0.6 copy.38
  391.8 38.0 %shard_map.319 = (f32[53248,128]{1,0:T(8,128)S(1)}, f32[8,128]{1,0:T(8,128)}) custom-call(s32[8192]{0:T(1024)} %bitcast.61, bf16[8192,128]{1,0:T(8,128)(2,1)} %bitcast.58), custom_call_target="tpu_custom_call" | custom-call | tf_op jit(solution)/shard_map/pallas_call | solution.py:1421
  429.8 0.0 copy-start
  429.8 1.2 copy-done
  431.0 0.0 copy-start.1
  431.0 1.1 copy-done.1
  432.0 0.0 copy-start.3
  432.0 0.7 copy-done.3
  432.7 0.0 copy-start.5
  432.7 0.8 copy-done.5
  433.5 0.7 copy-done.6
  434.2 14.9 %shard_map.320.norm = f32[8,128]{1,0:T(8,128)S(1)} custom-call(f32[8,1024]{1,0:T(8,128)S(1)} %copy-done.5, f32[8,128]{1,0:T(8,128)S(1)} %copy-done.6, f32[16,128]{1,0:T(8,128)S(1)} %copy-done.3, f32[8,32,896]{2,1,0:T(8,128)S(1)} %copy-done, f32[5,32,1024]{2,1,0:T(8,128)S(1)} %copy-done.1), custom_call_target="tpu_custom_call" | custom-call | tf_op jit(solution)/shard_map/pallas_call | solution.py:436
  449.1 0.0 copy-start.2
  449.1 0.5 fusion.18
  449.6 1.9 pad_maximum_fusion
  451.5 0.0 copy-done.2
  451.5 0.0 copy-start.9
  451.5 54.7 %shard_map.322 = (f32[128,50304]{1,0:T(8,128)}, f32[128,50304]{1,0:T(8,128)}, f32[128,50304]{1,0:T(8,128)}) custom-call(f32[8,128]{1,0:T(8,128)} %copy-done.2, f32[53248,128]{1,0:T(8,128)S(1)} %get-tuple-element.111.grads, f32[128,50304]{1,0:T(8,128)} %weight.1, f32[128,50304]{1,0:T(8,128)} %moment.1, f32[128,50304]{1,0:T(8,128)} %square.1), custom_call_target="tpu_custom_call" | custom-call | tf_op jit(solution)/shard_map/pallas_call | solution.py:1443
  506.2 0.0 copy-done.4
  506.2 0.0 copy-done.7
  506.2 0.0 copy-done.8
  506.2 0.0 copy-done.9
  506.2 1.3 multiply_subtract_fusion.1
  507.5 62.1 %multiply_subtract_fusion = (f32[1024,6288]{0,1:T(8,128)}, f32[1024,6288]{0,1:T(8,128)}, f32[1024,6288]{0,1:T(8,128)}) fusion(f32[1024,6288]{0,1:T(8,128)} %param.26, f32[6288,1024]{1,0:T(8,128)} %get-tuple-element.110, f32[]{:T(128)} %bitcast.27, f32[1024,6288]{0,1:T(8,128)} %param.34, f32[1024,6288]{0,1:T(8,128)} %param.35), kind=kLoop, calls=%fused_computation.4 | loop fusion | flops 103022592 | bytes 180289536 | tf_op jit(solution)/shard_map/sub | solution.py:104
  569.6 0.0 all-gather.5.cloned.1.call-done
  569.6 15.7 %shard_map.321 = (f32[128,7168]{1,0:T(8,128)}, f32[128,7168]{1,0:T(8,128)}, f32[128,7168]{1,0:T(8,128)}, f32[5,4,32,1024]{3,2,1,0:T(8,128)}, f32[5,4,32,1024]{3,2,1,0:T(8,128)}, /*index=5*/f32[5,4,32,1024]{3,2,1,0:T(8,128)}) custom-call(f32[8,128]{1,0:T(8,128)} %copy-done.2, f32[4,8,32,896]{3,2,1,0:T(8,128)} %bitcast.53, f32[4,5,32,1024]{3,2,1,0:T(8,128)} %bitcast.57, ...), custom_call_target="tpu_custom_call" | custom-call | tf_op jit(solution)/shard_map/pallas_call | solution.py:1486
  (10 shorter events, 0.0 us)
Async XLA Ops:
  7.2 562.4 %all-gather.7.cloned.1.call-start = ((), (), s32[]{:S(2)}) async-start(), calls=%async_computation.1 | async-start | bytes 3276800 | tf_op jit(solution)/shard_map/all_gather | solution.py:1877
  387.9 181.7 %all-gather.5.cloned.1.call-start = ((), (), s32[]{:S(2)}) async-start(), calls=%async_computation | async-start | bytes 4587520 | tf_op jit(solution)/shard_map/all_gather | solution.py:1876
  429.8 1.2 copy-start
  431.0 1.1 copy-start.1
  432.0 0.7 copy-start.3
  432.7 0.8 copy-start.5
  433.5 0.7 copy-start.6
  449.1 2.4 copy-start.2
  451.5 54.7 %copy-start.4 = (f32[16,128]{1,0:T(8,128)S(1)}, f32[16,128]{1,0:T(8,128)}, u32[]{:S(2)}) copy-start(f32[16,128]{1,0:T(8,128)} %get-tuple-element.101.smalls) | copy-start | bytes 24580
  451.5 54.7 %copy-start.7 = (f32[1792]{0:T(1024)S(1)}, f32[1792]{0:T(1024)}, u32[]{:S(2)}) copy-start(f32[1792]{0:T(1024)} %param.25) | copy-start | bytes 21508
  451.5 54.7 %copy-start.8 = (f32[1792]{0:T(1024)S(1)}, f32[1792]{0:T(1024)}, u32[]{:S(2)}) copy-start(f32[1792]{0:T(1024)} %param.32) | copy-start | bytes 21508
  451.5 54.7 %copy-start.9 = (f32[1792]{0:T(1024)S(1)}, f32[1792]{0:T(1024)}, u32[]{:S(2)}) copy-start(f32[1792]{0:T(1024)} %param.33) | copy-start | bytes 21508
Sparse Core Ops, SparseCore 0:
  388.0 29.5 all-gather.6
  419.2 31.6 all-gather.4
